TPU v7x, 32 devices: a whole 2x2x4 slice. The times are simulated.
32 devices in a mesh: rep: 2 (over x), node: 2 (over core), local: 8 (over z, y).
Axes of the slice: x: 2, y: 2, z: 4, core: 2. Of those that a mesh axis runs over, the one named last changes fastest.
Arguments:
- tokens: bfloat16 [4608, 7168], P(('rep', 'node', 'local')), parts along dimension 0, may hold values from -6 to 6
- expert_ids: int32 [4608, 8], P(('rep', 'node', 'local')), parts along dimension 0, may hold values from 0 to 255, as said below
- route_scores: float32 [4608, 8], P(('rep', 'node', 'local')), parts along dimension 0, may hold values from 0.05 to 1
- gate_weight: bfloat16 [16, 7168, 512], P(('node', 'local')), may hold values from -0.0625 to 0.0625
- up_weight: bfloat16 [16, 7168, 512], P(('node', 'local')), may hold values from -0.0625 to 0.0625
- down_weight: bfloat16 [16, 512, 7168], P(('node', 'local')), may hold values from -0.125 to 0.125
Outputs:
- moe_out: bfloat16 [4608, 7168], P(('rep', 'node', 'local')), parts along dimension 0
There are 2 independent parts, one for each index of `rep`. A program takes and returns all parts, laid end to end along the dimension named above; an argument that names none is the same for every part. Nothing has to cross between parts.
Inputs may be any that keep to these rules, and one draw needn't show every extreme that they name: `expert_ids`: each row names 8 different experts, two in each of 4 different groups of 32 consecutive experts. A row names at most one expert of the form r * 32 with r below 4. In each aligned block of 144 rows every such expert is named by 1 to 18 rows, and in every draw one of them is named by exactly 18 rows in every block.
All inputs are finite; a program needn't handle non-finite values.
Results may differ from a plain program's by a relative error of at most 0.009.
Values may be sent and summed in bfloat16 or wider, within the bound.
No kernel may reach another device: no remote copies, remote signals or barrier semaphores. Data moves between devices by JAX's collectives and lax.ppermute only.
A program may use at most 128 MiB of HBM per device.

v0:
```python
import jax
import jax.numpy as jnp
from jax import lax
from jax.sharding import PartitionSpec as P

TEAM = 4
CAP = 18
GSIZE = 32


route_scale = 2.5


def pack_matrix(expert_ids, flight_ids):
    matched = jnp.any(expert_ids[:, None, :] == flight_ids[None, :, None], axis=2)
    slot_index = jnp.cumsum(matched.astype(jnp.int32), axis=0) - 1
    capacity_iota = jnp.arange(CAP, dtype=jnp.int32)
    picked = matched.T[:, None, :] & (slot_index.T[:, None, :] == capacity_iota[None, :, None])
    return picked


def token_weights(expert_ids, route_scores, flight_ids):
    gate_values = route_scale * route_scores / jnp.sum(route_scores, axis=1, keepdims=True)
    hit_mask = (expert_ids[:, :, None] == flight_ids[None, None, :]).astype(jnp.float32)
    return jnp.sum(gate_values[:, :, None] * hit_mask, axis=1)


def local(tokens, expert_ids, route_scores, gate_weight, up_weight, down_weight):
    model_width = tokens.shape[1]
    node_count = lax.axis_size("node")
    local_count = lax.axis_size("local")
    exp_node = local_count // TEAM
    flight = node_count * exp_node
    flight_ids = jnp.arange(flight, dtype=jnp.int32) * GSIZE
    picked = pack_matrix(expert_ids, flight_ids)
    dispatched = jnp.einsum(
        "fct,td->fcd", picked.astype(jnp.bfloat16), tokens, preferred_element_type=jnp.float32
    ).astype(jnp.bfloat16)
    gate_local = gate_weight[0]
    up_local = up_weight[0]
    down_local = down_weight[0]
    spread = jnp.repeat(dispatched, TEAM, axis=0)
    arrived_part = lax.all_to_all(
        spread, ("node", "local"), split_axis=0, concat_axis=0, tiled=True
    )
    row_count = arrived_part.shape[1]
    row_block = arrived_part.reshape(-1, model_width)
    gate_part = jnp.dot(row_block, gate_local, preferred_element_type=jnp.float32)
    up_part = jnp.dot(row_block, up_local, preferred_element_type=jnp.float32)
    hidden = (jax.nn.silu(gate_part) * up_part).astype(jnp.bfloat16)
    partial_value = jnp.dot(hidden, down_local, preferred_element_type=jnp.float32).astype(
        jnp.bfloat16
    )
    partial_value = partial_value.reshape(-1, row_count, model_width)
    returned_parts = lax.all_to_all(
        partial_value, ("node", "local"), split_axis=0, concat_axis=0, tiled=True
    )
    returned_parts = returned_parts.reshape(flight, TEAM, CAP, model_width)
    returned = jnp.sum(returned_parts, axis=1, dtype=jnp.float32).astype(jnp.bfloat16)
    weights_now = token_weights(expert_ids, route_scores, flight_ids)
    coefficient = picked.astype(jnp.float32) * weights_now.T[:, None, :]
    combined = jnp.einsum("fct,fcd->td", coefficient, returned.astype(jnp.float32))
    return combined.astype(jnp.bfloat16)


def solution(mesh):
    in_specs = (
        P(("rep", "node", "local"), None),
        P(("rep", "node", "local"), None),
        P(("rep", "node", "local"), None),
        P(("node", "local"), None, None),
        P(("node", "local"), None, None),
        P(("node", "local"), None, None),
    )
    out_specs = P(("rep", "node", "local"), None)
    return jax.shard_map(local, mesh=mesh, in_specs=in_specs, out_specs=out_specs, check_vma=False)
```

profile of v0, /device:TPU:0, one launch (start us, length us, event | category | flops | bytes accessed | tf_op | source)
XLA Modules:
  0.0 290.9 jit_solution(4960847778709009192)
XLA Ops:
  0.0 0.0 copy-start
  0.0 0.9 compare_reduce_fusion
  1.0 1.2 reduce-window.6
  2.2 0.1 slice.12
  2.3 0.1 copy.17
  2.4 0.1 copy.18
  2.5 0.1 add_bitcast_fusion
  2.6 0.0 copy-done
  2.6 0.5 convolution_convert_fusion.1
  3.1 0.6 broadcast_in_dim.2
  3.8 130.0 %all_to_all.10 = bf16[16,18,7168]{2,1,0:T(8,128)(2,1)} all-to-all(bf16[16,18,7168]{2,1,0:T(8,128)(2,1)S(1)} %bitcast.41), channel_id=1, replica_groups=mesh['rep'=2,'node'=2,'local'=8] {'node','local'}, dimensions={0} | all-to-all | bytes 8257536 | tf_op jit(solution)/shard_map/all_to_all | solution.py:43
  133.8 5.6 %reshape.41 = bf16[288,7168]{1,0:T(8,128)(2,1)} reshape(bf16[16,18,7168]{2,1,0:T(8,128)(2,1)} %all_to_all.10) | data formatting | bytes 8257536 | tf_op jit(solution)/shard_map/reshape | solution.py:47
  139.4 6.6 %fusion.4 = f32[288,512]{1,0:T(8,128)S(1)} fusion(bf16[288,7168]{1,0:T(8,128)(2,1)} %reshape.41, bf16[1,7168,512]{2,1,0:T(8,128)(2,1)} %param.9), kind=kOutput, calls=%fused_computation.7 | convolution fusion | flops 2113929216 | bytes 12058624 | tf_op jit(solution)/shard_map/dot_general | solution.py:48
  146.0 12.9 %convolution_convert_fusion = bf16[288,7168]{1,0:T(8,128)(2,1)} fusion(bf16[1,512,7168]{2,1,0:T(8,128)(2,1)} %param.11, bf16[288,7168]{1,0:T(8,128)(2,1)} %reshape.41, bf16[1,7168,512]{2,1,0:T(8,128)(2,1)} %param.10, f32[288,512]{1,0:T(8,128)S(1)} %fusion.4), kind=kOutput, calls=%fused_computation | convolution fusion | flops 4230807552 | bytes 23527424 | tf_op jit(solution)/shard_map/dot_general | solution.py:51
  158.9 5.6 %reshape.42 = bf16[16,18,7168]{2,1,0:T(8,128)(2,1)} reshape(bf16[288,7168]{1,0:T(8,128)(2,1)} %convolution_convert_fusion) | data formatting | bytes 8257536 | tf_op jit(solution)/shard_map/reshape | solution.py:54
  164.5 0.0 copy-start.2
  164.5 0.0 copy-start.1
  164.5 4.8 %all-to-all-start.1 = ((bf16[16,18,7168]{2,1,0:T(8,128)(2,1)}), bf16[16,18,7168]{2,1,0:T(8,128)(2,1)}, u32[]{:S(2)}, u32[]{:S(2)}) async-start(bf16[16,18,7168]{2,1,0:T(8,128)(2,1)} %reshape.42), calls=%async_computation.1 | async-start | bytes 11010048 | tf_op jit(solution)/shard_map/all_to_all | solution.py:55
  169.3 0.0 copy-done.2
  169.3 0.0 copy-done.1
  169.3 0.1 select_reduce_fusion
  169.4 115.9 %all-to-all-done.1 = bf16[16,18,7168]{2,1,0:T(8,128)(2,1)} async-done(((bf16[16,18,7168]{2,1,0:T(8,128)(2,1)}), bf16[16,18,7168]{2,1,0:T(8,128)(2,1)}, u32[]{:S(2)}, u32[]{:S(2)}) %all-to-all-start.1) | async-done | bytes 4128800 | tf_op jit(solution)/shard_map/all_to_all | solution.py:55
  285.3 3.6 %bitcast_reduce_fusion = bf16[4,18,7168]{2,1,0:T(8,128)(2,1)S(1)} fusion(bf16[16,18,7168]{2,1,0:T(8,128)(2,1)} %all-to-all-done.1), kind=kLoop, calls=%fused_computation.9 | loop fusion | flops 1548288 | bytes 5160960 | tf_op jit(solution)/shard_map/reduce_sum | solution.py:59
  288.9 2.0 fusion
  (9 shorter events, 0.1 us)
Async XLA Ops:
  0.0 2.6 copy-start
  164.5 4.8 %copy-start.2 = (f32[144,8]{0,1:T(8,128)S(1)}, f32[144,8]{0,1:T(8,128)}, u32[]{:S(2)}) copy-start(f32[144,8]{0,1:T(8,128)} %param.8) | copy-start | bytes 13828
  164.5 4.8 %copy-start.1 = (s32[144,8]{0,1:T(8,128)S(1)}, s32[144,8]{0,1:T(8,128)}, u32[]{:S(2)}) copy-start(s32[144,8]{0,1:T(8,128)} %param.7) | copy-start | bytes 13828
  164.5 120.8 %all-to-all-start.1 = ((bf16[16,18,7168]{2,1,0:T(8,128)(2,1)}), bf16[16,18,7168]{2,1,0:T(8,128)(2,1)}, u32[]{:S(2)}, u32[]{:S(2)}) async-start(bf16[16,18,7168]{2,1,0:T(8,128)(2,1)} %reshape.42), calls=%async_computation.1 | async-start | bytes 11010048 | tf_op jit(solution)/shard_map/all_to_all | solution.py:55
where the time goes:
time: 296 us; the launch traced here: 291 us
  blocking collectives  130 us (44%)
  waiting for transfers between devices  116 us (39%)
  matrix products  22.1 us (7%)
  local copies, waits for them, and re-layouts  12.2 us (4%)
  other arithmetic  6.01 us (2%)
  starting transfers between devices  4.75 us (2%)
    all_to_all x1, blocking collectives, local(): lax.all_to_all(spread, ('node', 'local'), split_axis=0, concat_axis=0, ti...  130 us
    all_to_all x1, waiting for transfers between devices, local(): lax.all_to_all(partial_value, ('node', 'local'), split_axis=0, concat_axi...  116 us
    dot_general x1, matrix products, local(): jnp.dot(hidden, down_local, preferred_element_type=jnp.float32)  12.9 us
    dot_general x1, matrix products, local(): jnp.dot(row_block, gate_local, preferred_element_type=jnp.float32)  6.62 us
  transfers between devices with their start and end apart: 1, of which 1 were waited for; matrix products, arithmetic and copies ran while one was open for 0% of the time, Pallas kernels for 0%

commit v1 on v0

v1 whole, which is shorter than its diff:
```python
import jax
import jax.numpy as jnp
from jax import lax
from jax.sharding import PartitionSpec as P

TEAM = 4
CAP = 18
GSIZE = 32
ROW_TILE = 8

route_scale = 2.5


def swap(value, axis, pairs):
    return lax.ppermute(value, axis, pairs)


def total(*terms):
    summed = terms[0].astype(jnp.float32)
    for term in terms[1:]:
        summed = summed + term.astype(jnp.float32)
    return summed.astype(jnp.bfloat16)


def local(tokens, expert_ids, route_scores, gate_weight, up_weight, down_weight):
    model_width = tokens.shape[1]
    half = model_width // 2
    node_count = lax.axis_size("node")
    local_count = lax.axis_size("local")
    teams = local_count // TEAM
    node = lax.axis_index("node")
    team = lax.axis_index("local") // TEAM

    slots = -(-(node_count * CAP) // ROW_TILE) * ROW_TILE
    offsets = [(n, d) for n in range(node_count) for d in range(teams)]
    flight_ids = jnp.stack(
        [((node + n) % node_count * teams + (team + d) % teams) * GSIZE for n, d in offsets]
    ).astype(jnp.int32)

    hits = expert_ids[:, None, :] == flight_ids[None, :, None]
    matched = jnp.any(hits, axis=2)
    slot_index = jnp.cumsum(matched.astype(jnp.int32), axis=0) - 1 + CAP * node
    slot_iota = jnp.arange(slots, dtype=jnp.int32)
    picked = matched.T[:, None, :] & (slot_index.T[:, None, :] == slot_iota[None, :, None])
    picked = picked.astype(jnp.bfloat16)
    dispatched = jnp.einsum(
        "fct,td->fcd", picked, tokens, preferred_element_type=jnp.float32
    ).astype(jnp.bfloat16)

    cores = [(n, (n + 1) % node_count) for n in range(node_count)]
    flip_y = [(i, i ^ 1) for i in range(local_count)]
    flip_z = [(i, i ^ 2) for i in range(local_count)]

    def to_team(d):
        return [(i, (i + d * TEAM) % local_count) for i in range(local_count)]

    got = swap(dispatched[teams:], "node", cores)
    blocks = dispatched[:teams] + got

    own = blocks[0]
    own_y = swap(own, "local", flip_y)
    own_z = swap(own, "local", flip_z)
    own_d = jnp.concatenate(
        [
            swap(own_y[:, :half], "local", flip_z),
            swap(own_z[:, half:], "local", flip_y),
        ],
        axis=1,
    )
    rows = [own, own_y, own_z, own_d]
    for d in range(1, teams):
        far = swap(blocks[d], "local", to_team(d))
        far_z = swap(far, "local", flip_z)
        far_y = swap(far, "local", flip_y)
        far_d = swap(far_z, "local", flip_y)
        rows += [far, far_y, far_z, far_d]

    row_block = jnp.concatenate(rows, axis=0)
    gate_part = jnp.dot(row_block, gate_weight[0], preferred_element_type=jnp.float32)
    up_part = jnp.dot(row_block, up_weight[0], preferred_element_type=jnp.float32)
    hidden = (jax.nn.silu(gate_part) * up_part).astype(jnp.bfloat16)
    partial = jnp.dot(hidden, down_weight[0], preferred_element_type=jnp.float32).astype(
        jnp.bfloat16
    )
    parts = [partial[i * slots : (i + 1) * slots] for i in range(TEAM * teams)]

    own, own_y, own_z, own_d = parts[:TEAM]
    back_z = swap(own_d[:, :half], "local", flip_z)
    back_y = swap(own_d[:, half:], "local", flip_y)
    own_y = jnp.concatenate([total(own_y[:, :half], back_z), own_y[:, half:]], axis=1)
    own_z = jnp.concatenate([own_z[:, :half], total(own_z[:, half:], back_y)], axis=1)
    sums = [total(own, swap(own_y, "local", flip_y), swap(own_z, "local", flip_z))]
    for d in range(1, teams):
        far, far_y, far_z, far_d = parts[TEAM * d : TEAM * (d + 1)]
        far_z = total(far_z, swap(far_d, "local", flip_y))
        far = total(far, swap(far_y, "local", flip_y), swap(far_z, "local", flip_z))
        sums.append(swap(far, "local", to_team(teams - d)))
    mine = jnp.stack(sums)
    theirs = swap(mine, "node", cores)
    returned = jnp.concatenate([mine, theirs]).reshape(-1, model_width)

    gate_values = route_scale * route_scores / jnp.sum(route_scores, axis=1, keepdims=True)
    weight = jnp.sum(gate_values * jnp.any(hits, axis=1), axis=1)
    placed = jnp.dot(
        picked.reshape(-1, picked.shape[2]).T, returned, preferred_element_type=jnp.float32
    )
    return (weight[:, None] * placed).astype(jnp.bfloat16)


def solution(mesh):
    in_specs = (
        P(("rep", "node", "local"), None),
        P(("rep", "node", "local"), None),
        P(("rep", "node", "local"), None),
        P(("node", "local"), None, None),
        P(("node", "local"), None, None),
        P(("node", "local"), None, None),
    )
    out_specs = P(("rep", "node", "local"), None)
    return jax.shard_map(local, mesh=mesh, in_specs=in_specs, out_specs=out_specs, check_vma=False)
```

time: 296 us -> 166 us (0.56); the launches traced: 291 us -> 166 us
  blocking collectives: 130 us -> 0 us
  starting transfers between devices: 4.75 us -> 25.7 us
  waiting for transfers between devices: 116 us -> 109 us
  local copies, waits for them, and re-layouts: 12.2 us -> 5.61 us
    all_to_all x1 -> x0, blocking collectives: 130 us -> none  [local(): lax.all_to_all(spread, ('node', 'local'), split_axis=0, concat_axis=0, ti...]
    all_to_all x1 -> x0, waiting for transfers between devices: 116 us -> none  [local(): lax.all_to_all(partial_value, ('node', 'local'), split_axis=0, concat_axi...]
    ppermute x0 -> x18, waiting for transfers between devices: none -> 109 us  [swap(): return lax.ppermute(value, axis, pairs)]
    ppermute x0 -> x18, starting transfers between devices: none -> 25.7 us  [swap(): return lax.ppermute(value, axis, pairs)]
    reshape x2 -> x0, local copies, waits for them, and re-layouts: 11.2 us -> none  [the longest x1 5.61 us: local(): partial_value = partial_value.reshape(-1, row_count, model_width)]
    all_to_all x1 -> x0, starting transfers between devices: 4.75 us -> none  [local(): lax.all_to_all(partial_value, ('node', 'local'), split_axis=0, concat_axi...]
    reduce_sum x3 -> x2, other arithmetic: 3.71 us -> 0.05 us  [the longest x1 0.03 us: local(): weight = jnp.sum(gate_values * jnp.any(hits, axis=1), axis=1)]
  transfers between devices with their start and end apart: 1 -> 18, of which waited for: 1 -> 16; matrix products, arithmetic and copies ran while one was open for 0% -> 1% of each run, Pallas kernels for 0% -> 0%
where the time goes in v1:
time: 166 us
  waiting for transfers between devices  109 us (66%)
  starting transfers between devices  25.7 us (15%)
  matrix products  20.3 us (12%)
  local copies, waits for them, and re-layouts  5.61 us (3%)
  other arithmetic  4.43 us (3%)
    ppermute x18, waiting for transfers between devices, swap(): return lax.ppermute(value, axis, pairs)  109 us
    ppermute x18, starting transfers between devices, swap(): return lax.ppermute(value, axis, pairs)  25.7 us
    dot_general x1, matrix products, local(): jnp.dot(hidden, down_weight[0], preferred_element_type=jnp.float32)  13.7 us
    dot_general x1, matrix products, local(): jnp.dot(picked.reshape(-1, picked.shape[2]).T, returned, preferred_elemen...  3.33 us
  transfers between devices with their start and end apart: 18, of which 16 were waited for; matrix products, arithmetic and copies ran while one was open for 1% of the time, Pallas kernels for 0%

profile of v1, /device:TPU:0, one launch (start us, length us, event | category | flops | bytes accessed | tf_op | source)
XLA Modules:
  0.0 165.5 jit_solution(10443517702907917513)
XLA Ops:
  0.1 0.9 compare_reduce_fusion.1
  1.0 1.2 reduce-window.6
  2.3 0.1 copy.10
  2.7 0.7 convolution_convert_fusion.1
  3.5 0.5 collective-permute-start
  4.0 2.4 %collective-permute-done = bf16[2,40,7168]{2,1,0:T(8,128)(2,1)S(1)} collective-permute-done((bf16[2,40,7168]{2,1,0:T(8,128)(2,1)S(1)}, bf16[2,40,7168]{2,1,0:T(8,128)(2,1)S(1)}, u32[]{:S(2)}, u32[]{:S(2)}) %collective-permute-start) | collective-permute-done | bytes 1146912 | tf_op jit(solution)/shard_map/ppermute | solution.py:15
  6.5 0.1 slice_add_fusion
  6.7 2.9 %collective-permute-start.1 = (bf16[40,7168]{1,0:T(8,128)(2,1)S(1)}, bf16[40,7168]{1,0:T(8,128)(2,1)S(1)}, u32[]{:S(2)}, u32[]{:S(2)}) collective-permute-start(bf16[40,7168]{1,0:T(8,128)(2,1)S(1)} %get-tuple-element.18), channel_id=1, source_target_pairs={{0,1},{1,0},{2,3},{3,2},{4,5},{5,4},{6,7},{7,6},{8,9},{9,8},{10,11... | collective-permute-start | bytes 1720328 | tf_op jit(solution)/shard_map/ppermute | solution.py:15
  9.6 1.6 collective-permute-start.2
  11.2 2.6 %collective-permute-start.5 = (bf16[40,7168]{1,0:T(8,128)(2,1)S(1)}, bf16[40,7168]{1,0:T(8,128)(2,1)S(1)}, u32[]{:S(2)}, u32[]{:S(2)}) collective-permute-start(bf16[40,7168]{1,0:T(8,128)(2,1)S(1)} %get-tuple-element.17), channel_id=1, source_target_pairs={{0,4},{1,5},{2,6},{3,7},{4,0},{5,1},{6,2},{7,3},{8,12},{9,13},{10,... | collective-permute-start | bytes 1720328 | tf_op jit(solution)/shard_map/ppermute | solution.py:15
  13.8 9.1 %collective-permute-done.1 = bf16[40,7168]{1,0:T(8,128)(2,1)S(1)} collective-permute-done((bf16[40,7168]{1,0:T(8,128)(2,1)S(1)}, bf16[40,7168]{1,0:T(8,128)(2,1)S(1)}, u32[]{:S(2)}, u32[]{:S(2)}) %collective-permute-start.1) | collective-permute-done | bytes 573472 | tf_op jit(solution)/shard_map/ppermute | solution.py:15
  22.9 1.9 %collective-permute-start.3 = (bf16[40,3584]{1,0:T(8,128)(2,1)S(1)}, bf16[40,3584]{1,0:T(8,128)(2,1)S(1)}, u32[]{:S(2)}, u32[]{:S(2)}) collective-permute-start(bf16[40,3584]{1,0:T(8,128)(2,1)S(1)} %slice.94), channel_id=1, source_target_pairs={{0,2},{1,3},{2,0},{3,1},{4,6},{5,7},{6,4},{7,5},{8,10},{9,11},{10,... | collective-permute-start | bytes 860168 | tf_op jit(solution)/shard_map/ppermute | solution.py:15
  24.8 12.9 %collective-permute-done.2 = bf16[40,7168]{1,0:T(8,128)(2,1)S(1)} collective-permute-done((bf16[40,7168]{1,0:T(8,128)(2,1)S(1)}, bf16[40,7168]{1,0:T(8,128)(2,1)S(1)}, u32[]{:S(2)}, u32[]{:S(2)}) %collective-permute-start.2) | collective-permute-done | bytes 573472 | tf_op jit(solution)/shard_map/ppermute | solution.py:15
  37.7 0.1 collective-permute-start.4
  37.8 0.1 collective-permute-done.5
  37.9 1.8 %collective-permute-start.6 = (bf16[40,7168]{1,0:T(8,128)(2,1)S(1)}, bf16[40,7168]{1,0:T(8,128)(2,1)S(1)}, u32[]{:S(2)}, u32[]{:S(2)}) collective-permute-start(bf16[40,7168]{1,0:T(8,128)(2,1)S(1)} %collective-permute-done.5), channel_id=1, source_target_pairs={{0,1},{1,0},{2,3},{3,2},{4,5},{5,4},{6,7},{7,6},{8,9},{9,8},{10,11... | collective-permute-start | bytes 1720328 | tf_op jit(solution)/shard_map/ppermute | solution.py:15
  39.8 1.1 collective-permute-start.7
  41.0 2.9 %collective-permute-done.3 = bf16[40,3584]{1,0:T(8,128)(2,1)S(1)} collective-permute-done((bf16[40,3584]{1,0:T(8,128)(2,1)S(1)}, bf16[40,3584]{1,0:T(8,128)(2,1)S(1)}, u32[]{:S(2)}, u32[]{:S(2)}) %collective-permute-start.3) | collective-permute-done | bytes 286752 | tf_op jit(solution)/shard_map/ppermute | solution.py:15
  43.9 3.6 %collective-permute-done.4 = bf16[40,3584]{1,0:T(8,128)(2,1)S(1)} collective-permute-done((bf16[40,3584]{1,0:T(8,128)(2,1)S(1)}, bf16[40,3584]{1,0:T(8,128)(2,1)S(1)}, u32[]{:S(2)}, u32[]{:S(2)}) %collective-permute-start.4) | collective-permute-done | bytes 286752 | tf_op jit(solution)/shard_map/ppermute | solution.py:15
  47.6 7.5 %collective-permute-done.7 = bf16[40,7168]{1,0:T(8,128)(2,1)S(1)} collective-permute-done((bf16[40,7168]{1,0:T(8,128)(2,1)S(1)}, bf16[40,7168]{1,0:T(8,128)(2,1)S(1)}, u32[]{:S(2)}, u32[]{:S(2)}) %collective-permute-start.7) | collective-permute-done | bytes 573472 | tf_op jit(solution)/shard_map/ppermute | solution.py:15
  55.1 0.4 collective-permute-start.8
  55.4 1.2 collective-permute-done.6
  56.7 12.2 %collective-permute-done.8 = bf16[40,7168]{1,0:T(8,128)(2,1)S(1)} collective-permute-done((bf16[40,7168]{1,0:T(8,128)(2,1)S(1)}, bf16[40,7168]{1,0:T(8,128)(2,1)S(1)}, u32[]{:S(2)}, u32[]{:S(2)}) %collective-permute-start.8) | collective-permute-done | bytes 573472 | tf_op jit(solution)/shard_map/ppermute | solution.py:15
  69.0 2.1 %copy-done.2 = bf16[320,7168]{1,0:T(8,128)(2,1)} copy-done((bf16[320,7168]{1,0:T(8,128)(2,1)}, bf16[320,7168]{1,0:T(8,128)(2,1)S(1)}, u32[]{:S(2)}) %copy-start.2) | copy-done | bytes 4587544
  71.1 2.5 %fusion.3 = f32[320,512]{1,0:T(8,128)S(1)} fusion(bf16[320,7168]{1,0:T(8,128)(2,1)S(1)} %constant_dynamic-update-slice_fusion, bf16[1,7168,512]{2,1,0:T(8,128)(2,1)S(1)} %bitcast.57), kind=kOutput, calls=%fused_computation.6 | convolution fusion | flops 2348810240 | bytes 12582912 | tf_op jit(solution)/shard_map/dot_general | solution.py:80
  73.6 13.7 %convolution_convert_fusion = bf16[320,7168]{1,0:T(8,128)(2,1)} fusion(bf16[1,512,7168]{2,1,0:T(8,128)(2,1)} %param.11, f32[320,512]{1,0:T(8,128)S(1)} %fusion.3, bf16[320,7168]{1,0:T(8,128)(2,1)} %copy-done.2, bf16[1,7168,512]{2,1,0:T(8,128)(2,1)} %param.9), kind=kOutput, calls=%fused_computation | convolution fusion | flops 4700897280 | bytes 24510464 | tf_op jit(solution)/shard_map/dot_general | solution.py:82
  87.3 1.4 fusion.30
  88.7 0.7 collective-permute-start.11
  89.4 1.5 collective-permute-start.9
  90.9 1.3 fusion.31
  92.2 1.6 collective-permute-start.14
  93.8 4.7 %collective-permute-done.11 = bf16[40,3584]{1,0:T(8,128)(2,1)S(1)} collective-permute-done((bf16[40,3584]{1,0:T(8,128)(2,1)S(1)}, bf16[40,3584]{1,0:T(8,128)(2,1)S(1)}, u32[]{:S(2)}, u32[]{:S(2)}) %collective-permute-start.11) | collective-permute-done | bytes 286752 | tf_op jit(solution)/shard_map/ppermute | solution.py:15
  98.6 0.1 add_convert_fusion.4
  98.8 0.7 collective-permute-start.10
  99.5 1.6 collective-permute-start.12
  101.1 1.5 collective-permute-start.13
  102.6 8.3 %collective-permute-done.14 = bf16[40,7168]{1,0:T(8,128)(2,1)S(1)} collective-permute-done((bf16[40,7168]{1,0:T(8,128)(2,1)S(1)}, bf16[40,7168]{1,0:T(8,128)(2,1)S(1)}, u32[]{:S(2)}, u32[]{:S(2)}) %collective-permute-start.14) | collective-permute-done | bytes 573472 | tf_op jit(solution)/shard_map/ppermute | solution.py:15
  110.9 12.3 %collective-permute-done.10 = bf16[40,7168]{1,0:T(8,128)(2,1)S(1)} collective-permute-done((bf16[40,7168]{1,0:T(8,128)(2,1)S(1)}, bf16[40,7168]{1,0:T(8,128)(2,1)S(1)}, u32[]{:S(2)}, u32[]{:S(2)}) %collective-permute-start.10) | collective-permute-done | bytes 573472 | tf_op jit(solution)/shard_map/ppermute | solution.py:15
  123.1 0.3 fusion.13
  123.5 1.7 %collective-permute-start.15 = (bf16[40,7168]{1,0:T(8,128)(2,1)S(1)}, bf16[40,7168]{1,0:T(8,128)(2,1)S(1)}, u32[]{:S(2)}, u32[]{:S(2)}) collective-permute-start(bf16[40,7168]{1,0:T(8,128)(2,1)S(1)} %get-tuple-element.8), channel_id=1, source_target_pairs={{0,2},{1,3},{2,0},{3,1},{4,6},{5,7},{6,4},{7,5},{8,10},{9,11},{10,... | collective-permute-start | bytes 1720328 | tf_op jit(solution)/shard_map/ppermute | solution.py:15
  125.2 7.3 %collective-permute-done.13 = bf16[40,7168]{1,0:T(8,128)(2,1)S(1)} collective-permute-done((bf16[40,7168]{1,0:T(8,128)(2,1)S(1)}, bf16[40,7168]{1,0:T(8,128)(2,1)S(1)}, u32[]{:S(2)}, u32[]{:S(2)}) %collective-permute-start.13) | collective-permute-done | bytes 573472 | tf_op jit(solution)/shard_map/ppermute | solution.py:15
  132.5 0.8 collective-permute-done.15
  133.3 0.2 add_convert_fusion
  133.5 3.5 %collective-permute-start.16 = (bf16[40,7168]{1,0:T(8,128)(2,1)S(1)}, bf16[40,7168]{1,0:T(8,128)(2,1)S(1)}, u32[]{:S(2)}, u32[]{:S(2)}) collective-permute-start(bf16[40,7168]{1,0:T(8,128)(2,1)S(1)} %add_convert_fusion), channel_id=1, source_target_pairs={{0,4},{1,5},{2,6},{3,7},{4,0},{5,1},{6,2},{7,3},{8,12},{9,13},{10,... | collective-permute-start | bytes 1720328 | tf_op jit(solution)/shard_map/ppermute | solution.py:15
  137.0 21.0 %collective-permute-done.16 = bf16[40,7168]{1,0:T(8,128)(2,1)S(1)} collective-permute-done((bf16[40,7168]{1,0:T(8,128)(2,1)S(1)}, bf16[40,7168]{1,0:T(8,128)(2,1)S(1)}, u32[]{:S(2)}, u32[]{:S(2)}) %collective-permute-start.16) | collective-permute-done | bytes 573472 | tf_op jit(solution)/shard_map/ppermute | solution.py:15
  158.0 1.1 pad_maximum_fusion
  159.1 3.1 %collective-permute-done.17 = bf16[2,40,7168]{2,1,0:T(8,128)(2,1)} collective-permute-done((bf16[2,40,7168]{2,1,0:T(8,128)(2,1)}, bf16[2,40,7168]{2,1,0:T(8,128)(2,1)}, u32[]{:S(2)}, u32[]{:S(2)}) %collective-permute-start.17) | collective-permute-done | bytes 1146912 | tf_op jit(solution)/shard_map/ppermute | solution.py:15
  162.2 3.3 %fusion.1 = bf16[144,7168]{1,0:T(8,128)(2,1)} fusion(bf16[2,40,7168]{2,1,0:T(8,128)(2,1)} %collective-permute-done.17, bf16[1,40,7168]{2,1,0:T(8,128)(2,1)S(1)} %bitcast.50, bf16[1,40,7168]{2,1,0:T(8,128)(2,1)S(1)} %get-tuple-element.7, f32[144]{0:T(256)S(1)} %select_reduce_fusion, s32[4,144]{1,0:T(4,128)S(1)} %fusion.27, pred[4,144]{1,0:T(4,128)(4,1)S(1)} %bitcast.54), kind=kOutput, calls=%fused_computation.4 | convolution fusion | flops 334705664 | bytes 4361600 | tf_op jit(solution)/shard_map/dot_general | solution.py:104
  (41 shorter events, 1.1 us)
Async XLA Ops:
  0.0 2.7 %copy-start = (bf16[144,7168]{1,0:T(8,128)(2,1)S(1)}, bf16[144,7168]{1,0:T(8,128)(2,1)}, u32[]{:S(2)}) copy-start(bf16[144,7168]{1,0:T(8,128)(2,1)} %param.6) | copy-start | bytes 6193156
  3.5 3.0 %collective-permute-start = (bf16[2,40,7168]{2,1,0:T(8,128)(2,1)S(1)}, bf16[2,40,7168]{2,1,0:T(8,128)(2,1)S(1)}, u32[]{:S(2)}, u32[]{:S(2)}) collective-permute-start(bf16[2,40,7168]{2,1,0:T(8,128)(2,1)S(1)} %slice.92), channel_id=1, source_target_pairs={{0,8},{8,0},{1,9},{9,1},{2,10},{10,2},{3,11},{11,3},{4,12},{12,4},... | collective-permute-start | bytes 3440648 | tf_op jit(solution)/shard_map/ppermute | solution.py:15
  6.5 64.6 %slice-start = ((s8[7340032]{0:T(1024)(128)(4,1)}), s8[4194304]{0:T(1024)(128)(4,1)S(1)}, s32[]{:S(2)}) async-start(s8[7340032]{0:T(1024)(128)(4,1)} %bitcast.56), calls=%async_computation | async-start | bytes 8388608
  6.7 16.2 %collective-permute-start.1 = (bf16[40,7168]{1,0:T(8,128)(2,1)S(1)}, bf16[40,7168]{1,0:T(8,128)(2,1)S(1)}, u32[]{:S(2)}, u32[]{:S(2)}) collective-permute-start(bf16[40,7168]{1,0:T(8,128)(2,1)S(1)} %get-tuple-element.18), channel_id=1, source_target_pairs={{0,1},{1,0},{2,3},{3,2},{4,5},{5,4},{6,7},{7,6},{8,9},{9,8},{10,11... | collective-permute-start | bytes 1720328 | tf_op jit(solution)/shard_map/ppermute | solution.py:15
  9.6 28.0 %collective-permute-start.2 = (bf16[40,7168]{1,0:T(8,128)(2,1)S(1)}, bf16[40,7168]{1,0:T(8,128)(2,1)S(1)}, u32[]{:S(2)}, u32[]{:S(2)}) collective-permute-start(bf16[40,7168]{1,0:T(8,128)(2,1)S(1)} %get-tuple-element.18), channel_id=1, source_target_pairs={{0,2},{1,3},{2,0},{3,1},{4,6},{5,7},{6,4},{7,5},{8,10},{9,11},{10,... | collective-permute-start | bytes 1720328 | tf_op jit(solution)/shard_map/ppermute | solution.py:15
  11.2 26.7 %collective-permute-start.5 = (bf16[40,7168]{1,0:T(8,128)(2,1)S(1)}, bf16[40,7168]{1,0:T(8,128)(2,1)S(1)}, u32[]{:S(2)}, u32[]{:S(2)}) collective-permute-start(bf16[40,7168]{1,0:T(8,128)(2,1)S(1)} %get-tuple-element.17), channel_id=1, source_target_pairs={{0,4},{1,5},{2,6},{3,7},{4,0},{5,1},{6,2},{7,3},{8,12},{9,13},{10,... | collective-permute-start | bytes 1720328 | tf_op jit(solution)/shard_map/ppermute | solution.py:15
  22.9 48.2 %slice-start.1 = ((s8[7340032]{0:T(1024)(128)(4,1)}), s8[3145728]{0:T(1024)(128)(4,1)S(1)}, s32[]{:S(2)}) async-start(s8[7340032]{0:T(1024)(128)(4,1)} %bitcast.56), calls=%async_computation.1 | async-start | bytes 6291456
  22.9 21.0 %collective-permute-start.3 = (bf16[40,3584]{1,0:T(8,128)(2,1)S(1)}, bf16[40,3584]{1,0:T(8,128)(2,1)S(1)}, u32[]{:S(2)}, u32[]{:S(2)}) collective-permute-start(bf16[40,3584]{1,0:T(8,128)(2,1)S(1)} %slice.94), channel_id=1, source_target_pairs={{0,2},{1,3},{2,0},{3,1},{4,6},{5,7},{6,4},{7,5},{8,10},{9,11},{10,... | collective-permute-start | bytes 860168 | tf_op jit(solution)/shard_map/ppermute | solution.py:15
  37.7 9.8 %collective-permute-start.4 = (bf16[40,3584]{1,0:T(8,128)(2,1)S(1)}, bf16[40,3584]{1,0:T(8,128)(2,1)S(1)}, u32[]{:S(2)}, u32[]{:S(2)}) collective-permute-start(bf16[40,3584]{1,0:T(8,128)(2,1)S(1)} %slice.95), channel_id=1, source_target_pairs={{0,1},{1,0},{2,3},{3,2},{4,5},{5,4},{6,7},{7,6},{8,9},{9,8},{10,11... | collective-permute-start | bytes 860168 | tf_op jit(solution)/shard_map/ppermute | solution.py:15
  37.9 18.7 %collective-permute-start.6 = (bf16[40,7168]{1,0:T(8,128)(2,1)S(1)}, bf16[40,7168]{1,0:T(8,128)(2,1)S(1)}, u32[]{:S(2)}, u32[]{:S(2)}) collective-permute-start(bf16[40,7168]{1,0:T(8,128)(2,1)S(1)} %collective-permute-done.5), channel_id=1, source_target_pairs={{0,1},{1,0},{2,3},{3,2},{4,5},{5,4},{6,7},{7,6},{8,9},{9,8},{10,11... | collective-permute-start | bytes 1720328 | tf_op jit(solution)/shard_map/ppermute | solution.py:15
  39.8 15.3 %collective-permute-start.7 = (bf16[40,7168]{1,0:T(8,128)(2,1)S(1)}, bf16[40,7168]{1,0:T(8,128)(2,1)S(1)}, u32[]{:S(2)}, u32[]{:S(2)}) collective-permute-start(bf16[40,7168]{1,0:T(8,128)(2,1)S(1)} %collective-permute-done.5), channel_id=1, source_target_pairs={{0,2},{1,3},{2,0},{3,1},{4,6},{5,7},{6,4},{7,5},{8,10},{9,11},{10,... | collective-permute-start | bytes 1720328 | tf_op jit(solution)/shard_map/ppermute | solution.py:15
  55.1 13.9 %collective-permute-start.8 = (bf16[40,7168]{1,0:T(8,128)(2,1)S(1)}, bf16[40,7168]{1,0:T(8,128)(2,1)S(1)}, u32[]{:S(2)}, u32[]{:S(2)}) collective-permute-start(bf16[40,7168]{1,0:T(8,128)(2,1)S(1)} %collective-permute-done.7), channel_id=1, source_target_pairs={{0,1},{1,0},{2,3},{3,2},{4,5},{5,4},{6,7},{7,6},{8,9},{9,8},{10,11... | collective-permute-start | bytes 1720328 | tf_op jit(solution)/shard_map/ppermute | solution.py:15
  69.0 2.1 %copy-start.2 = (bf16[320,7168]{1,0:T(8,128)(2,1)}, bf16[320,7168]{1,0:T(8,128)(2,1)S(1)}, u32[]{:S(2)}) copy-start(bf16[320,7168]{1,0:T(8,128)(2,1)S(1)} %constant_dynamic-update-slice_fusion) | copy-start | bytes 13762564
  87.3 11.3 %copy-start.1 = (bf16[320,7168]{1,0:T(8,128)(2,1)S(1)}, bf16[320,7168]{1,0:T(8,128)(2,1)}, u32[]{:S(2)}) copy-start(bf16[320,7168]{1,0:T(8,128)(2,1)} %convolution_convert_fusion) | copy-start | bytes 13762564
  88.7 9.8 %collective-permute-start.11 = (bf16[40,3584]{1,0:T(8,128)(2,1)S(1)}, bf16[40,3584]{1,0:T(8,128)(2,1)S(1)}, u32[]{:S(2)}, u32[]{:S(2)}) collective-permute-start(bf16[40,3584]{1,0:T(8,128)(2,1)S(1)} %get-tuple-element.12), channel_id=1, source_target_pairs={{0,1},{1,0},{2,3},{3,2},{4,5},{5,4},{6,7},{7,6},{8,9},{9,8},{10,11... | collective-permute-start | bytes 860168 | tf_op jit(solution)/shard_map/ppermute | solution.py:15
  89.4 9.1 %collective-permute-start.9 = (bf16[40,3584]{1,0:T(8,128)(2,1)S(1)}, bf16[40,3584]{1,0:T(8,128)(2,1)S(1)}, u32[]{:S(2)}, u32[]{:S(2)}) collective-permute-start(bf16[40,3584]{1,0:T(8,128)(2,1)S(1)} %get-tuple-element.11), channel_id=1, source_target_pairs={{0,2},{1,3},{2,0},{3,1},{4,6},{5,7},{6,4},{7,5},{8,10},{9,11},{10,... | collective-permute-start | bytes 860168 | tf_op jit(solution)/shard_map/ppermute | solution.py:15
  92.2 18.6 %collective-permute-start.14 = (bf16[40,7168]{1,0:T(8,128)(2,1)S(1)}, bf16[40,7168]{1,0:T(8,128)(2,1)S(1)}, u32[]{:S(2)}, u32[]{:S(2)}) collective-permute-start(bf16[40,7168]{1,0:T(8,128)(2,1)S(1)} %get-tuple-element.16), channel_id=1, source_target_pairs={{0,1},{1,0},{2,3},{3,2},{4,5},{5,4},{6,7},{7,6},{8,9},{9,8},{10,11... | collective-permute-start | bytes 1720328 | tf_op jit(solution)/shard_map/ppermute | solution.py:15
  98.8 24.4 %collective-permute-start.10 = (bf16[40,7168]{1,0:T(8,128)(2,1)S(1)}, bf16[40,7168]{1,0:T(8,128)(2,1)S(1)}, u32[]{:S(2)}, u32[]{:S(2)}) collective-permute-start(bf16[40,7168]{1,0:T(8,128)(2,1)S(1)} %pad_maximum_fusion.1), channel_id=1, source_target_pairs={{0,1},{1,0},{2,3},{3,2},{4,5},{5,4},{6,7},{7,6},{8,9},{9,8},{10,11... | collective-permute-start | bytes 1720328 | tf_op jit(solution)/shard_map/ppermute | solution.py:15
  99.5 23.7 %collective-permute-start.12 = (bf16[40,7168]{1,0:T(8,128)(2,1)S(1)}, bf16[40,7168]{1,0:T(8,128)(2,1)S(1)}, u32[]{:S(2)}, u32[]{:S(2)}) collective-permute-start(bf16[40,7168]{1,0:T(8,128)(2,1)S(1)} %pad_maximum_fusion.2), channel_id=1, source_target_pairs={{0,2},{1,3},{2,0},{3,1},{4,6},{5,7},{6,4},{7,5},{8,10},{9,11},{10,... | collective-permute-start | bytes 1720328 | tf_op jit(solution)/shard_map/ppermute | solution.py:15
  101.1 58.0 %copy-start.3 = (f32[144,8]{0,1:T(8,128)S(1)}, f32[144,8]{0,1:T(8,128)}, u32[]{:S(2)}) copy-start(f32[144,8]{0,1:T(8,128)} %param.8) | copy-start | bytes 13828
  101.1 31.4 %collective-permute-start.13 = (bf16[40,7168]{1,0:T(8,128)(2,1)S(1)}, bf16[40,7168]{1,0:T(8,128)(2,1)S(1)}, u32[]{:S(2)}, u32[]{:S(2)}) collective-permute-start(bf16[40,7168]{1,0:T(8,128)(2,1)S(1)} %get-tuple-element.15), channel_id=1, source_target_pairs={{0,1},{1,0},{2,3},{3,2},{4,5},{5,4},{6,7},{7,6},{8,9},{9,8},{10,11... | collective-permute-start | bytes 1720328 | tf_op jit(solution)/shard_map/ppermute | solution.py:15
  123.5 9.8 %collective-permute-start.15 = (bf16[40,7168]{1,0:T(8,128)(2,1)S(1)}, bf16[40,7168]{1,0:T(8,128)(2,1)S(1)}, u32[]{:S(2)}, u32[]{:S(2)}) collective-permute-start(bf16[40,7168]{1,0:T(8,128)(2,1)S(1)} %get-tuple-element.8), channel_id=1, source_target_pairs={{0,2},{1,3},{2,0},{3,1},{4,6},{5,7},{6,4},{7,5},{8,10},{9,11},{10,... | collective-permute-start | bytes 1720328 | tf_op jit(solution)/shard_map/ppermute | solution.py:15
  133.5 24.5 %collective-permute-start.16 = (bf16[40,7168]{1,0:T(8,128)(2,1)S(1)}, bf16[40,7168]{1,0:T(8,128)(2,1)S(1)}, u32[]{:S(2)}, u32[]{:S(2)}) collective-permute-start(bf16[40,7168]{1,0:T(8,128)(2,1)S(1)} %add_convert_fusion), channel_id=1, source_target_pairs={{0,4},{1,5},{2,6},{3,7},{4,0},{5,1},{6,2},{7,3},{8,12},{9,13},{10,... | collective-permute-start | bytes 1720328 | tf_op jit(solution)/shard_map/ppermute | solution.py:15
  159.1 3.1 %collective-permute-start.17 = (bf16[2,40,7168]{2,1,0:T(8,128)(2,1)}, bf16[2,40,7168]{2,1,0:T(8,128)(2,1)}, u32[]{:S(2)}, u32[]{:S(2)}) collective-permute-start(bf16[2,40,7168]{2,1,0:T(8,128)(2,1)} %pad_maximum_fusion), channel_id=1, source_target_pairs={{0,8},{8,0},{1,9},{9,1},{2,10},{10,2},{3,11},{11,3},{4,12},{12,4},... | collective-permute-start | bytes 3440648 | tf_op jit(solution)/shard_map/ppermute | solution.py:15

commit v2 on v1

v2 whole, which is shorter than its diff:
```python
import functools

import jax
import jax.numpy as jnp
from jax import lax
from jax.experimental import pallas as pl
from jax.experimental.pallas import tpu as pltpu
from jax.sharding import PartitionSpec as P

TEAM = 4
CAP = 18
GSIZE = 32
CHUNKS = 2
STACK = 2

route_scale = 2.5
VMEM = pl.BlockSpec(memory_space=pltpu.VMEM)
HBM = pl.BlockSpec(memory_space=pl.ANY)


def dot(a, b):
    return jnp.dot(a, b, preferred_element_type=jnp.float32)


def params(mib):
    return pltpu.CompilerParams(vmem_limit_bytes=mib << 20)


def pack_kernel(pick_ref, tokens_ref, *out_refs):
    experts = len(out_refs)
    rows, width = out_refs[0].shape[1:]
    for c in range(CHUNKS):
        acc = None
        for q in range(STACK):
            first = (c * STACK + q) * width
            term = dot(pick_ref[q], tokens_ref[:, first : first + width])
            acc = term if acc is None else acc + term
        acc = acc.astype(jnp.bfloat16)
        for e in range(experts):
            out_refs[e][c] = acc[e * rows : (e + 1) * rows]


def expert_kernel(spread_ref, place_ref, *refs):
    blocks = refs[: CHUNKS * TEAM]
    gate_hbm, up_hbm, down_hbm = refs[CHUNKS * TEAM : CHUNKS * TEAM + 3]
    outs = refs[CHUNKS * TEAM + 3 : 2 * CHUNKS * TEAM + 3]
    gate, up, down, sems = refs[2 * CHUNKS * TEAM + 3 :]
    width = blocks[0].shape[1]
    pieces = CHUNKS * STACK
    copies = []
    for p in range(pieces):
        span = pl.ds(p * width, width)
        copies.append(
            (
                pltpu.make_async_copy(gate_hbm.at[0, span], gate.at[p], sems.at[0, p]),
                pltpu.make_async_copy(up_hbm.at[0, span], up.at[p], sems.at[1, p]),
            )
        )
    downs = [
        pltpu.make_async_copy(
            down_hbm.at[0, :, pl.ds(p * width, width)], down.at[p], sems.at[2, p]
        )
        for p in range(pieces)
    ]
    for pair in copies:
        for copy in pair:
            copy.start()
    for copy in downs:
        copy.start()
    gate_part = up_part = None
    for c in range(CHUNKS):
        stacked = jnp.concatenate([blocks[c * TEAM + b][...] for b in range(TEAM)], axis=0)
        for q in range(STACK):
            p = c * STACK + q
            rows = dot(spread_ref[q], stacked).astype(jnp.bfloat16)
            copies[p][0].wait()
            copies[p][1].wait()
            gate_term = dot(rows, gate[p])
            up_term = dot(rows, up[p])
            gate_part = gate_term if gate_part is None else gate_part + gate_term
            up_part = up_term if up_part is None else up_part + up_term
    hidden = gate_part / (1.0 + jnp.exp(-gate_part)) * up_part
    hidden = hidden.astype(jnp.bfloat16)
    placed = [dot(place_ref[q], hidden).astype(jnp.bfloat16) for q in range(STACK)]
    count = outs[0].shape[0]
    for c in range(CHUNKS):
        acc = None
        for q in range(STACK):
            p = c * STACK + q
            downs[p].wait()
            term = dot(placed[q], down[p])
            acc = term if acc is None else acc + term
        acc = acc.astype(jnp.bfloat16)
        for b in range(TEAM):
            outs[c * TEAM + b][...] = acc[b * count : (b + 1) * count]


def final_kernel(pick_ref, weight_ref, *refs):
    blocks, out_ref = refs[:-1], refs[-1]
    experts = len(blocks) // CHUNKS
    width = blocks[0].shape[1]
    for c in range(CHUNKS):
        stacked = jnp.concatenate(
            [blocks[c * experts + e][...] for e in range(experts)], axis=0
        )
        for q in range(STACK):
            first = (c * STACK + q) * width
            placed = dot(pick_ref[q], stacked)
            out_ref[:, first : first + width] = (placed * weight_ref[...]).astype(jnp.bfloat16)


def total(*terms):
    summed = terms[0].astype(jnp.float32)
    for term in terms[1:]:
        summed = summed + term.astype(jnp.float32)
    return summed.astype(jnp.bfloat16)


def local(tokens, expert_ids, route_scores, gate_weight, up_weight, down_weight):
    token_count, model_width = tokens.shape
    node_count = lax.axis_size("node")
    local_count = lax.axis_size("local")
    teams = local_count // TEAM
    flight = node_count * teams
    node = lax.axis_index("node")
    team = lax.axis_index("local") // TEAM
    slots = node_count * CAP
    rows = STACK * slots
    width = model_width // (CHUNKS * STACK)
    block = jax.ShapeDtypeStruct((rows, width), jnp.bfloat16)

    offsets = [(n, d) for n in range(node_count) for d in range(teams)]
    flight_ids = jnp.stack(
        [((node + n) % node_count * teams + (team + d) % teams) * GSIZE for n, d in offsets]
    ).astype(jnp.int32)
    hits = expert_ids[:, None, :] == flight_ids[None, :, None]
    matched = jnp.any(hits, axis=2)
    slot_index = jnp.cumsum(matched.astype(jnp.int32), axis=0) - 1 + CAP * node
    place = jnp.arange(rows, dtype=jnp.int32)
    stack_of, slot_of = place // slots, place % slots
    chosen = matched.T[:, None, :] & (slot_index.T[:, None, :] == slot_of[None, :, None])
    pick = chosen[None] & (stack_of[None, None, :, None] == jnp.arange(STACK)[:, None, None, None])
    pick = pick.astype(jnp.bfloat16).reshape(STACK, flight * rows, token_count)
    pick_back = jnp.swapaxes(pick, 1, 2)
    gate_values = route_scale * route_scores / jnp.sum(route_scores, axis=1, keepdims=True)
    weight = jnp.sum(gate_values * jnp.any(hits, axis=1), axis=1)[:, None]

    index = jnp.arange(TEAM * rows, dtype=jnp.int32)
    target = index // rows * slots + index % slots
    stack_at = index % rows // slots
    line = jnp.arange(TEAM * slots, dtype=jnp.int32)
    spread = jnp.stack(
        [(line[:, None] == target[None]) & (stack_at[None] == q) for q in range(STACK)]
    ).astype(jnp.bfloat16)
    spread_back = jnp.swapaxes(spread, 1, 2)

    cores = [(n, (n + 1) % node_count) for n in range(node_count)]
    flip_y = [(i, i ^ 1) for i in range(local_count)]
    flip_z = [(i, i ^ 2) for i in range(local_count)]

    def swap_core(value):
        return lax.ppermute(value, "node", cores)

    def swap_y(value):
        return lax.ppermute(value, "local", flip_y)

    def swap_z(value):
        return lax.ppermute(value, "local", flip_z)

    def to_team(value, d):
        pairs = [(i, (i + d * TEAM) % local_count) for i in range(local_count)]
        return lax.ppermute(value, "local", pairs)

    pair = jax.ShapeDtypeStruct((CHUNKS, rows, width), jnp.bfloat16)
    packed = pl.pallas_call(
        pack_kernel,
        out_shape=[pair] * flight,
        in_specs=[VMEM] * 2,
        out_specs=[VMEM] * flight,
        compiler_params=params(40),
        name="pack",
    )(pick, tokens)

    def experts(blocks):
        scratch = (CHUNKS * STACK, width, gate_weight.shape[2])
        return pl.pallas_call(
            expert_kernel,
            out_shape=[block] * (CHUNKS * TEAM),
            in_specs=[VMEM] * (2 + CHUNKS * TEAM) + [HBM] * 3,
            out_specs=[VMEM] * (CHUNKS * TEAM),
            scratch_shapes=[
                pltpu.VMEM(scratch, jnp.bfloat16),
                pltpu.VMEM(scratch, jnp.bfloat16),
                pltpu.VMEM((scratch[0], scratch[2], scratch[1]), jnp.bfloat16),
                pltpu.SemaphoreType.DMA((3, CHUNKS * STACK)),
            ],
            compiler_params=params(48),
            cost_estimate=pl.CostEstimate(
                flops=6 * TEAM * slots * model_width * gate_weight.shape[2],
                bytes_accessed=6 * model_width * gate_weight.shape[2],
                transcendentals=0,
            ),
            name="experts",
        )(spread, spread_back, *blocks, gate_weight, up_weight, down_weight)

    far = {}
    for d in range(1, teams):
        got = swap_core(packed[teams + d])
        mine = packed[d] + got
        far[d] = [to_team(mine[c], d) for c in range(CHUNKS)]
    got = swap_core(packed[teams])
    mine = packed[0] + got
    own = [mine[c] for c in range(CHUNKS)]
    own_y = [swap_y(v) for v in own]
    own_z = [swap_z(v) for v in own]
    own_d = [swap_z(own_y[0]), swap_y(own_z[1])]
    own_parts = experts([v[c] for c in range(CHUNKS) for v in (own, own_y, own_z, own_d)])

    far_parts = {}
    for d in range(1, teams):
        blocks = []
        for c in range(CHUNKS):
            x = far[d][c]
            x_z = swap_z(x)
            x_y = swap_y(x)
            x_d = swap_y(x_z)
            blocks += [x, x_y, x_z, x_d]
        far_parts[d] = experts(blocks)

    sums = {}
    for d in range(1, teams):
        for c in range(CHUNKS):
            x, x_y, x_z, x_d = far_parts[d][c * TEAM : (c + 1) * TEAM]
            x_z = total(x_z, swap_y(x_d))
            x = total(x, swap_y(x_y), swap_z(x_z))
            sums[d, c] = to_team(x, teams - d)
    (a, a_y, a_z, a_d), (b, b_y, b_z, b_d) = own_parts[:TEAM], own_parts[TEAM:]
    a_y = total(a_y, swap_z(a_d))
    b_z = total(b_z, swap_y(b_d))
    sums[0, 0] = total(a, swap_y(a_y), swap_z(a_z))
    sums[0, 1] = total(b, swap_y(b_y), swap_z(b_z))
    theirs = {key: swap_core(v) for key, v in sums.items()}
    returned = [
        part[d, c] for c in range(CHUNKS) for part in (sums, theirs) for d in range(teams)
    ]
    return pl.pallas_call(
        final_kernel,
        out_shape=jax.ShapeDtypeStruct(tokens.shape, jnp.bfloat16),
        in_specs=[VMEM] * (2 + len(returned)),
        out_specs=VMEM,
        compiler_params=params(40),
        name="combine",
    )(pick_back, weight, *returned)


def solution(mesh):
    in_specs = (
        P(("rep", "node", "local"), None),
        P(("rep", "node", "local"), None),
        P(("rep", "node", "local"), None),
        P(("node", "local"), None, None),
        P(("node", "local"), None, None),
        P(("node", "local"), None, None),
    )
    out_specs = P(("rep", "node", "local"), None)
    return jax.shard_map(local, mesh=mesh, in_specs=in_specs, out_specs=out_specs, check_vma=False)
```

time: 166 us -> 150 us (0.904)
  waiting for transfers between devices: 109 us -> 80 us
  Pallas kernels: 0 us -> 24.2 us
  matrix products: 20.3 us -> 0 us
  starting transfers between devices: 25.7 us -> 35.7 us
    ppermute x18 -> x34, waiting for transfers between devices: 109 us -> 80 us  [the longest x10 40 us: swap_z(): return lax.ppermute(value, 'local', flip_z)]
    pallas_call x0 -> x4, Pallas kernels: none -> 24.2 us  [the longest x2 20.5 us: experts(): pl.pallas_call(expert_kernel, out_shape=[block] * (CHUNKS * TEAM), in_spe...]
    dot_general x4 -> x0, matrix products: 20.3 us -> none  [the longest x1 13.7 us: local(): jnp.dot(hidden, down_weight[0], preferred_element_type=jnp.float32)]
    ppermute x18 -> x34, starting transfers between devices: 25.7 us -> 35.7 us  [the longest x14 20.3 us: swap_y(): return lax.ppermute(value, 'local', flip_y)]
    slice x7 -> x2, local copies, waits for them, and re-layouts: 3.04 us -> 0.18 us  [the longest x1 1.44 us: local(): back_z = swap(own_d[:, :half], 'local', flip_z)]
  transfers between devices with their start and end apart: 18 -> 34, of which waited for: 16 -> 18; matrix products, arithmetic and copies ran while one was open for 1% -> 2% of each run, Pallas kernels for 0% -> 14%
where the time goes in v2:
time: 150 us
  waiting for transfers between devices  80 us (53%)
  starting transfers between devices  35.7 us (24%)
  Pallas kernels  24.2 us (16%)
  local copies, waits for them, and re-layouts  5.84 us (4%)
  other arithmetic  3.59 us (2%)
    ppermute x10, waiting for transfers between devices, swap_z(): return lax.ppermute(value, 'local', flip_z)  40 us
    ppermute x14, waiting for transfers between devices, swap_y(): return lax.ppermute(value, 'local', flip_y)  26.8 us
    pallas_call x2, Pallas kernels, experts(): pl.pallas_call(expert_kernel, out_shape=[block] * (CHUNKS * TEAM), in_spe...  20.5 us
    ppermute x14, starting transfers between devices, swap_y(): return lax.ppermute(value, 'local', flip_y)  20.3 us
    ppermute x4, waiting for transfers between devices, to_team(): return lax.ppermute(value, 'local', pairs)  10.4 us
    ppermute x4, starting transfers between devices, to_team(): return lax.ppermute(value, 'local', pairs)  7.56 us
    ppermute x10, starting transfers between devices, swap_z(): return lax.ppermute(value, 'local', flip_z)  7.1 us
    unnamed x9, local copies, waits for them, and re-layouts  3.01 us
  transfers between devices with their start and end apart: 34, of which 18 were waited for; matrix products, arithmetic and copies ran while one was open for 2% of the time, Pallas kernels for 14%

profile of v2, /device:TPU:0, one launch (start us, length us, event | category | flops | bytes accessed | tf_op | source)
XLA Modules:
  0.0 149.7 jit_solution(12605687006553199965)
XLA Ops:
  0.1 0.8 compare_reduce_fusion
  1.3 1.2 reduce-window.6
  2.9 0.2 and.170
  3.4 0.2 eq.132
  3.6 0.2 eq.133
  4.2 1.6 %copy-done = bf16[144,7168]{1,0:T(8,128)(2,1)S(1)} copy-done((bf16[144,7168]{1,0:T(8,128)(2,1)S(1)}, bf16[144,7168]{1,0:T(8,128)(2,1)}, u32[]{:S(2)}) %copy-start) | copy-done | bytes 2064408
  5.8 1.2 pack.1
  7.0 0.5 collective-permute-start
  7.7 1.4 collective-permute-done
  9.2 3.0 %collective-permute-start.5 = (bf16[72,1792]{1,0:T(8,128)(2,1)S(1)}, bf16[72,1792]{1,0:T(8,128)(2,1)S(1)}, u32[]{:S(2)}, u32[]{:S(2)}) collective-permute-start(bf16[72,1792]{1,0:T(8,128)(2,1)S(1)} %get-tuple-element.49.refs_4_), channel_id=1, source_target_pairs={{0,2},{1,3},{2,0},{3,1},{4,6},{5,7},{6,4},{7,5},{8,10},{9,11},{10,... | collective-permute-start | bytes 774152 | tf_op jit(solution)/shard_map/ppermute | solution.py:168
  12.2 1.5 %collective-permute-start.1 = (bf16[72,1792]{1,0:T(8,128)(2,1)S(1)}, bf16[72,1792]{1,0:T(8,128)(2,1)S(1)}, u32[]{:S(2)}, u32[]{:S(2)}) collective-permute-start(bf16[72,1792]{1,0:T(8,128)(2,1)S(1)} %get-tuple-element.50.refs_0_), channel_id=1, source_target_pairs={{0,1},{1,0},{2,3},{3,2},{4,5},{5,4},{6,7},{7,6},{8,9},{9,8},{10,11... | collective-permute-start | bytes 774152 | tf_op jit(solution)/shard_map/ppermute | solution.py:165
  14.1 0.6 collective-permute-start.4
  14.8 4.4 %collective-permute-done.5.refs_6_ = bf16[72,1792]{1,0:T(8,128)(2,1)S(1)} collective-permute-done((bf16[72,1792]{1,0:T(8,128)(2,1)S(1)}, bf16[72,1792]{1,0:T(8,128)(2,1)S(1)}, u32[]{:S(2)}, u32[]{:S(2)}) %collective-permute-start.5) | collective-permute-done | bytes 258080 | tf_op jit(solution)/shard_map/ppermute | solution.py:168
  19.2 2.0 %collective-permute-start.6 = (bf16[72,1792]{1,0:T(8,128)(2,1)S(1)}, bf16[72,1792]{1,0:T(8,128)(2,1)S(1)}, u32[]{:S(2)}, u32[]{:S(2)}) collective-permute-start(bf16[72,1792]{1,0:T(8,128)(2,1)S(1)} %collective-permute-done.5.refs_6_), channel_id=1, source_target_pairs={{0,1},{1,0},{2,3},{3,2},{4,5},{5,4},{6,7},{7,6},{8,9},{9,8},{10,11... | collective-permute-start | bytes 774152 | tf_op jit(solution)/shard_map/ppermute | solution.py:165
  21.4 1.5 collective-permute-start.3
  22.8 0.8 slice_bitcast_fusion
  23.7 2.6 %collective-permute-start.15 = (bf16[72,1792]{1,0:T(8,128)(2,1)}, bf16[72,1792]{1,0:T(8,128)(2,1)S(1)}, u32[]{:S(2)}, u32[]{:S(2)}) collective-permute-start(bf16[72,1792]{1,0:T(8,128)(2,1)} %get-tuple-element.47), channel_id=1, source_target_pairs={{0,4},{1,5},{2,6},{3,7},{4,0},{5,1},{6,2},{7,3},{8,12},{9,13},{10,... | collective-permute-start | bytes 774152 | tf_op jit(solution)/shard_map/ppermute | solution.py:172
  26.3 0.6 collective-permute-done.4.refs_5_
  26.9 2.6 %collective-permute-start.11 = (bf16[72,1792]{1,0:T(8,128)(2,1)}, bf16[72,1792]{1,0:T(8,128)(2,1)S(1)}, u32[]{:S(2)}, u32[]{:S(2)}) collective-permute-start(bf16[72,1792]{1,0:T(8,128)(2,1)} %get-tuple-element.48), channel_id=1, source_target_pairs={{0,4},{1,5},{2,6},{3,7},{4,0},{5,1},{6,2},{7,3},{8,12},{9,13},{10,... | collective-permute-start | bytes 774152 | tf_op jit(solution)/shard_map/ppermute | solution.py:172
  29.5 1.8 %collective-permute-done.6.refs_7_ = bf16[72,1792]{1,0:T(8,128)(2,1)S(1)} collective-permute-done((bf16[72,1792]{1,0:T(8,128)(2,1)S(1)}, bf16[72,1792]{1,0:T(8,128)(2,1)S(1)}, u32[]{:S(2)}, u32[]{:S(2)}) %collective-permute-start.6) | collective-permute-done | bytes 258080 | tf_op jit(solution)/shard_map/ppermute | solution.py:165
  31.3 5.1 %collective-permute-done.3.refs_3_ = bf16[72,1792]{1,0:T(8,128)(2,1)S(1)} collective-permute-done((bf16[72,1792]{1,0:T(8,128)(2,1)S(1)}, bf16[72,1792]{1,0:T(8,128)(2,1)S(1)}, u32[]{:S(2)}, u32[]{:S(2)}) %collective-permute-start.3) | collective-permute-done | bytes 258080 | tf_op jit(solution)/shard_map/ppermute | solution.py:168
  36.4 10.1 %experts.2 = (bf16[72,1792]{1,0:T(8,128)(2,1)S(1)}, bf16[72,1792]{1,0:T(8,128)(2,1)S(1)}, bf16[72,1792]{1,0:T(8,128)(2,1)S(1)}, bf16[72,1792]{1,0:T(8,128)(2,1)}...) custom-call(bf16[2,144,288]{2,1,0:T(8,128)(2,1)S(1)} %add_convert_fu, ...), custom_call_target="tpu_custom_call" | custom-call | flops 3170893824 | bytes 22020096 | tf_op jit(solution)/shard_map/experts/pallas_call | solution.py:186
  46.5 0.7 copy-done.1
  47.2 0.7 copy-done.2
  48.0 2.1 %collective-permute-start.17 = (bf16[72,1792]{1,0:T(8,128)(2,1)S(1)}, bf16[72,1792]{1,0:T(8,128)(2,1)S(1)}, u32[]{:S(2)}, u32[]{:S(2)}) collective-permute-start(bf16[72,1792]{1,0:T(8,128)(2,1)S(1)} %collective-permute-done.15.refs_4_), channel_id=1, source_target_pairs={{0,2},{1,3},{2,0},{3,1},{4,6},{5,7},{6,4},{7,5},{8,10},{9,11},{10,... | collective-permute-start | bytes 774152 | tf_op jit(solution)/shard_map/ppermute | solution.py:168
  50.1 2.7 %collective-permute-start.16 = (bf16[72,1792]{1,0:T(8,128)(2,1)S(1)}, bf16[72,1792]{1,0:T(8,128)(2,1)S(1)}, u32[]{:S(2)}, u32[]{:S(2)}) collective-permute-start(bf16[72,1792]{1,0:T(8,128)(2,1)S(1)} %collective-permute-done.15.refs_4_), channel_id=1, source_target_pairs={{0,1},{1,0},{2,3},{3,2},{4,5},{5,4},{6,7},{7,6},{8,9},{9,8},{10,11... | collective-permute-start | bytes 774152 | tf_op jit(solution)/shard_map/ppermute | solution.py:165
  52.9 4.4 %collective-permute-done.7 = bf16[72,1792]{1,0:T(8,128)(2,1)S(1)} collective-permute-done((bf16[72,1792]{1,0:T(8,128)(2,1)}, bf16[72,1792]{1,0:T(8,128)(2,1)S(1)}, u32[]{:S(2)}, u32[]{:S(2)}) %collective-permute-start.7) | collective-permute-done | bytes 258080 | tf_op jit(solution)/shard_map/ppermute | solution.py:168
  57.3 2.7 %collective-permute-start.26 = (bf16[72,1792]{1,0:T(8,128)(2,1)}, bf16[72,1792]{1,0:T(8,128)(2,1)S(1)}, u32[]{:S(2)}, u32[]{:S(2)}) collective-permute-start(bf16[72,1792]{1,0:T(8,128)(2,1)} %copy-done.2), channel_id=1, source_target_pairs={{0,1},{1,0},{2,3},{3,2},{4,5},{5,4},{6,7},{7,6},{8,9},{9,8},{10,11... | collective-permute-start | bytes 774152 | tf_op jit(solution)/shard_map/ppermute | solution.py:165
  60.1 2.8 %collective-permute-done.17.refs_6_ = bf16[72,1792]{1,0:T(8,128)(2,1)S(1)} collective-permute-done((bf16[72,1792]{1,0:T(8,128)(2,1)S(1)}, bf16[72,1792]{1,0:T(8,128)(2,1)S(1)}, u32[]{:S(2)}, u32[]{:S(2)}) %collective-permute-start.17) | collective-permute-done | bytes 258080 | tf_op jit(solution)/shard_map/ppermute | solution.py:168
  62.8 5.5 %collective-permute-done.13.refs_2_ = bf16[72,1792]{1,0:T(8,128)(2,1)S(1)} collective-permute-done((bf16[72,1792]{1,0:T(8,128)(2,1)S(1)}, bf16[72,1792]{1,0:T(8,128)(2,1)S(1)}, u32[]{:S(2)}, u32[]{:S(2)}) %collective-permute-start.13) | collective-permute-done | bytes 258080 | tf_op jit(solution)/shard_map/ppermute | solution.py:168
  68.4 2.7 %collective-permute-start.18 = (bf16[72,1792]{1,0:T(8,128)(2,1)S(1)}, bf16[72,1792]{1,0:T(8,128)(2,1)S(1)}, u32[]{:S(2)}, u32[]{:S(2)}) collective-permute-start(bf16[72,1792]{1,0:T(8,128)(2,1)S(1)} %collective-permute-done.17.refs_6_), channel_id=1, source_target_pairs={{0,1},{1,0},{2,3},{3,2},{4,5},{5,4},{6,7},{7,6},{8,9},{9,8},{10,11... | collective-permute-start | bytes 774152 | tf_op jit(solution)/shard_map/ppermute | solution.py:165
  71.2 2.1 %collective-permute-start.25 = (bf16[72,1792]{1,0:T(8,128)(2,1)S(1)}, bf16[72,1792]{1,0:T(8,128)(2,1)S(1)}, u32[]{:S(2)}, u32[]{:S(2)}) collective-permute-start(bf16[72,1792]{1,0:T(8,128)(2,1)S(1)} %get-tuple-element.38), channel_id=1, source_target_pairs={{0,1},{1,0},{2,3},{3,2},{4,5},{5,4},{6,7},{7,6},{8,9},{9,8},{10,11... | collective-permute-start | bytes 774152 | tf_op jit(solution)/shard_map/ppermute | solution.py:165
  73.3 4.9 %collective-permute-done.18.refs_7_ = bf16[72,1792]{1,0:T(8,128)(2,1)S(1)} collective-permute-done((bf16[72,1792]{1,0:T(8,128)(2,1)S(1)}, bf16[72,1792]{1,0:T(8,128)(2,1)S(1)}, u32[]{:S(2)}, u32[]{:S(2)}) %collective-permute-start.18) | collective-permute-done | bytes 258080 | tf_op jit(solution)/shard_map/ppermute | solution.py:165
  78.2 5.5 %collective-permute-done.14.refs_3_ = bf16[72,1792]{1,0:T(8,128)(2,1)S(1)} collective-permute-done((bf16[72,1792]{1,0:T(8,128)(2,1)S(1)}, bf16[72,1792]{1,0:T(8,128)(2,1)S(1)}, u32[]{:S(2)}, u32[]{:S(2)}) %collective-permute-start.14) | collective-permute-done | bytes 258080 | tf_op jit(solution)/shard_map/ppermute | solution.py:165
  83.7 10.3 %experts.3 = (bf16[72,1792]{1,0:T(8,128)(2,1)S(1)}, bf16[72,1792]{1,0:T(8,128)(2,1)S(1)}, bf16[72,1792]{1,0:T(8,128)(2,1)S(1)}, bf16[72,1792]{1,0:T(8,128)(2,1)S...) custom-call(bf16[2,144,288]{2,1,0:T(8,128)(2,1)S(1)} %add_convert_fu, ...), custom_call_target="tpu_custom_call" | custom-call | flops 3170893824 | bytes 22020096 | tf_op jit(solution)/shard_map/experts/pallas_call | solution.py:186
  94.1 2.1 %collective-permute-start.19 = (bf16[72,1792]{1,0:T(8,128)(2,1)S(1)}, bf16[72,1792]{1,0:T(8,128)(2,1)S(1)}, u32[]{:S(2)}, u32[]{:S(2)}) collective-permute-start(bf16[72,1792]{1,0:T(8,128)(2,1)S(1)} %get-tuple-element.34), channel_id=1, source_target_pairs={{0,1},{1,0},{2,3},{3,2},{4,5},{5,4},{6,7},{7,6},{8,9},{9,8},{10,11... | collective-permute-start | bytes 774152 | tf_op jit(solution)/shard_map/ppermute | solution.py:165
  96.3 1.9 %collective-permute-start.28 = (bf16[72,1792]{1,0:T(8,128)(2,1)S(1)}, bf16[72,1792]{1,0:T(8,128)(2,1)S(1)}, u32[]{:S(2)}, u32[]{:S(2)}) collective-permute-start(bf16[72,1792]{1,0:T(8,128)(2,1)S(1)} %get-tuple-element.42), channel_id=1, source_target_pairs={{0,1},{1,0},{2,3},{3,2},{4,5},{5,4},{6,7},{7,6},{8,9},{9,8},{10,11... | collective-permute-start | bytes 774152 | tf_op jit(solution)/shard_map/ppermute | solution.py:165
  98.3 9.4 %collective-permute-done.20 = bf16[72,1792]{1,0:T(8,128)(2,1)S(1)} collective-permute-done((bf16[72,1792]{1,0:T(8,128)(2,1)S(1)}, bf16[72,1792]{1,0:T(8,128)(2,1)S(1)}, u32[]{:S(2)}, u32[]{:S(2)}) %collective-permute-start.20) | collective-permute-done | bytes 258080 | tf_op jit(solution)/shard_map/ppermute | solution.py:165
  107.7 1.7 %collective-permute-start.29 = (bf16[72,1792]{1,0:T(8,128)(2,1)S(1)}, bf16[72,1792]{1,0:T(8,128)(2,1)S(1)}, u32[]{:S(2)}, u32[]{:S(2)}) collective-permute-start(bf16[72,1792]{1,0:T(8,128)(2,1)S(1)} %get-tuple-element.44), channel_id=1, source_target_pairs={{0,1},{1,0},{2,3},{3,2},{4,5},{5,4},{6,7},{7,6},{8,9},{9,8},{10,11... | collective-permute-start | bytes 774152 | tf_op jit(solution)/shard_map/ppermute | solution.py:165
  109.5 4.5 %collective-permute-done.29 = bf16[72,1792]{1,0:T(8,128)(2,1)S(1)} collective-permute-done((bf16[72,1792]{1,0:T(8,128)(2,1)S(1)}, bf16[72,1792]{1,0:T(8,128)(2,1)S(1)}, u32[]{:S(2)}, u32[]{:S(2)}) %collective-permute-start.29) | collective-permute-done | bytes 258080 | tf_op jit(solution)/shard_map/ppermute | solution.py:165
  114.0 0.4 collective-permute-start.21
  114.5 11.3 %collective-permute-done.21 = bf16[72,1792]{1,0:T(8,128)(2,1)S(1)} collective-permute-done((bf16[72,1792]{1,0:T(8,128)(2,1)S(1)}, bf16[72,1792]{1,0:T(8,128)(2,1)S(1)}, u32[]{:S(2)}, u32[]{:S(2)}) %collective-permute-start.21) | collective-permute-done | bytes 258080 | tf_op jit(solution)/shard_map/ppermute | solution.py:168
  125.9 2.2 %collective-permute-start.22 = (bf16[72,1792]{1,0:T(8,128)(2,1)S(1)}, bf16[72,1792]{1,0:T(8,128)(2,1)S(1)}, u32[]{:S(2)}, u32[]{:S(2)}) collective-permute-start(bf16[72,1792]{1,0:T(8,128)(2,1)S(1)} %add_convert_fusion.4), channel_id=1, source_target_pairs={{0,4},{1,5},{2,6},{3,7},{4,0},{5,1},{6,2},{7,3},{8,12},{9,13},{10,... | collective-permute-start | bytes 774152 | tf_op jit(solution)/shard_map/ppermute | solution.py:172
  128.1 6.5 %collective-permute-done.30 = bf16[72,1792]{1,0:T(8,128)(2,1)S(1)} collective-permute-done((bf16[72,1792]{1,0:T(8,128)(2,1)S(1)}, bf16[72,1792]{1,0:T(8,128)(2,1)S(1)}, u32[]{:S(2)}, u32[]{:S(2)}) %collective-permute-start.30) | collective-permute-done | bytes 258080 | tf_op jit(solution)/shard_map/ppermute | solution.py:168
  135.1 7.7 %collective-permute-done.22.refs_1_ = bf16[72,1792]{1,0:T(8,128)(2,1)S(1)} collective-permute-done((bf16[72,1792]{1,0:T(8,128)(2,1)S(1)}, bf16[72,1792]{1,0:T(8,128)(2,1)S(1)}, u32[]{:S(2)}, u32[]{:S(2)}) %collective-permute-start.22) | collective-permute-done | bytes 258080 | tf_op jit(solution)/shard_map/ppermute | solution.py:172
  142.8 2.8 %collective-permute-done.31.refs_5_ = bf16[72,1792]{1,0:T(8,128)(2,1)S(1)} collective-permute-done((bf16[72,1792]{1,0:T(8,128)(2,1)S(1)}, bf16[72,1792]{1,0:T(8,128)(2,1)S(1)}, u32[]{:S(2)}, u32[]{:S(2)}) %collective-permute-start.31) | collective-permute-done | bytes 258080 | tf_op jit(solution)/shard_map/ppermute | solution.py:172
  145.8 1.3 collective-permute-done.33.refs_7_
  147.1 2.6 %combine.1 = bf16[144,7168]{1,0:T(8,128)(2,1)} custom-call(bf16[2,144,288]{2,1,0:T(8,128)(2,1)S(1)} %and_convert_fusion.1.pick_ref, f32[144,1]{1,0:T(8,128)S(1)} %copy.38.weight_ref, bf16[72,1792]{1,0:T(8,128)(2,1)S(1)} %add_convert_fusion.6.refs_0_, bf16[72,1792]{1,0:T(8,128)(2,1)S(1)} %collective-permute-done.22.refs_1_, ...), custom_call_target="tpu_custom_call" | custom-call | tf_op jit(solution)/shard_map/combine/pallas_call | solution.py:246
  (82 shorter events, 4.0 us)
Async XLA Ops:
  4.2 1.6 %copy-start = (bf16[144,7168]{1,0:T(8,128)(2,1)S(1)}, bf16[144,7168]{1,0:T(8,128)(2,1)}, u32[]{:S(2)}) copy-start(bf16[144,7168]{1,0:T(8,128)(2,1)} %tokens_ref.1) | copy-start | bytes 6193156
  7.0 2.0 %collective-permute-start = (bf16[2,72,1792]{2,1,0:T(8,128)(2,1)S(1)}, bf16[2,72,1792]{2,1,0:T(8,128)(2,1)S(1)}, u32[]{:S(2)}, u32[]{:S(2)}) collective-permute-start(bf16[2,72,1792]{2,1,0:T(8,128)(2,1)S(1)} %get-tuple-element.26), channel_id=1, source_target_pairs={{0,8},{8,0},{1,9},{9,1},{2,10},{10,2},{3,11},{11,3},{4,12},{12,4},... | collective-permute-start | bytes 1548296 | tf_op jit(solution)/shard_map/ppermute | solution.py:162
  7.6 7.2 %collective-permute-start.10 = (bf16[2,72,1792]{2,1,0:T(8,128)(2,1)S(1)}, bf16[2,72,1792]{2,1,0:T(8,128)(2,1)S(1)}, u32[]{:S(2)}, u32[]{:S(2)}) collective-permute-start(bf16[2,72,1792]{2,1,0:T(8,128)(2,1)S(1)} %get-tuple-element.32), channel_id=1, source_target_pairs={{0,8},{8,0},{1,9},{9,1},{2,10},{10,2},{3,11},{11,3},{4,12},{12,4},... | collective-permute-start | bytes 1548296 | tf_op jit(solution)/shard_map/ppermute | solution.py:162
  9.2 10.0 %collective-permute-start.5 = (bf16[72,1792]{1,0:T(8,128)(2,1)S(1)}, bf16[72,1792]{1,0:T(8,128)(2,1)S(1)}, u32[]{:S(2)}, u32[]{:S(2)}) collective-permute-start(bf16[72,1792]{1,0:T(8,128)(2,1)S(1)} %get-tuple-element.49.refs_4_), channel_id=1, source_target_pairs={{0,2},{1,3},{2,0},{3,1},{4,6},{5,7},{6,4},{7,5},{8,10},{9,11},{10,... | collective-permute-start | bytes 774152 | tf_op jit(solution)/shard_map/ppermute | solution.py:168
  12.2 9.1 %collective-permute-start.1 = (bf16[72,1792]{1,0:T(8,128)(2,1)S(1)}, bf16[72,1792]{1,0:T(8,128)(2,1)S(1)}, u32[]{:S(2)}, u32[]{:S(2)}) collective-permute-start(bf16[72,1792]{1,0:T(8,128)(2,1)S(1)} %get-tuple-element.50.refs_0_), channel_id=1, source_target_pairs={{0,1},{1,0},{2,3},{3,2},{4,5},{5,4},{6,7},{7,6},{8,9},{9,8},{10,11... | collective-permute-start | bytes 774152 | tf_op jit(solution)/shard_map/ppermute | solution.py:165
  14.1 12.8 %collective-permute-start.4 = (bf16[72,1792]{1,0:T(8,128)(2,1)S(1)}, bf16[72,1792]{1,0:T(8,128)(2,1)S(1)}, u32[]{:S(2)}, u32[]{:S(2)}) collective-permute-start(bf16[72,1792]{1,0:T(8,128)(2,1)S(1)} %get-tuple-element.49.refs_4_), channel_id=1, source_target_pairs={{0,1},{1,0},{2,3},{3,2},{4,5},{5,4},{6,7},{7,6},{8,9},{9,8},{10,11... | collective-permute-start | bytes 774152 | tf_op jit(solution)/shard_map/ppermute | solution.py:165
  14.6 14.8 %collective-permute-start.2 = (bf16[72,1792]{1,0:T(8,128)(2,1)S(1)}, bf16[72,1792]{1,0:T(8,128)(2,1)S(1)}, u32[]{:S(2)}, u32[]{:S(2)}) collective-permute-start(bf16[72,1792]{1,0:T(8,128)(2,1)S(1)} %get-tuple-element.50.refs_0_), channel_id=1, source_target_pairs={{0,2},{1,3},{2,0},{3,1},{4,6},{5,7},{6,4},{7,5},{8,10},{9,11},{10,... | collective-permute-start | bytes 774152 | tf_op jit(solution)/shard_map/ppermute | solution.py:168
  19.2 12.0 %collective-permute-start.6 = (bf16[72,1792]{1,0:T(8,128)(2,1)S(1)}, bf16[72,1792]{1,0:T(8,128)(2,1)S(1)}, u32[]{:S(2)}, u32[]{:S(2)}) collective-permute-start(bf16[72,1792]{1,0:T(8,128)(2,1)S(1)} %collective-permute-done.5.refs_6_), channel_id=1, source_target_pairs={{0,1},{1,0},{2,3},{3,2},{4,5},{5,4},{6,7},{7,6},{8,9},{9,8},{10,11... | collective-permute-start | bytes 774152 | tf_op jit(solution)/shard_map/ppermute | solution.py:165
  21.4 15.0 %collective-permute-start.3 = (bf16[72,1792]{1,0:T(8,128)(2,1)S(1)}, bf16[72,1792]{1,0:T(8,128)(2,1)S(1)}, u32[]{:S(2)}, u32[]{:S(2)}) collective-permute-start(bf16[72,1792]{1,0:T(8,128)(2,1)S(1)} %collective-permute-done.1.refs_1_), channel_id=1, source_target_pairs={{0,2},{1,3},{2,0},{3,1},{4,6},{5,7},{6,4},{7,5},{8,10},{9,11},{10,... | collective-permute-start | bytes 774152 | tf_op jit(solution)/shard_map/ppermute | solution.py:168
  23.7 24.3 %collective-permute-start.15 = (bf16[72,1792]{1,0:T(8,128)(2,1)}, bf16[72,1792]{1,0:T(8,128)(2,1)S(1)}, u32[]{:S(2)}, u32[]{:S(2)}) collective-permute-start(bf16[72,1792]{1,0:T(8,128)(2,1)} %get-tuple-element.47), channel_id=1, source_target_pairs={{0,4},{1,5},{2,6},{3,7},{4,0},{5,1},{6,2},{7,3},{8,12},{9,13},{10,... | collective-permute-start | bytes 774152 | tf_op jit(solution)/shard_map/ppermute | solution.py:172
  26.9 25.9 %collective-permute-start.11 = (bf16[72,1792]{1,0:T(8,128)(2,1)}, bf16[72,1792]{1,0:T(8,128)(2,1)S(1)}, u32[]{:S(2)}, u32[]{:S(2)}) collective-permute-start(bf16[72,1792]{1,0:T(8,128)(2,1)} %get-tuple-element.48), channel_id=1, source_target_pairs={{0,4},{1,5},{2,6},{3,7},{4,0},{5,1},{6,2},{7,3},{8,12},{9,13},{10,... | collective-permute-start | bytes 774152 | tf_op jit(solution)/shard_map/ppermute | solution.py:172
  36.4 11.6 %copy-start.3 = (f32[144,8]{0,1:T(8,128)S(1)}, f32[144,8]{0,1:T(8,128)}, u32[]{:S(2)}) copy-start(f32[144,8]{0,1:T(8,128)} %param.8) | copy-start | bytes 13828
  46.5 0.7 copy-start.1
  47.2 0.7 copy-start.2
  47.9 9.4 %collective-permute-start.7 = (bf16[72,1792]{1,0:T(8,128)(2,1)}, bf16[72,1792]{1,0:T(8,128)(2,1)S(1)}, u32[]{:S(2)}, u32[]{:S(2)}) collective-permute-start(bf16[72,1792]{1,0:T(8,128)(2,1)} %get-tuple-element.29), channel_id=1, source_target_pairs={{0,2},{1,3},{2,0},{3,1},{4,6},{5,7},{6,4},{7,5},{8,10},{9,11},{10,... | collective-permute-start | bytes 774152 | tf_op jit(solution)/shard_map/ppermute | solution.py:168
  48.0 14.9 %collective-permute-start.17 = (bf16[72,1792]{1,0:T(8,128)(2,1)S(1)}, bf16[72,1792]{1,0:T(8,128)(2,1)S(1)}, u32[]{:S(2)}, u32[]{:S(2)}) collective-permute-start(bf16[72,1792]{1,0:T(8,128)(2,1)S(1)} %collective-permute-done.15.refs_4_), channel_id=1, source_target_pairs={{0,2},{1,3},{2,0},{3,1},{4,6},{5,7},{6,4},{7,5},{8,10},{9,11},{10,... | collective-permute-start | bytes 774152 | tf_op jit(solution)/shard_map/ppermute | solution.py:168
  50.1 21.1 %collective-permute-start.16 = (bf16[72,1792]{1,0:T(8,128)(2,1)S(1)}, bf16[72,1792]{1,0:T(8,128)(2,1)S(1)}, u32[]{:S(2)}, u32[]{:S(2)}) collective-permute-start(bf16[72,1792]{1,0:T(8,128)(2,1)S(1)} %collective-permute-done.15.refs_4_), channel_id=1, source_target_pairs={{0,1},{1,0},{2,3},{3,2},{4,5},{5,4},{6,7},{7,6},{8,9},{9,8},{10,11... | collective-permute-start | bytes 774152 | tf_op jit(solution)/shard_map/ppermute | solution.py:165
  52.8 15.6 %collective-permute-start.13 = (bf16[72,1792]{1,0:T(8,128)(2,1)S(1)}, bf16[72,1792]{1,0:T(8,128)(2,1)S(1)}, u32[]{:S(2)}, u32[]{:S(2)}) collective-permute-start(bf16[72,1792]{1,0:T(8,128)(2,1)S(1)} %collective-permute-done.11.refs_0_), channel_id=1, source_target_pairs={{0,2},{1,3},{2,0},{3,1},{4,6},{5,7},{6,4},{7,5},{8,10},{9,11},{10,... | collective-permute-start | bytes 774152 | tf_op jit(solution)/shard_map/ppermute | solution.py:168
  52.8 20.4 %collective-permute-start.12 = (bf16[72,1792]{1,0:T(8,128)(2,1)S(1)}, bf16[72,1792]{1,0:T(8,128)(2,1)S(1)}, u32[]{:S(2)}, u32[]{:S(2)}) collective-permute-start(bf16[72,1792]{1,0:T(8,128)(2,1)S(1)} %collective-permute-done.11.refs_0_), channel_id=1, source_target_pairs={{0,1},{1,0},{2,3},{3,2},{4,5},{5,4},{6,7},{7,6},{8,9},{9,8},{10,11... | collective-permute-start | bytes 774152 | tf_op jit(solution)/shard_map/ppermute | solution.py:165
  57.3 13.8 %collective-permute-start.26 = (bf16[72,1792]{1,0:T(8,128)(2,1)}, bf16[72,1792]{1,0:T(8,128)(2,1)S(1)}, u32[]{:S(2)}, u32[]{:S(2)}) collective-permute-start(bf16[72,1792]{1,0:T(8,128)(2,1)} %copy-done.2), channel_id=1, source_target_pairs={{0,1},{1,0},{2,3},{3,2},{4,5},{5,4},{6,7},{7,6},{8,9},{9,8},{10,11... | collective-permute-start | bytes 774152 | tf_op jit(solution)/shard_map/ppermute | solution.py:165
  62.8 33.3 %collective-permute-start.9 = (bf16[72,1792]{1,0:T(8,128)(2,1)}, bf16[72,1792]{1,0:T(8,128)(2,1)S(1)}, u32[]{:S(2)}, u32[]{:S(2)}) collective-permute-start(bf16[72,1792]{1,0:T(8,128)(2,1)} %copy-done.1), channel_id=1, source_target_pairs={{0,2},{1,3},{2,0},{3,1},{4,6},{5,7},{6,4},{7,5},{8,10},{9,11},{10,... | collective-permute-start | bytes 774152 | tf_op jit(solution)/shard_map/ppermute | solution.py:168
  68.4 9.8 %collective-permute-start.18 = (bf16[72,1792]{1,0:T(8,128)(2,1)S(1)}, bf16[72,1792]{1,0:T(8,128)(2,1)S(1)}, u32[]{:S(2)}, u32[]{:S(2)}) collective-permute-start(bf16[72,1792]{1,0:T(8,128)(2,1)S(1)} %collective-permute-done.17.refs_6_), channel_id=1, source_target_pairs={{0,1},{1,0},{2,3},{3,2},{4,5},{5,4},{6,7},{7,6},{8,9},{9,8},{10,11... | collective-permute-start | bytes 774152 | tf_op jit(solution)/shard_map/ppermute | solution.py:165
  71.1 12.7 %collective-permute-start.14 = (bf16[72,1792]{1,0:T(8,128)(2,1)S(1)}, bf16[72,1792]{1,0:T(8,128)(2,1)S(1)}, u32[]{:S(2)}, u32[]{:S(2)}) collective-permute-start(bf16[72,1792]{1,0:T(8,128)(2,1)S(1)} %collective-permute-done.13.refs_2_), channel_id=1, source_target_pairs={{0,1},{1,0},{2,3},{3,2},{4,5},{5,4},{6,7},{7,6},{8,9},{9,8},{10,11... | collective-permute-start | bytes 774152 | tf_op jit(solution)/shard_map/ppermute | solution.py:165
  71.2 63.7 %collective-permute-start.25 = (bf16[72,1792]{1,0:T(8,128)(2,1)S(1)}, bf16[72,1792]{1,0:T(8,128)(2,1)S(1)}, u32[]{:S(2)}, u32[]{:S(2)}) collective-permute-start(bf16[72,1792]{1,0:T(8,128)(2,1)S(1)} %get-tuple-element.38), channel_id=1, source_target_pairs={{0,1},{1,0},{2,3},{3,2},{4,5},{5,4},{6,7},{7,6},{8,9},{9,8},{10,11... | collective-permute-start | bytes 774152 | tf_op jit(solution)/shard_map/ppermute | solution.py:165
  73.3 23.0 %collective-permute-start.8 = (bf16[72,1792]{1,0:T(8,128)(2,1)S(1)}, bf16[72,1792]{1,0:T(8,128)(2,1)S(1)}, u32[]{:S(2)}, u32[]{:S(2)}) collective-permute-start(bf16[72,1792]{1,0:T(8,128)(2,1)S(1)} %add_convert_fusion.7), channel_id=1, source_target_pairs={{0,1},{1,0},{2,3},{3,2},{4,5},{5,4},{6,7},{7,6},{8,9},{9,8},{10,11... | collective-permute-start | bytes 774152 | tf_op jit(solution)/shard_map/ppermute | solution.py:165
  78.2 56.7 %collective-permute-start.27 = (bf16[72,1792]{1,0:T(8,128)(2,1)S(1)}, bf16[72,1792]{1,0:T(8,128)(2,1)S(1)}, u32[]{:S(2)}, u32[]{:S(2)}) collective-permute-start(bf16[72,1792]{1,0:T(8,128)(2,1)S(1)} %add_convert_fusion.3), channel_id=1, source_target_pairs={{0,2},{1,3},{2,0},{3,1},{4,6},{5,7},{6,4},{7,5},{8,10},{9,11},{10,... | collective-permute-start | bytes 774152 | tf_op jit(solution)/shard_map/ppermute | solution.py:168
  94.1 20.4 %collective-permute-start.19 = (bf16[72,1792]{1,0:T(8,128)(2,1)S(1)}, bf16[72,1792]{1,0:T(8,128)(2,1)S(1)}, u32[]{:S(2)}, u32[]{:S(2)}) collective-permute-start(bf16[72,1792]{1,0:T(8,128)(2,1)S(1)} %get-tuple-element.34), channel_id=1, source_target_pairs={{0,1},{1,0},{2,3},{3,2},{4,5},{5,4},{6,7},{7,6},{8,9},{9,8},{10,11... | collective-permute-start | bytes 774152 | tf_op jit(solution)/shard_map/ppermute | solution.py:165
  96.2 11.5 %collective-permute-start.20 = (bf16[72,1792]{1,0:T(8,128)(2,1)S(1)}, bf16[72,1792]{1,0:T(8,128)(2,1)S(1)}, u32[]{:S(2)}, u32[]{:S(2)}) collective-permute-start(bf16[72,1792]{1,0:T(8,128)(2,1)S(1)} %get-tuple-element.36), channel_id=1, source_target_pairs={{0,1},{1,0},{2,3},{3,2},{4,5},{5,4},{6,7},{7,6},{8,9},{9,8},{10,11... | collective-permute-start | bytes 774152 | tf_op jit(solution)/shard_map/ppermute | solution.py:165
  96.3 29.6 %collective-permute-start.28 = (bf16[72,1792]{1,0:T(8,128)(2,1)S(1)}, bf16[72,1792]{1,0:T(8,128)(2,1)S(1)}, u32[]{:S(2)}, u32[]{:S(2)}) collective-permute-start(bf16[72,1792]{1,0:T(8,128)(2,1)S(1)} %get-tuple-element.42), channel_id=1, source_target_pairs={{0,1},{1,0},{2,3},{3,2},{4,5},{5,4},{6,7},{7,6},{8,9},{9,8},{10,11... | collective-permute-start | bytes 774152 | tf_op jit(solution)/shard_map/ppermute | solution.py:165
  107.7 6.3 %collective-permute-start.29 = (bf16[72,1792]{1,0:T(8,128)(2,1)S(1)}, bf16[72,1792]{1,0:T(8,128)(2,1)S(1)}, u32[]{:S(2)}, u32[]{:S(2)}) collective-permute-start(bf16[72,1792]{1,0:T(8,128)(2,1)S(1)} %get-tuple-element.44), channel_id=1, source_target_pairs={{0,1},{1,0},{2,3},{3,2},{4,5},{5,4},{6,7},{7,6},{8,9},{9,8},{10,11... | collective-permute-start | bytes 774152 | tf_op jit(solution)/shard_map/ppermute | solution.py:165
  114.0 11.8 %collective-permute-start.21 = (bf16[72,1792]{1,0:T(8,128)(2,1)S(1)}, bf16[72,1792]{1,0:T(8,128)(2,1)S(1)}, u32[]{:S(2)}, u32[]{:S(2)}) collective-permute-start(bf16[72,1792]{1,0:T(8,128)(2,1)S(1)} %add_convert_fusion.5), channel_id=1, source_target_pairs={{0,2},{1,3},{2,0},{3,1},{4,6},{5,7},{6,4},{7,5},{8,10},{9,11},{10,... | collective-permute-start | bytes 774152 | tf_op jit(solution)/shard_map/ppermute | solution.py:168
  114.4 31.3 %collective-permute-start.23 = (bf16[72,1792]{1,0:T(8,128)(2,1)S(1)}, bf16[72,1792]{1,0:T(8,128)(2,1)S(1)}, u32[]{:S(2)}, u32[]{:S(2)}) collective-permute-start(bf16[72,1792]{1,0:T(8,128)(2,1)S(1)} %add_convert_fusion.6.refs_0_), channel_id=1, source_target_pairs={{0,8},{8,0},{1,9},{9,1},{2,10},{10,2},{3,11},{11,3},{4,12},{12,4},... | collective-permute-start | bytes 774152 | tf_op jit(solution)/shard_map/ppermute | solution.py:162
  125.8 8.9 %collective-permute-start.30 = (bf16[72,1792]{1,0:T(8,128)(2,1)S(1)}, bf16[72,1792]{1,0:T(8,128)(2,1)S(1)}, u32[]{:S(2)}, u32[]{:S(2)}) collective-permute-start(bf16[72,1792]{1,0:T(8,128)(2,1)S(1)} %add_convert_fusion.1), channel_id=1, source_target_pairs={{0,2},{1,3},{2,0},{3,1},{4,6},{5,7},{6,4},{7,5},{8,10},{9,11},{10,... | collective-permute-start | bytes 774152 | tf_op jit(solution)/shard_map/ppermute | solution.py:168
  125.9 16.9 %collective-permute-start.22 = (bf16[72,1792]{1,0:T(8,128)(2,1)S(1)}, bf16[72,1792]{1,0:T(8,128)(2,1)S(1)}, u32[]{:S(2)}, u32[]{:S(2)}) collective-permute-start(bf16[72,1792]{1,0:T(8,128)(2,1)S(1)} %add_convert_fusion.4), channel_id=1, source_target_pairs={{0,4},{1,5},{2,6},{3,7},{4,0},{5,1},{6,2},{7,3},{8,12},{9,13},{10,... | collective-permute-start | bytes 774152 | tf_op jit(solution)/shard_map/ppermute | solution.py:172
  134.8 10.8 %collective-permute-start.31 = (bf16[72,1792]{1,0:T(8,128)(2,1)S(1)}, bf16[72,1792]{1,0:T(8,128)(2,1)S(1)}, u32[]{:S(2)}, u32[]{:S(2)}) collective-permute-start(bf16[72,1792]{1,0:T(8,128)(2,1)S(1)} %add_convert_fusion), channel_id=1, source_target_pairs={{0,4},{1,5},{2,6},{3,7},{4,0},{5,1},{6,2},{7,3},{8,12},{9,13},{10,... | collective-permute-start | bytes 774152 | tf_op jit(solution)/shard_map/ppermute | solution.py:172
  135.0 10.7 %collective-permute-start.32 = (bf16[72,1792]{1,0:T(8,128)(2,1)S(1)}, bf16[72,1792]{1,0:T(8,128)(2,1)S(1)}, u32[]{:S(2)}, u32[]{:S(2)}) collective-permute-start(bf16[72,1792]{1,0:T(8,128)(2,1)S(1)} %add_convert_fusion.2.refs_4_), channel_id=1, source_target_pairs={{0,8},{8,0},{1,9},{9,1},{2,10},{10,2},{3,11},{11,3},{4,12},{12,4},... | collective-permute-start | bytes 774152 | tf_op jit(solution)/shard_map/ppermute | solution.py:162
  142.8 3.0 %collective-permute-start.24 = (bf16[72,1792]{1,0:T(8,128)(2,1)S(1)}, bf16[72,1792]{1,0:T(8,128)(2,1)S(1)}, u32[]{:S(2)}, u32[]{:S(2)}) collective-permute-start(bf16[72,1792]{1,0:T(8,128)(2,1)S(1)} %collective-permute-done.22.refs_1_), channel_id=1, source_target_pairs={{0,8},{8,0},{1,9},{9,1},{2,10},{10,2},{3,11},{11,3},{4,12},{12,4},... | collective-permute-start | bytes 774152 | tf_op jit(solution)/shard_map/ppermute | solution.py:162
  145.6 1.5 %collective-permute-start.33 = (bf16[72,1792]{1,0:T(8,128)(2,1)S(1)}, bf16[72,1792]{1,0:T(8,128)(2,1)S(1)}, u32[]{:S(2)}, u32[]{:S(2)}) collective-permute-start(bf16[72,1792]{1,0:T(8,128)(2,1)S(1)} %collective-permute-done.31.refs_5_), channel_id=1, source_target_pairs={{0,8},{8,0},{1,9},{9,1},{2,10},{10,2},{3,11},{11,3},{4,12},{12,4},... | collective-permute-start | bytes 774152 | tf_op jit(solution)/shard_map/ppermute | solution.py:162

commit v3 on v0

v3 whole, which is shorter than its diff:
```python
import jax
import jax.numpy as jnp
from jax import lax
from jax.experimental import pallas as pl
from jax.experimental.pallas import tpu as pltpu
from jax.sharding import PartitionSpec as P

TEAM = 4
CAP = 18
GSIZE = 32
STACK = 4
COST = 60

route_scale = 2.5
VMEM = pl.BlockSpec(memory_space=pltpu.VMEM)
SMEM = pl.BlockSpec(memory_space=pltpu.SMEM)
HBM = pl.BlockSpec(memory_space=pltpu.HBM)


def dot(a, b):
    return jnp.dot(a, b, preferred_element_type=jnp.float32)


def params(mib):
    return pltpu.CompilerParams(vmem_limit_bytes=mib << 20)


def pieces_of(value, q):
    return value[q * CAP : (q + 1) * CAP]


def pack_kernel(flight_ref, ids_ref, scores_ref, tokens_hbm, *refs):
    tokens, sems = refs[-2:]
    outs, pick_ref, weight_ref = refs[:-4], refs[-4], refs[-3]
    experts = len(outs)
    width = outs[0].shape[1]
    copies = [
        pltpu.make_async_copy(
            tokens_hbm.at[:, pl.ds(q * width, width)], tokens.at[q], sems.at[q]
        )
        for q in range(STACK)
    ]
    for copy in copies:
        copy.start()
    ids = ids_ref[...]
    scores = scores_ref[...]
    count = ids.shape[1]
    earlier = lax.broadcasted_iota(jnp.int32, (count, count), 0) < lax.broadcasted_iota(
        jnp.int32, (count, count), 1
    )
    earlier = jnp.where(earlier, 1.0, 0.0).astype(jnp.bfloat16)
    slot = lax.broadcasted_iota(jnp.int32, (CAP, count), 0).astype(jnp.float32)
    hits = [jnp.where(ids == flight_ref[e], 1.0, 0.0) for e in range(experts)]
    rows = jnp.concatenate([jnp.sum(hit, axis=0, keepdims=True) for hit in hits], axis=0)
    ranks = dot(rows.astype(jnp.bfloat16), earlier)
    pick = jnp.concatenate(
        [
            jnp.where(slot == ranks[e : e + 1], rows[e : e + 1], 0.0)
            for e in range(experts)
        ],
        axis=0,
    )
    pick_ref[...] = pick.astype(jnp.bfloat16)
    gate_values = route_scale * scores / jnp.sum(scores, axis=0, keepdims=True)
    weight = jnp.sum(gate_values * sum(hits), axis=0, keepdims=True)
    weight_ref[...] = jnp.sum(pick * weight, axis=1, keepdims=True)
    pick = pick.astype(jnp.bfloat16)
    parts = []
    for q in range(STACK):
        copies[q].wait()
        parts.append(dot(pick, tokens[q]).astype(jnp.bfloat16))
    for e in range(experts):
        outs[e][...] = jnp.concatenate([p[e * CAP : (e + 1) * CAP] for p in parts], axis=0)


def load_kernel(gate_hbm, up_hbm, down_hbm, gate, up, down, sems):
    width = gate.shape[1]
    copies = []
    for q in range(STACK):
        span = pl.ds(q * width, width)
        copies += [
            pltpu.make_async_copy(gate_hbm.at[0, span], gate.at[q], sems.at[0, q]),
            pltpu.make_async_copy(up_hbm.at[0, span], up.at[q], sems.at[1, q]),
            pltpu.make_async_copy(down_hbm.at[0, :, span], down.at[q], sems.at[2, q]),
        ]
    for copy in copies:
        copy.start()
    for copy in copies:
        copy.wait()


def expert_kernel(gate, up, down, *refs):
    count = len(refs) // 2
    blocks, outs = refs[:count], refs[count:]
    values = [block[...] for block in blocks]
    gate_part = up_part = None
    for q in range(STACK):
        rows = jnp.concatenate([pieces_of(value, q) for value in values], axis=0)
        gate_term = dot(rows, gate[q])
        up_term = dot(rows, up[q])
        gate_part = gate_term if gate_part is None else gate_part + gate_term
        up_part = up_term if up_part is None else up_part + up_term
    hidden = gate_part / (1.0 + jnp.exp(-gate_part)) * up_part
    hidden = hidden.astype(jnp.bfloat16)
    parts = [dot(hidden, down[q]).astype(jnp.bfloat16) for q in range(STACK)]
    for b in range(count):
        outs[b][...] = jnp.concatenate([p[b * CAP : (b + 1) * CAP] for p in parts], axis=0)


def final_kernel(pick_ref, weight_ref, *refs):
    blocks, out_ref = refs[:-1], refs[-1]
    width = blocks[0].shape[1]
    values = [block[...] for block in blocks]
    pick = pick_ref[...]
    for q in range(STACK):
        rows = jnp.concatenate([pieces_of(value, q) for value in values], axis=0)
        rows = (rows.astype(jnp.float32) * weight_ref[...]).astype(jnp.bfloat16)
        placed = lax.dot_general(
            pick, rows, (((0,), (0,)), ((), ())), preferred_element_type=jnp.float32
        )
        out_ref[:, q * width : (q + 1) * width] = placed.astype(jnp.bfloat16)


def in_hbm(value):
    return pltpu.with_memory_space_constraint(value, pltpu.HBM)


def after(value, *done):
    return lax.optimization_barrier((value, *done))[0]


class Line:
    def __init__(self, send):
        self.send, self.done = send, []

    def __call__(self, name, value, *done):
        self.done.append(self.send(name, value, *done, *self.done[-2:-1]))
        return self.done[-1]


def total(*terms):
    summed = terms[0].astype(jnp.float32)
    for term in terms[1:]:
        summed = summed + term.astype(jnp.float32)
    return summed.astype(jnp.bfloat16)


def local(tokens, expert_ids, route_scores, gate_weight, up_weight, down_weight):
    token_count, model_width = tokens.shape
    hidden_width = gate_weight.shape[2]
    nodes = lax.axis_size("node")
    places = lax.axis_size("local")
    teams = places // TEAM
    flight = nodes * teams
    node = lax.axis_index("node")
    team = lax.axis_index("local") // TEAM
    width = model_width // STACK
    block = jax.ShapeDtypeStruct((STACK * CAP, width), jnp.bfloat16)

    offsets = [(n, d) for n in range(nodes) for d in range(teams)]
    flight_ids = jnp.stack(
        [((node + n) % nodes * teams + (team + d) % teams) * GSIZE for n, d in offsets]
    ).astype(jnp.int32)
    packed = pl.pallas_call(
        pack_kernel,
        out_shape=[block] * flight
        + [
            jax.ShapeDtypeStruct((flight * CAP, token_count), jnp.bfloat16),
            jax.ShapeDtypeStruct((flight * CAP, 1), jnp.float32),
        ],
        in_specs=[SMEM] + [VMEM] * 2 + [HBM],
        out_specs=[VMEM] * (flight + 2),
        scratch_shapes=[
            pltpu.VMEM((STACK, token_count, width), jnp.bfloat16),
            pltpu.SemaphoreType.DMA((STACK,)),
        ],
        compiler_params=params(20),
        name="pack",
    )(flight_ids, expert_ids.T, route_scores.T, in_hbm(tokens))
    pick, weight = packed[flight:]
    packed = dict(zip(offsets, packed))

    def experts(blocks, *done):
        blocks = [after(blocks[0], *done), *blocks[1:]]
        return pl.pallas_call(
            expert_kernel,
            out_shape=[block] * len(blocks),
            in_specs=[VMEM] * (3 + len(blocks)),
            out_specs=[VMEM] * len(blocks),
            compiler_params=params(20),
            cost_estimate=pl.CostEstimate(
                flops=COST * len(blocks) * CAP * model_width * hidden_width,
                bytes_accessed=COST * model_width * hidden_width,
                transcendentals=0,
            ),
            name="experts",
        )(*weights, *blocks)

    def send(value, n, d, flip, *done):
        pairs = [
            (
                i * places + j,
                (i + n) % nodes * places + ((j + d * TEAM) % places ^ flip),
            )
            for i in range(nodes)
            for j in range(places)
        ]
        return lax.ppermute(after(value, *done) if done else value, ("node", "local"), pairs)

    def swap_y(name, value, *done):
        with jax.named_scope(name):
            return send(value, 0, 0, 1, *done)

    def swap_z(name, value, *done):
        with jax.named_scope(name):
            return send(value, 0, 0, 2, *done)

    def shift(name, value, n, d, *done):
        with jax.named_scope(name):
            return send(value, n, d, 0, *done)

    fars = [(n, d) for d in range(1, teams) for n in range(nodes)]
    own = [shift("own_core", packed[n, 0], n, 0) if n else packed[0, 0] for n in range(nodes)]
    weights = pl.pallas_call(
        load_kernel,
        out_shape=[
            pltpu.VMEM((STACK, width, hidden_width), jnp.bfloat16),
            pltpu.VMEM((STACK, width, hidden_width), jnp.bfloat16),
            pltpu.VMEM((STACK, hidden_width, width), jnp.bfloat16),
        ],
        in_specs=[HBM] * 3,
        out_specs=[VMEM] * 3,
        scratch_shapes=[pltpu.SemaphoreType.DMA((3, STACK))],
        compiler_params=params(20),
        cost_estimate=pl.CostEstimate(
            flops=0, bytes_accessed=COST * model_width * hidden_width, transcendentals=0
        ),
        name="load",
    )(in_hbm(after(gate_weight, own[-1])), in_hbm(up_weight), in_hbm(down_weight))

    y, z = Line(swap_y), Line(swap_z)
    own_y = [y("own_y%d" % n, own[n], own[-1]) for n in reversed(range(nodes))][::-1]
    own_z, own_d = [None] * nodes, [None] * nodes
    own_z[-1] = z("own_z%d" % (nodes - 1), own[-1])
    spread = {}
    x = None
    for i, key in enumerate(fars):
        tag = "far%d_" % i
        x = shift(tag, packed[key], *key, *([x, weights[0]] if i else []))
        x_z = z(tag + "z", x, weights[0], own_z[-1])
        if i:
            x_y = y(tag + "y", x)
        else:
            x_y = y(tag + "y", x, weights[0])
            for n in range(1, nodes, 2):
                own_d[n] = y("own_d%d" % n, own_z[n])
        x_d = y(tag + "d", x_z)
        spread[key] = (x, x_y, x_z, x_d)
    for n in range(nodes - 1):
        own_z[n] = z("own_z%d" % n, own[n])
    for n in range(0, nodes, 2):
        own_d[n] = z("own_d%d" % n, own_y[n])

    parts, back = {}, {}
    own_blocks = [v for n in range(nodes) for v in (own[n], own_y[n], own_z[n], own_d[n])]
    last = None
    for i, key in enumerate(fars):
        parts[key] = experts(spread[key], *([last] if i else []))
        last = parts[key][0]
    own_parts = experts(own_blocks, last)
    own_parts = [own_parts[n * TEAM : (n + 1) * TEAM] for n in range(nodes)]
    z = Line(swap_z)
    mine_y, mine_z, mine_d = [None] * nodes, [None] * nodes, [None] * nodes
    for n in range(0, nodes, 2):
        mine_d[n] = z("mine%d_d" % n, own_parts[n][3])
    for i, key in enumerate(fars):
        tag = "back%d_" % i
        x, x_y, x_z, x_d = parts[key]
        x_d = y(tag + "d", x_d)
        x_y = y(tag + "y", x_y)
        x_z = z(tag + "z", total(x_z, x_d))
        n, d = key
        back[key] = shift(tag, total(x, x_y, x_z), nodes - n, teams - d)
        if i == 0:
            mine_z[0] = z("mine0_z", own_parts[0][2])
    for n in range(1, nodes, 2):
        mine_d[n] = y("mine%d_d" % n, own_parts[n][3])
    for n in range(nodes):
        x, a_y, a_z, a_d = own_parts[n]
        tag = "mine%d_" % n
        if n % 2:
            a_z = total(a_z, mine_d[n])
        else:
            a_y = total(a_y, mine_d[n])
        a_y = y(tag + "y", a_y)
        a_z = z(tag + "z", a_z) if mine_z[n] is None else mine_z[n]
        x = total(x, a_y, a_z)
        back[n, 0] = shift("mine_core", x, nodes - n, 0) if n else x

    return pl.pallas_call(
        final_kernel,
        out_shape=jax.ShapeDtypeStruct(tokens.shape, jnp.bfloat16),
        in_specs=[VMEM] * (2 + flight),
        out_specs=VMEM,
        compiler_params=params(20),
        name="combine",
    )(pick, weight, *[back[key] for key in offsets])


def solution(mesh):
    in_specs = (
        P(("rep", "node", "local"), None),
        P(("rep", "node", "local"), None),
        P(("rep", "node", "local"), None),
        P(("node", "local"), None, None),
        P(("node", "local"), None, None),
        P(("node", "local"), None, None),
    )
    out_specs = P(("rep", "node", "local"), None)
    return jax.shard_map(local, mesh=mesh, in_specs=in_specs, out_specs=out_specs, check_vma=False)
```

time: 296 us -> 111 us (0.38); the launches traced: 291 us -> 111 us
  blocking collectives: 130 us -> 0 us
  waiting for transfers between devices: 116 us -> 54.2 us
  starting transfers between devices: 4.75 us -> 30.5 us
  Pallas kernels: 0 us -> 23.7 us
  matrix products: 22.1 us -> 0 us
  local copies, waits for them, and re-layouts: 12.2 us -> 1.39 us
  other arithmetic: 6.01 us -> 0.75 us
    all_to_all x1 -> x0, blocking collectives: 130 us -> none  [local(): lax.all_to_all(spread, ('node', 'local'), split_axis=0, concat_axis=0, ti...]
    all_to_all x1 -> x0, waiting for transfers between devices: 116 us -> none  [local(): lax.all_to_all(partial_value, ('node', 'local'), split_axis=0, concat_axi...]
    ppermute x0 -> x30, waiting for transfers between devices: none -> 54.2 us  [send(): lax.ppermute(after(value, *done) if done else value, ('node', 'local'), p...]
    ppermute x0 -> x30, starting transfers between devices: none -> 30.5 us  [send(): lax.ppermute(after(value, *done) if done else value, ('node', 'local'), p...]
    pallas_call x0 -> x6, Pallas kernels: none -> 23.7 us  [the longest x3 11.6 us: experts(): pl.pallas_call(expert_kernel, out_shape=[block] * len(blocks), in_specs=[...]
    dot_general x4 -> x0, matrix products: 22.1 us -> none  [the longest x1 12.9 us: local(): jnp.dot(hidden, down_local, preferred_element_type=jnp.float32)]
    reshape x2 -> x0, local copies, waits for them, and re-layouts: 11.2 us -> none  [the longest x1 5.61 us: local(): partial_value = partial_value.reshape(-1, row_count, model_width)]
    all_to_all x1 -> x0, starting transfers between devices: 4.75 us -> none  [local(): lax.all_to_all(partial_value, ('node', 'local'), split_axis=0, concat_axi...]
  transfers between devices with their start and end apart: 1 -> 30, of which waited for: 1 -> 17; matrix products, arithmetic and copies ran while one was open for 0% -> 1% of each run, Pallas kernels for 0% -> 17%
where the time goes in v3:
time: 111 us
  waiting for transfers between devices  54.2 us (49%)
  starting transfers between devices  30.5 us (27%)
  Pallas kernels  23.7 us (21%)
  local copies, waits for them, and re-layouts  1.39 us (1%)
    ppermute x30, waiting for transfers between devices, send(): lax.ppermute(after(value, *done) if done else value, ('node', 'local'), p...  54.2 us
    ppermute x30, starting transfers between devices, send(): lax.ppermute(after(value, *done) if done else value, ('node', 'local'), p...  30.5 us
    pallas_call x3, Pallas kernels, experts(): pl.pallas_call(expert_kernel, out_shape=[block] * len(blocks), in_specs=[...  11.6 us
    pallas_call x1, Pallas kernels, local(): pl.pallas_call(load_kernel, out_shape=[pltpu.VMEM((STACK, width, hidden_w...  7.44 us
    pallas_call x1, Pallas kernels, local(): pl.pallas_call(pack_kernel, out_shape=[block] * flight + [jax.ShapeDtypeS...  2.56 us
  transfers between devices with their start and end apart: 30, of which 17 were waited for; matrix products, arithmetic and copies ran while one was open for 1% of the time, Pallas kernels for 17%

profile of v3, /device:TPU:0, one launch (start us, length us, event | category | flops | bytes accessed | tf_op | source)
XLA Modules:
  0.0 110.6 jit_solution(16985494614181643441)
XLA Ops:
  0.1 0.7 copy-done
  0.8 0.7 copy-done.1
  1.5 2.6 %pack.1 = (bf16[72,1792]{1,0:T(8,128)(2,1)S(1)}, bf16[72,1792]{1,0:T(8,128)(2,1)S(1)}, bf16[72,1792]{1,0:T(8,128)(2,1)S(1)}, bf16[72,1792]{1,0:T(8,128)(2,1)S(1)...) custom-call(s32[4]{0:T(128)S(1)} %pad_add_fusion.flight_ref, s32[8,144]{1,0:T(8,128)S(1)} %bitcast.6, ...), custom_call_target="tpu_custom_call" | custom-call | tf_op jit(solution)/shard_map/pack/pallas_call | solution.py:164
  4.0 0.5 collective-permute-start
  4.6 3.7 %collective-permute-start.1 = (bf16[72,1792]{1,0:T(8,128)(2,1)S(1)}, bf16[72,1792]{1,0:T(8,128)(2,1)S(1)}, u32[]{:S(2)}, u32[]{:S(2)}) collective-permute-start(bf16[72,1792]{1,0:T(8,128)(2,1)S(1)} %get-tuple-element.64), channel_id=1, source_target_pairs={{0,4},{1,5},{2,6},{3,7},{4,0},{5,1},{6,2},{7,3},{8,12},{9,13},{10,... | collective-permute-start | bytes 774152 | tf_op jit(solution)/shard_map/far0_/ppermute | solution.py:208
  8.2 1.6 %collective-permute-start.5 = (bf16[72,1792]{1,0:T(8,128)(2,1)S(1)}, bf16[72,1792]{1,0:T(8,128)(2,1)S(1)}, u32[]{:S(2)}, u32[]{:S(2)}) collective-permute-start(bf16[72,1792]{1,0:T(8,128)(2,1)S(1)} %collective-permute-done.refs_4_), channel_id=1, source_target_pairs={{0,2},{1,3},{2,0},{3,1},{4,6},{5,7},{6,4},{7,5},{8,10},{9,11},{10,... | collective-permute-start | bytes 774152 | tf_op jit(solution)/shard_map/own_z1/ppermute | solution.py:208
  9.8 1.5 %collective-permute-start.3 = (bf16[72,1792]{1,0:T(8,128)(2,1)S(1)}, bf16[72,1792]{1,0:T(8,128)(2,1)S(1)}, u32[]{:S(2)}, u32[]{:S(2)}) collective-permute-start(bf16[72,1792]{1,0:T(8,128)(2,1)S(1)} %collective-permute-done.refs_4_), channel_id=1, source_target_pairs={{0,1},{1,0},{2,3},{3,2},{4,5},{5,4},{6,7},{7,6},{8,9},{9,8},{10,11... | collective-permute-start | bytes 774152 | tf_op jit(solution)/shard_map/own_y1/ppermute | solution.py:208
  11.3 0.5 collective-permute-start.8
  11.8 7.4 %load.1 = (bf16[4,1792,512]{2,1,0:T(8,128)(2,1)S(1)}, bf16[4,1792,512]{2,1,0:T(8,128)(2,1)S(1)}, bf16[4,512,1792]{2,1,0:T(8,128)(2,1)S(1)}) custom-call(bf16[1,7168,512]{2,1,0:T(8,128)(2,1)} %gate_hbm, bf16[1,7168,512]{2,1,0:T(8,128)(2,1)} %up_hbm.1, bf16[1,512,7168]{2,1,0:T(8,128)(2,1)} %down_hbm.1), custom_call_target="tpu_custom_call" | custom-call | bytes 220200960 | tf_op jit(solution)/shard_map/load/pallas_call | solution.py:224
  19.3 1.4 %collective-permute-done.1.refs_0_ = bf16[72,1792]{1,0:T(8,128)(2,1)S(1)} collective-permute-done((bf16[72,1792]{1,0:T(8,128)(2,1)S(1)}, bf16[72,1792]{1,0:T(8,128)(2,1)S(1)}, u32[]{:S(2)}, u32[]{:S(2)}) %collective-permute-start.1) | collective-permute-done | bytes 258080 | tf_op jit(solution)/shard_map/far0_/ppermute | solution.py:208
  20.9 1.6 %collective-permute-start.4 = (bf16[72,1792]{1,0:T(8,128)(2,1)S(1)}, bf16[72,1792]{1,0:T(8,128)(2,1)S(1)}, u32[]{:S(2)}, u32[]{:S(2)}) collective-permute-start(bf16[72,1792]{1,0:T(8,128)(2,1)S(1)} %collective-permute-done.1.refs_0_), channel_id=1, source_target_pairs={{0,1},{1,0},{2,3},{3,2},{4,5},{5,4},{6,7},{7,6},{8,9},{9,8},{10,11... | collective-permute-start | bytes 774152 | tf_op jit(solution)/shard_map/far0_y/ppermute | solution.py:208
  22.5 1.4 %collective-permute-start.6 = (bf16[72,1792]{1,0:T(8,128)(2,1)S(1)}, bf16[72,1792]{1,0:T(8,128)(2,1)S(1)}, u32[]{:S(2)}, u32[]{:S(2)}) collective-permute-start(bf16[72,1792]{1,0:T(8,128)(2,1)S(1)} %collective-permute-done.1.refs_0_), channel_id=1, source_target_pairs={{0,2},{1,3},{2,0},{3,1},{4,6},{5,7},{6,4},{7,5},{8,10},{9,11},{10,... | collective-permute-start | bytes 774152 | tf_op jit(solution)/shard_map/far0_z/ppermute | solution.py:208
  23.9 1.5 %collective-permute-start.2 = (bf16[72,1792]{1,0:T(8,128)(2,1)S(1)}, bf16[72,1792]{1,0:T(8,128)(2,1)S(1)}, u32[]{:S(2)}, u32[]{:S(2)}) collective-permute-start(bf16[72,1792]{1,0:T(8,128)(2,1)S(1)} %get-tuple-element.65), channel_id=1, source_target_pairs={{0,12},{1,13},{2,14},{3,15},{4,8},{5,9},{6,10},{7,11},{8,4},{9,5},... | collective-permute-start | bytes 774152 | tf_op jit(solution)/shard_map/far1_/ppermute | solution.py:208
  25.4 0.5 collective-permute-start.9
  25.9 3.0 %collective-permute-done.4.refs_1_ = bf16[72,1792]{1,0:T(8,128)(2,1)S(1)} collective-permute-done((bf16[72,1792]{1,0:T(8,128)(2,1)S(1)}, bf16[72,1792]{1,0:T(8,128)(2,1)S(1)}, u32[]{:S(2)}, u32[]{:S(2)}) %collective-permute-start.4) | collective-permute-done | bytes 258080 | tf_op jit(solution)/shard_map/far0_y/ppermute | solution.py:208
  28.9 5.0 %collective-permute-done.6.refs_2_ = bf16[72,1792]{1,0:T(8,128)(2,1)S(1)} collective-permute-done((bf16[72,1792]{1,0:T(8,128)(2,1)S(1)}, bf16[72,1792]{1,0:T(8,128)(2,1)S(1)}, u32[]{:S(2)}, u32[]{:S(2)}) %collective-permute-start.6) | collective-permute-done | bytes 258080 | tf_op jit(solution)/shard_map/far0_z/ppermute | solution.py:208
  33.9 0.6 collective-permute-start.7
  34.5 4.1 %collective-permute-done.2.refs_0_ = bf16[72,1792]{1,0:T(8,128)(2,1)S(1)} collective-permute-done((bf16[72,1792]{1,0:T(8,128)(2,1)S(1)}, bf16[72,1792]{1,0:T(8,128)(2,1)S(1)}, u32[]{:S(2)}, u32[]{:S(2)}) %collective-permute-start.2) | collective-permute-done | bytes 258080 | tf_op jit(solution)/shard_map/far1_/ppermute | solution.py:208
  38.6 0.5 collective-permute-start.10
  39.1 1.1 collective-permute-done.7.refs_3_
  40.2 4.0 %experts.3 = (bf16[72,1792]{1,0:T(8,128)(2,1)S(1)}, bf16[72,1792]{1,0:T(8,128)(2,1)S(1)}, bf16[72,1792]{1,0:T(8,128)(2,1)S(1)}, bf16[72,1792]{1,0:T(8,128)(2,1)S(1)}) custom-call(bf16[4,1792,512]{2,1,0:T(8,128)(2,1)S(1)} %get-tuple-element.59.gate, bf16[4,1792,512]{2,1,0:T(8,128)(2,1)S(1)} %get-tuple-element.60.up, ...), custom_call_target="tpu_custom_call" | custom-call | flops 15854469120 | bytes 220200960 | tf_op jit(solution)/shard_map/experts/pallas_call | solution.py:185
  44.2 2.7 %collective-permute-done.10.refs_1_ = bf16[72,1792]{1,0:T(8,128)(2,1)S(1)} collective-permute-done((bf16[72,1792]{1,0:T(8,128)(2,1)S(1)}, bf16[72,1792]{1,0:T(8,128)(2,1)S(1)}, u32[]{:S(2)}, u32[]{:S(2)}) %collective-permute-start.10) | collective-permute-done | bytes 258080 | tf_op jit(solution)/shard_map/far1_y/ppermute | solution.py:208
  46.8 0.5 collective-permute-start.20
  47.4 1.7 %collective-permute-start.14 = (bf16[72,1792]{1,0:T(8,128)(2,1)S(1)}, bf16[72,1792]{1,0:T(8,128)(2,1)S(1)}, u32[]{:S(2)}, u32[]{:S(2)}) collective-permute-start(bf16[72,1792]{1,0:T(8,128)(2,1)S(1)} %collective-permute-done.8.refs_1_), channel_id=1, source_target_pairs={{0,2},{1,3},{2,0},{3,1},{4,6},{5,7},{6,4},{7,5},{8,10},{9,11},{10,... | collective-permute-start | bytes 774152 | tf_op jit(solution)/shard_map/own_d0/ppermute | solution.py:208
  49.4 1.5 %collective-permute-start.12 = (bf16[72,1792]{1,0:T(8,128)(2,1)S(1)}, bf16[72,1792]{1,0:T(8,128)(2,1)S(1)}, u32[]{:S(2)}, u32[]{:S(2)}) collective-permute-start(bf16[72,1792]{1,0:T(8,128)(2,1)S(1)} %collective-permute-done.11.refs_2_), channel_id=1, source_target_pairs={{0,1},{1,0},{2,3},{3,2},{4,5},{5,4},{6,7},{7,6},{8,9},{9,8},{10,11... | collective-permute-start | bytes 774152 | tf_op jit(solution)/shard_map/far1_d/ppermute | solution.py:208
  50.9 5.1 %collective-permute-done.20 = bf16[72,1792]{1,0:T(8,128)(2,1)S(1)} collective-permute-done((bf16[72,1792]{1,0:T(8,128)(2,1)S(1)}, bf16[72,1792]{1,0:T(8,128)(2,1)S(1)}, u32[]{:S(2)}, u32[]{:S(2)}) %collective-permute-start.20) | collective-permute-done | bytes 258080 | tf_op jit(solution)/shard_map/back0_d/ppermute | solution.py:208
  56.1 1.8 %collective-permute-start.21 = (bf16[72,1792]{1,0:T(8,128)(2,1)S(1)}, bf16[72,1792]{1,0:T(8,128)(2,1)S(1)}, u32[]{:S(2)}, u32[]{:S(2)}) collective-permute-start(bf16[72,1792]{1,0:T(8,128)(2,1)S(1)} %add_convert_fusion.5), channel_id=1, source_target_pairs={{0,2},{1,3},{2,0},{3,1},{4,6},{5,7},{6,4},{7,5},{8,10},{9,11},{10,... | collective-permute-start | bytes 774152 | tf_op jit(solution)/shard_map/back0_z/ppermute | solution.py:208
  57.9 1.9 %collective-permute-done.12.refs_3_ = bf16[72,1792]{1,0:T(8,128)(2,1)S(1)} collective-permute-done((bf16[72,1792]{1,0:T(8,128)(2,1)S(1)}, bf16[72,1792]{1,0:T(8,128)(2,1)S(1)}, u32[]{:S(2)}, u32[]{:S(2)}) %collective-permute-start.12) | collective-permute-done | bytes 258080 | tf_op jit(solution)/shard_map/far1_d/ppermute | solution.py:208
  59.8 4.0 %experts.4 = (bf16[72,1792]{1,0:T(8,128)(2,1)S(1)}, bf16[72,1792]{1,0:T(8,128)(2,1)S(1)}, bf16[72,1792]{1,0:T(8,128)(2,1)S(1)}, bf16[72,1792]{1,0:T(8,128)(2,1)S(1)}) custom-call(bf16[4,1792,512]{2,1,0:T(8,128)(2,1)S(1)} %get-tuple-element.59.gate, bf16[4,1792,512]{2,1,0:T(8,128)(2,1)S(1)} %get-tuple-element.60.up, ...), custom_call_target="tpu_custom_call" | custom-call | flops 15854469120 | bytes 220200960 | tf_op jit(solution)/shard_map/experts/pallas_call | solution.py:185
  63.8 0.6 collective-permute-start.23
  64.4 1.5 %collective-permute-start.16 = (bf16[72,1792]{1,0:T(8,128)(2,1)S(1)}, bf16[72,1792]{1,0:T(8,128)(2,1)S(1)}, u32[]{:S(2)}, u32[]{:S(2)}) collective-permute-start(bf16[72,1792]{1,0:T(8,128)(2,1)S(1)} %get-tuple-element.86), channel_id=1, source_target_pairs={{0,1},{1,0},{2,3},{3,2},{4,5},{5,4},{6,7},{7,6},{8,9},{9,8},{10,11... | collective-permute-start | bytes 774152 | tf_op jit(solution)/shard_map/back0_y/ppermute | solution.py:208
  65.9 3.6 %experts.5 = (bf16[72,1792]{1,0:T(8,128)(2,1)S(1)}, bf16[72,1792]{1,0:T(8,128)(2,1)S(1)}, bf16[72,1792]{1,0:T(8,128)(2,1)S(1)}, bf16[72,1792]{1,0:T(8,128)(2,1)S...) custom-call(bf16[4,1792,512]{2,1,0:T(8,128)(2,1)S(1)} %get-tuple-ele, ...), custom_call_target="tpu_custom_call" | custom-call | flops 31708938240 | bytes 220200960 | tf_op jit(solution)/shard_map/experts/pallas_call | solution.py:185
  69.5 1.5 %collective-permute-start.15 = (bf16[72,1792]{1,0:T(8,128)(2,1)S(1)}, bf16[72,1792]{1,0:T(8,128)(2,1)S(1)}, u32[]{:S(2)}, u32[]{:S(2)}) collective-permute-start(bf16[72,1792]{1,0:T(8,128)(2,1)S(1)} %get-tuple-element.83), channel_id=1, source_target_pairs={{0,2},{1,3},{2,0},{3,1},{4,6},{5,7},{6,4},{7,5},{8,10},{9,11},{10,... | collective-permute-start | bytes 774152 | tf_op jit(solution)/shard_map/mine0_d/ppermute | solution.py:208
  71.0 2.0 %collective-permute-done.23 = bf16[72,1792]{1,0:T(8,128)(2,1)S(1)} collective-permute-done((bf16[72,1792]{1,0:T(8,128)(2,1)S(1)}, bf16[72,1792]{1,0:T(8,128)(2,1)S(1)}, u32[]{:S(2)}, u32[]{:S(2)}) %collective-permute-start.23) | collective-permute-done | bytes 258080 | tf_op jit(solution)/shard_map/back1_d/ppermute | solution.py:208
  73.1 1.3 %collective-permute-start.28 = (bf16[72,1792]{1,0:T(8,128)(2,1)S(1)}, bf16[72,1792]{1,0:T(8,128)(2,1)S(1)}, u32[]{:S(2)}, u32[]{:S(2)}) collective-permute-start(bf16[72,1792]{1,0:T(8,128)(2,1)S(1)} %add_convert_fusion.1), channel_id=1, source_target_pairs={{0,2},{1,3},{2,0},{3,1},{4,6},{5,7},{6,4},{7,5},{8,10},{9,11},{10,... | collective-permute-start | bytes 774152 | tf_op jit(solution)/shard_map/back1_z/ppermute | solution.py:208
  74.4 1.5 %collective-permute-done.16 = bf16[72,1792]{1,0:T(8,128)(2,1)S(1)} collective-permute-done((bf16[72,1792]{1,0:T(8,128)(2,1)S(1)}, bf16[72,1792]{1,0:T(8,128)(2,1)S(1)}, u32[]{:S(2)}, u32[]{:S(2)}) %collective-permute-start.16) | collective-permute-done | bytes 258080 | tf_op jit(solution)/shard_map/back0_y/ppermute | solution.py:208
  75.9 0.5 collective-permute-start.17
  76.5 1.3 %collective-permute-start.22 = (bf16[72,1792]{1,0:T(8,128)(2,1)S(1)}, bf16[72,1792]{1,0:T(8,128)(2,1)S(1)}, u32[]{:S(2)}, u32[]{:S(2)}) collective-permute-start(bf16[72,1792]{1,0:T(8,128)(2,1)S(1)} %add_convert_fusion.4), channel_id=1, source_target_pairs={{0,4},{1,5},{2,6},{3,7},{4,0},{5,1},{6,2},{7,3},{8,12},{9,13},{10,... | collective-permute-start | bytes 774152 | tf_op jit(solution)/shard_map/back0_/ppermute | solution.py:208
  77.8 1.5 %collective-permute-start.24 = (bf16[72,1792]{1,0:T(8,128)(2,1)S(1)}, bf16[72,1792]{1,0:T(8,128)(2,1)S(1)}, u32[]{:S(2)}, u32[]{:S(2)}) collective-permute-start(bf16[72,1792]{1,0:T(8,128)(2,1)S(1)} %get-tuple-element.99), channel_id=1, source_target_pairs={{0,1},{1,0},{2,3},{3,2},{4,5},{5,4},{6,7},{7,6},{8,9},{9,8},{10,11... | collective-permute-start | bytes 774152 | tf_op jit(solution)/shard_map/mine1_d/ppermute | solution.py:208
  79.3 2.3 %collective-permute-done.15 = bf16[72,1792]{1,0:T(8,128)(2,1)S(1)} collective-permute-done((bf16[72,1792]{1,0:T(8,128)(2,1)S(1)}, bf16[72,1792]{1,0:T(8,128)(2,1)S(1)}, u32[]{:S(2)}, u32[]{:S(2)}) %collective-permute-start.15) | collective-permute-done | bytes 258080 | tf_op jit(solution)/shard_map/mine0_d/ppermute | solution.py:208
  81.7 6.1 %collective-permute-done.24 = bf16[72,1792]{1,0:T(8,128)(2,1)S(1)} collective-permute-done((bf16[72,1792]{1,0:T(8,128)(2,1)S(1)}, bf16[72,1792]{1,0:T(8,128)(2,1)S(1)}, u32[]{:S(2)}, u32[]{:S(2)}) %collective-permute-start.24) | collective-permute-done | bytes 258080 | tf_op jit(solution)/shard_map/mine1_d/ppermute | solution.py:208
  87.8 0.5 collective-permute-start.25
  88.4 4.2 %collective-permute-done.19 = bf16[72,1792]{1,0:T(8,128)(2,1)S(1)} collective-permute-done((bf16[72,1792]{1,0:T(8,128)(2,1)S(1)}, bf16[72,1792]{1,0:T(8,128)(2,1)S(1)}, u32[]{:S(2)}, u32[]{:S(2)}) %collective-permute-start.19) | collective-permute-done | bytes 258080 | tf_op jit(solution)/shard_map/mine0_z/ppermute | solution.py:208
  92.6 1.4 %collective-permute-start.26 = (bf16[72,1792]{1,0:T(8,128)(2,1)S(1)}, bf16[72,1792]{1,0:T(8,128)(2,1)S(1)}, u32[]{:S(2)}, u32[]{:S(2)}) collective-permute-start(bf16[72,1792]{1,0:T(8,128)(2,1)S(1)} %add_convert_fusion.3), channel_id=1, source_target_pairs={{0,2},{1,3},{2,0},{3,1},{4,6},{5,7},{6,4},{7,5},{8,10},{9,11},{10,... | collective-permute-start | bytes 774152 | tf_op jit(solution)/shard_map/mine1_z/ppermute | solution.py:208
  94.7 6.3 %collective-permute-done.26 = bf16[72,1792]{1,0:T(8,128)(2,1)S(1)} collective-permute-done((bf16[72,1792]{1,0:T(8,128)(2,1)S(1)}, bf16[72,1792]{1,0:T(8,128)(2,1)S(1)}, u32[]{:S(2)}, u32[]{:S(2)}) %collective-permute-start.26) | collective-permute-done | bytes 258080 | tf_op jit(solution)/shard_map/mine1_z/ppermute | solution.py:208
  101.1 1.4 %collective-permute-done.18 = bf16[72,1792]{1,0:T(8,128)(2,1)S(1)} collective-permute-done((bf16[72,1792]{1,0:T(8,128)(2,1)S(1)}, bf16[72,1792]{1,0:T(8,128)(2,1)S(1)}, u32[]{:S(2)}, u32[]{:S(2)}) %collective-permute-start.18) | collective-permute-done | bytes 258080 | tf_op jit(solution)/shard_map/mine0_y/ppermute | solution.py:208
  102.6 5.9 %collective-permute-done.29.refs_3_ = bf16[72,1792]{1,0:T(8,128)(2,1)S(1)} collective-permute-done((bf16[72,1792]{1,0:T(8,128)(2,1)S(1)}, bf16[72,1792]{1,0:T(8,128)(2,1)S(1)}, u32[]{:S(2)}, u32[]{:S(2)}) %collective-permute-start.29) | collective-permute-done | bytes 258080 | tf_op jit(solution)/shard_map/back1_/ppermute | solution.py:208
  108.5 2.1 %combine.1 = bf16[144,7168]{1,0:T(8,128)(2,1)} custom-call(bf16[72,144]{1,0:T(8,128)(2,1)S(1)} %get-tuple-element.55.pick_ref, f32[72,1]{1,0:T(8,128)S(1)} %get-tuple-element.56.weight_ref, bf16[72,1792]{1,0:T(8,128)(2,1)S(1)} %add_convert_fusion.6.refs_0_, bf16[72,1792]{1,0:T(8,128)(2,1)S(1)} %collective-permute-done.22.refs_1_, ...), custom_call_target="tpu_custom_call" | custom-call | tf_op jit(solution)/shard_map/combine/pallas_call | solution.py:300
  (31 shorter events, 1.9 us)
Async XLA Ops:
  0.1 0.7 copy-start
  0.8 0.7 copy-start.1
  4.0 4.2 %collective-permute-start = (bf16[72,1792]{1,0:T(8,128)(2,1)S(1)}, bf16[72,1792]{1,0:T(8,128)(2,1)S(1)}, u32[]{:S(2)}, u32[]{:S(2)}) collective-permute-start(bf16[72,1792]{1,0:T(8,128)(2,1)S(1)} %get-tuple-element.57), channel_id=1, source_target_pairs={{0,8},{1,9},{2,10},{3,11},{4,12},{5,13},{6,14},{7,15},{8,0},{9,1},... | collective-permute-start | bytes 774152 | tf_op jit(solution)/shard_map/own_core/ppermute | solution.py:208
  4.6 16.1 %collective-permute-start.1 = (bf16[72,1792]{1,0:T(8,128)(2,1)S(1)}, bf16[72,1792]{1,0:T(8,128)(2,1)S(1)}, u32[]{:S(2)}, u32[]{:S(2)}) collective-permute-start(bf16[72,1792]{1,0:T(8,128)(2,1)S(1)} %get-tuple-element.64), channel_id=1, source_target_pairs={{0,4},{1,5},{2,6},{3,7},{4,0},{5,1},{6,2},{7,3},{8,12},{9,13},{10,... | collective-permute-start | bytes 774152 | tf_op jit(solution)/shard_map/far0_/ppermute | solution.py:208
  8.2 12.6 %collective-permute-start.5 = (bf16[72,1792]{1,0:T(8,128)(2,1)S(1)}, bf16[72,1792]{1,0:T(8,128)(2,1)S(1)}, u32[]{:S(2)}, u32[]{:S(2)}) collective-permute-start(bf16[72,1792]{1,0:T(8,128)(2,1)S(1)} %collective-permute-done.refs_4_), channel_id=1, source_target_pairs={{0,2},{1,3},{2,0},{3,1},{4,6},{5,7},{6,4},{7,5},{8,10},{9,11},{10,... | collective-permute-start | bytes 774152 | tf_op jit(solution)/shard_map/own_z1/ppermute | solution.py:208
  9.8 11.1 %collective-permute-start.3 = (bf16[72,1792]{1,0:T(8,128)(2,1)S(1)}, bf16[72,1792]{1,0:T(8,128)(2,1)S(1)}, u32[]{:S(2)}, u32[]{:S(2)}) collective-permute-start(bf16[72,1792]{1,0:T(8,128)(2,1)S(1)} %collective-permute-done.refs_4_), channel_id=1, source_target_pairs={{0,1},{1,0},{2,3},{3,2},{4,5},{5,4},{6,7},{7,6},{8,9},{9,8},{10,11... | collective-permute-start | bytes 774152 | tf_op jit(solution)/shard_map/own_y1/ppermute | solution.py:208
  11.3 14.0 %collective-permute-start.8 = (bf16[72,1792]{1,0:T(8,128)(2,1)S(1)}, bf16[72,1792]{1,0:T(8,128)(2,1)S(1)}, u32[]{:S(2)}, u32[]{:S(2)}) collective-permute-start(bf16[72,1792]{1,0:T(8,128)(2,1)S(1)} %get-tuple-element.79.refs_0_), channel_id=1, source_target_pairs={{0,1},{1,0},{2,3},{3,2},{4,5},{5,4},{6,7},{7,6},{8,9},{9,8},{10,11... | collective-permute-start | bytes 774152 | tf_op jit(solution)/shard_map/own_y0/ppermute | solution.py:208
  20.9 8.0 %collective-permute-start.4 = (bf16[72,1792]{1,0:T(8,128)(2,1)S(1)}, bf16[72,1792]{1,0:T(8,128)(2,1)S(1)}, u32[]{:S(2)}, u32[]{:S(2)}) collective-permute-start(bf16[72,1792]{1,0:T(8,128)(2,1)S(1)} %collective-permute-done.1.refs_0_), channel_id=1, source_target_pairs={{0,1},{1,0},{2,3},{3,2},{4,5},{5,4},{6,7},{7,6},{8,9},{9,8},{10,11... | collective-permute-start | bytes 774152 | tf_op jit(solution)/shard_map/far0_y/ppermute | solution.py:208
  22.5 11.4 %collective-permute-start.6 = (bf16[72,1792]{1,0:T(8,128)(2,1)S(1)}, bf16[72,1792]{1,0:T(8,128)(2,1)S(1)}, u32[]{:S(2)}, u32[]{:S(2)}) collective-permute-start(bf16[72,1792]{1,0:T(8,128)(2,1)S(1)} %collective-permute-done.1.refs_0_), channel_id=1, source_target_pairs={{0,2},{1,3},{2,0},{3,1},{4,6},{5,7},{6,4},{7,5},{8,10},{9,11},{10,... | collective-permute-start | bytes 774152 | tf_op jit(solution)/shard_map/far0_z/ppermute | solution.py:208
  23.9 14.7 %collective-permute-start.2 = (bf16[72,1792]{1,0:T(8,128)(2,1)S(1)}, bf16[72,1792]{1,0:T(8,128)(2,1)S(1)}, u32[]{:S(2)}, u32[]{:S(2)}) collective-permute-start(bf16[72,1792]{1,0:T(8,128)(2,1)S(1)} %get-tuple-element.65), channel_id=1, source_target_pairs={{0,12},{1,13},{2,14},{3,15},{4,8},{5,9},{6,10},{7,11},{8,4},{9,5},... | collective-permute-start | bytes 774152 | tf_op jit(solution)/shard_map/far1_/ppermute | solution.py:208
  25.4 13.2 %collective-permute-start.9 = (bf16[72,1792]{1,0:T(8,128)(2,1)S(1)}, bf16[72,1792]{1,0:T(8,128)(2,1)S(1)}, u32[]{:S(2)}, u32[]{:S(2)}) collective-permute-start(bf16[72,1792]{1,0:T(8,128)(2,1)S(1)} %collective-permute-done.5.refs_6_), channel_id=1, source_target_pairs={{0,1},{1,0},{2,3},{3,2},{4,5},{5,4},{6,7},{7,6},{8,9},{9,8},{10,11... | collective-permute-start | bytes 774152 | tf_op jit(solution)/shard_map/own_d1/ppermute | solution.py:208
  33.9 6.3 %collective-permute-start.7 = (bf16[72,1792]{1,0:T(8,128)(2,1)S(1)}, bf16[72,1792]{1,0:T(8,128)(2,1)S(1)}, u32[]{:S(2)}, u32[]{:S(2)}) collective-permute-start(bf16[72,1792]{1,0:T(8,128)(2,1)S(1)} %collective-permute-done.6.refs_2_), channel_id=1, source_target_pairs={{0,1},{1,0},{2,3},{3,2},{4,5},{5,4},{6,7},{7,6},{8,9},{9,8},{10,11... | collective-permute-start | bytes 774152 | tf_op jit(solution)/shard_map/far0_d/ppermute | solution.py:208
  38.6 8.8 %collective-permute-start.11 = (bf16[72,1792]{1,0:T(8,128)(2,1)S(1)}, bf16[72,1792]{1,0:T(8,128)(2,1)S(1)}, u32[]{:S(2)}, u32[]{:S(2)}) collective-permute-start(bf16[72,1792]{1,0:T(8,128)(2,1)S(1)} %collective-permute-done.2.refs_0_), channel_id=1, source_target_pairs={{0,2},{1,3},{2,0},{3,1},{4,6},{5,7},{6,4},{7,5},{8,10},{9,11},{10,... | collective-permute-start | bytes 774152 | tf_op jit(solution)/shard_map/far1_z/ppermute | solution.py:208
  38.6 8.3 %collective-permute-start.10 = (bf16[72,1792]{1,0:T(8,128)(2,1)S(1)}, bf16[72,1792]{1,0:T(8,128)(2,1)S(1)}, u32[]{:S(2)}, u32[]{:S(2)}) collective-permute-start(bf16[72,1792]{1,0:T(8,128)(2,1)S(1)} %collective-permute-done.2.refs_0_), channel_id=1, source_target_pairs={{0,1},{1,0},{2,3},{3,2},{4,5},{5,4},{6,7},{7,6},{8,9},{9,8},{10,11... | collective-permute-start | bytes 774152 | tf_op jit(solution)/shard_map/far1_y/ppermute | solution.py:208
  46.8 9.2 %collective-permute-start.20 = (bf16[72,1792]{1,0:T(8,128)(2,1)S(1)}, bf16[72,1792]{1,0:T(8,128)(2,1)S(1)}, u32[]{:S(2)}, u32[]{:S(2)}) collective-permute-start(bf16[72,1792]{1,0:T(8,128)(2,1)S(1)} %get-tuple-element.93), channel_id=1, source_target_pairs={{0,1},{1,0},{2,3},{3,2},{4,5},{5,4},{6,7},{7,6},{8,9},{9,8},{10,11... | collective-permute-start | bytes 774152 | tf_op jit(solution)/shard_map/back0_d/ppermute | solution.py:208
  47.4 18.5 %collective-permute-start.14 = (bf16[72,1792]{1,0:T(8,128)(2,1)S(1)}, bf16[72,1792]{1,0:T(8,128)(2,1)S(1)}, u32[]{:S(2)}, u32[]{:S(2)}) collective-permute-start(bf16[72,1792]{1,0:T(8,128)(2,1)S(1)} %collective-permute-done.8.refs_1_), channel_id=1, source_target_pairs={{0,2},{1,3},{2,0},{3,1},{4,6},{5,7},{6,4},{7,5},{8,10},{9,11},{10,... | collective-permute-start | bytes 774152 | tf_op jit(solution)/shard_map/own_d0/ppermute | solution.py:208
  49.1 16.8 %collective-permute-start.13 = (bf16[72,1792]{1,0:T(8,128)(2,1)S(1)}, bf16[72,1792]{1,0:T(8,128)(2,1)S(1)}, u32[]{:S(2)}, u32[]{:S(2)}) collective-permute-start(bf16[72,1792]{1,0:T(8,128)(2,1)S(1)} %get-tuple-element.79.refs_0_), channel_id=1, source_target_pairs={{0,2},{1,3},{2,0},{3,1},{4,6},{5,7},{6,4},{7,5},{8,10},{9,11},{10,... | collective-permute-start | bytes 774152 | tf_op jit(solution)/shard_map/own_z0/ppermute | solution.py:208
  49.4 10.4 %collective-permute-start.12 = (bf16[72,1792]{1,0:T(8,128)(2,1)S(1)}, bf16[72,1792]{1,0:T(8,128)(2,1)S(1)}, u32[]{:S(2)}, u32[]{:S(2)}) collective-permute-start(bf16[72,1792]{1,0:T(8,128)(2,1)S(1)} %collective-permute-done.11.refs_2_), channel_id=1, source_target_pairs={{0,1},{1,0},{2,3},{3,2},{4,5},{5,4},{6,7},{7,6},{8,9},{9,8},{10,11... | collective-permute-start | bytes 774152 | tf_op jit(solution)/shard_map/far1_d/ppermute | solution.py:208
  56.1 17.0 %collective-permute-start.21 = (bf16[72,1792]{1,0:T(8,128)(2,1)S(1)}, bf16[72,1792]{1,0:T(8,128)(2,1)S(1)}, u32[]{:S(2)}, u32[]{:S(2)}) collective-permute-start(bf16[72,1792]{1,0:T(8,128)(2,1)S(1)} %add_convert_fusion.5), channel_id=1, source_target_pairs={{0,2},{1,3},{2,0},{3,1},{4,6},{5,7},{6,4},{7,5},{8,10},{9,11},{10,... | collective-permute-start | bytes 774152 | tf_op jit(solution)/shard_map/back0_z/ppermute | solution.py:208
  63.8 9.2 %collective-permute-start.23 = (bf16[72,1792]{1,0:T(8,128)(2,1)S(1)}, bf16[72,1792]{1,0:T(8,128)(2,1)S(1)}, u32[]{:S(2)}, u32[]{:S(2)}) collective-permute-start(bf16[72,1792]{1,0:T(8,128)(2,1)S(1)} %get-tuple-element.98), channel_id=1, source_target_pairs={{0,1},{1,0},{2,3},{3,2},{4,5},{5,4},{6,7},{7,6},{8,9},{9,8},{10,11... | collective-permute-start | bytes 774152 | tf_op jit(solution)/shard_map/back1_d/ppermute | solution.py:208
  64.4 11.5 %collective-permute-start.16 = (bf16[72,1792]{1,0:T(8,128)(2,1)S(1)}, bf16[72,1792]{1,0:T(8,128)(2,1)S(1)}, u32[]{:S(2)}, u32[]{:S(2)}) collective-permute-start(bf16[72,1792]{1,0:T(8,128)(2,1)S(1)} %get-tuple-element.86), channel_id=1, source_target_pairs={{0,1},{1,0},{2,3},{3,2},{4,5},{5,4},{6,7},{7,6},{8,9},{9,8},{10,11... | collective-permute-start | bytes 774152 | tf_op jit(solution)/shard_map/back0_y/ppermute | solution.py:208
  69.5 12.1 %collective-permute-start.15 = (bf16[72,1792]{1,0:T(8,128)(2,1)S(1)}, bf16[72,1792]{1,0:T(8,128)(2,1)S(1)}, u32[]{:S(2)}, u32[]{:S(2)}) collective-permute-start(bf16[72,1792]{1,0:T(8,128)(2,1)S(1)} %get-tuple-element.83), channel_id=1, source_target_pairs={{0,2},{1,3},{2,0},{3,1},{4,6},{5,7},{6,4},{7,5},{8,10},{9,11},{10,... | collective-permute-start | bytes 774152 | tf_op jit(solution)/shard_map/mine0_d/ppermute | solution.py:208
  73.1 20.9 %collective-permute-start.28 = (bf16[72,1792]{1,0:T(8,128)(2,1)S(1)}, bf16[72,1792]{1,0:T(8,128)(2,1)S(1)}, u32[]{:S(2)}, u32[]{:S(2)}) collective-permute-start(bf16[72,1792]{1,0:T(8,128)(2,1)S(1)} %add_convert_fusion.1), channel_id=1, source_target_pairs={{0,2},{1,3},{2,0},{3,1},{4,6},{5,7},{6,4},{7,5},{8,10},{9,11},{10,... | collective-permute-start | bytes 774152 | tf_op jit(solution)/shard_map/back1_z/ppermute | solution.py:208
  75.9 18.1 %collective-permute-start.17 = (bf16[72,1792]{1,0:T(8,128)(2,1)S(1)}, bf16[72,1792]{1,0:T(8,128)(2,1)S(1)}, u32[]{:S(2)}, u32[]{:S(2)}) collective-permute-start(bf16[72,1792]{1,0:T(8,128)(2,1)S(1)} %get-tuple-element.87), channel_id=1, source_target_pairs={{0,1},{1,0},{2,3},{3,2},{4,5},{5,4},{6,7},{7,6},{8,9},{9,8},{10,11... | collective-permute-start | bytes 774152 | tf_op jit(solution)/shard_map/back1_y/ppermute | solution.py:208
  76.5 26.1 %collective-permute-start.22 = (bf16[72,1792]{1,0:T(8,128)(2,1)S(1)}, bf16[72,1792]{1,0:T(8,128)(2,1)S(1)}, u32[]{:S(2)}, u32[]{:S(2)}) collective-permute-start(bf16[72,1792]{1,0:T(8,128)(2,1)S(1)} %add_convert_fusion.4), channel_id=1, source_target_pairs={{0,4},{1,5},{2,6},{3,7},{4,0},{5,1},{6,2},{7,3},{8,12},{9,13},{10,... | collective-permute-start | bytes 774152 | tf_op jit(solution)/shard_map/back0_/ppermute | solution.py:208
  77.8 10.0 %collective-permute-start.24 = (bf16[72,1792]{1,0:T(8,128)(2,1)S(1)}, bf16[72,1792]{1,0:T(8,128)(2,1)S(1)}, u32[]{:S(2)}, u32[]{:S(2)}) collective-permute-start(bf16[72,1792]{1,0:T(8,128)(2,1)S(1)} %get-tuple-element.99), channel_id=1, source_target_pairs={{0,1},{1,0},{2,3},{3,2},{4,5},{5,4},{6,7},{7,6},{8,9},{9,8},{10,11... | collective-permute-start | bytes 774152 | tf_op jit(solution)/shard_map/mine1_d/ppermute | solution.py:208
  81.6 10.9 %collective-permute-start.19 = (bf16[72,1792]{1,0:T(8,128)(2,1)S(1)}, bf16[72,1792]{1,0:T(8,128)(2,1)S(1)}, u32[]{:S(2)}, u32[]{:S(2)}) collective-permute-start(bf16[72,1792]{1,0:T(8,128)(2,1)S(1)} %get-tuple-element.90), channel_id=1, source_target_pairs={{0,2},{1,3},{2,0},{3,1},{4,6},{5,7},{6,4},{7,5},{8,10},{9,11},{10,... | collective-permute-start | bytes 774152 | tf_op jit(solution)/shard_map/mine0_z/ppermute | solution.py:208
  87.8 6.8 %collective-permute-start.25 = (bf16[72,1792]{1,0:T(8,128)(2,1)S(1)}, bf16[72,1792]{1,0:T(8,128)(2,1)S(1)}, u32[]{:S(2)}, u32[]{:S(2)}) collective-permute-start(bf16[72,1792]{1,0:T(8,128)(2,1)S(1)} %get-tuple-element.100), channel_id=1, source_target_pairs={{0,1},{1,0},{2,3},{3,2},{4,5},{5,4},{6,7},{7,6},{8,9},{9,8},{10,11... | collective-permute-start | bytes 774152 | tf_op jit(solution)/shard_map/mine1_y/ppermute | solution.py:208
  92.6 8.4 %collective-permute-start.26 = (bf16[72,1792]{1,0:T(8,128)(2,1)S(1)}, bf16[72,1792]{1,0:T(8,128)(2,1)S(1)}, u32[]{:S(2)}, u32[]{:S(2)}) collective-permute-start(bf16[72,1792]{1,0:T(8,128)(2,1)S(1)} %add_convert_fusion.3), channel_id=1, source_target_pairs={{0,2},{1,3},{2,0},{3,1},{4,6},{5,7},{6,4},{7,5},{8,10},{9,11},{10,... | collective-permute-start | bytes 774152 | tf_op jit(solution)/shard_map/mine1_z/ppermute | solution.py:208
  94.1 14.4 %collective-permute-start.29 = (bf16[72,1792]{1,0:T(8,128)(2,1)S(1)}, bf16[72,1792]{1,0:T(8,128)(2,1)S(1)}, u32[]{:S(2)}, u32[]{:S(2)}) collective-permute-start(bf16[72,1792]{1,0:T(8,128)(2,1)S(1)} %add_convert_fusion), channel_id=1, source_target_pairs={{0,12},{1,13},{2,14},{3,15},{4,8},{5,9},{6,10},{7,11},{8,4},{9,5},... | collective-permute-start | bytes 774152 | tf_op jit(solution)/shard_map/back1_/ppermute | solution.py:208
  94.2 8.3 %collective-permute-start.18 = (bf16[72,1792]{1,0:T(8,128)(2,1)S(1)}, bf16[72,1792]{1,0:T(8,128)(2,1)S(1)}, u32[]{:S(2)}, u32[]{:S(2)}) collective-permute-start(bf16[72,1792]{1,0:T(8,128)(2,1)S(1)} %add_convert_fusion.7), channel_id=1, source_target_pairs={{0,1},{1,0},{2,3},{3,2},{4,5},{5,4},{6,7},{7,6},{8,9},{9,8},{10,11... | collective-permute-start | bytes 774152 | tf_op jit(solution)/shard_map/mine0_y/ppermute | solution.py:208
  101.1 7.5 %collective-permute-start.27 = (bf16[72,1792]{1,0:T(8,128)(2,1)S(1)}, bf16[72,1792]{1,0:T(8,128)(2,1)S(1)}, u32[]{:S(2)}, u32[]{:S(2)}) collective-permute-start(bf16[72,1792]{1,0:T(8,128)(2,1)S(1)} %add_convert_fusion.2), channel_id=1, source_target_pairs={{0,8},{1,9},{2,10},{3,11},{4,12},{5,13},{6,14},{7,15},{8,0},{9,1},... | collective-permute-start | bytes 774152 | tf_op jit(solution)/shard_map/mine_core/ppermute | solution.py:208

commit v4 on v3

v4 whole, which is shorter than its diff:
```python
import jax
import jax.numpy as jnp
from jax import lax
from jax.experimental import pallas as pl
from jax.experimental.pallas import tpu as pltpu
from jax.sharding import PartitionSpec as P

TEAM = 4
CAP = 18
GSIZE = 32
STACK = 4
COST = 60

AFTER = {
    "load": ("own1",),
    "own_y0": ("own1",),
    "own_z0": ("own_z1",),
    "own_d0": ("own_z0",),
    "own_d1": ("own_y0",),
    "far0_d": ("far0_y",),
    "far0_y": ("load", "own_y1"),
    "far0_z": ("load", "own_z1"),
    "far1": ("far0", "load"),
    "far1_d": ("far0_d",),
    "far1_experts": ("own_experts",),
    "far1_y": ("own_d1",),
    "far1_z": ("load", "own_z1"),
    "own_experts": ("far0_experts",),
    "back0_y": ("back0_d",),
    "back1_y": ("back0_y",),
    "back1_z": ("back0_z",),
    "mine_d1": ("far1_d",),
    "mine_y0": ("back1_y",),
    "mine_y1": ("back1_y",),
    "mine_z0": ("back0_z",),
    "mine_z1": ("back0_z",),
}

route_scale = 2.5
VMEM = pl.BlockSpec(memory_space=pltpu.VMEM)
SMEM = pl.BlockSpec(memory_space=pltpu.SMEM)
HBM = pl.BlockSpec(memory_space=pltpu.HBM)


def dot(a, b):
    return jnp.dot(a, b, preferred_element_type=jnp.float32)


def params(mib):
    return pltpu.CompilerParams(vmem_limit_bytes=mib << 20)


def pieces_of(value, q):
    return value[q * CAP : (q + 1) * CAP]


def pack_kernel(flight_ref, ids_hbm, scores_hbm, tokens_hbm, *refs):
    tokens, ids_ref, scores_ref, sems = refs[-4:]
    outs, pick_ref, weight_ref = refs[:-6], refs[-6], refs[-5]
    experts = len(outs)
    width = outs[0].shape[1]
    copies = [
        pltpu.make_async_copy(
            tokens_hbm.at[:, pl.ds(q * width, width)], tokens.at[q], sems.at[q]
        )
        for q in range(STACK)
    ]
    small = [
        pltpu.make_async_copy(ids_hbm, ids_ref, sems.at[STACK]),
        pltpu.make_async_copy(scores_hbm, scores_ref, sems.at[STACK + 1]),
    ]
    for copy in small + copies:
        copy.start()
    for copy in small:
        copy.wait()
    ids = ids_ref[...]
    scores = scores_ref[...]
    count = ids.shape[1]
    earlier = lax.broadcasted_iota(jnp.int32, (count, count), 0) < lax.broadcasted_iota(
        jnp.int32, (count, count), 1
    )
    earlier = jnp.where(earlier, 1.0, 0.0).astype(jnp.bfloat16)
    slot = lax.broadcasted_iota(jnp.int32, (CAP, count), 0).astype(jnp.float32)
    hits = [jnp.where(ids == flight_ref[e], 1.0, 0.0) for e in range(experts)]
    rows = jnp.concatenate([jnp.sum(hit, axis=0, keepdims=True) for hit in hits], axis=0)
    ranks = dot(rows.astype(jnp.bfloat16), earlier)
    pick = jnp.concatenate(
        [
            jnp.where(slot == ranks[e : e + 1], rows[e : e + 1], 0.0)
            for e in range(experts)
        ],
        axis=0,
    )
    pick_ref[...] = pick.astype(jnp.bfloat16)
    gate_values = route_scale * scores / jnp.sum(scores, axis=0, keepdims=True)
    weight = jnp.sum(gate_values * sum(hits), axis=0, keepdims=True)
    weight_ref[...] = jnp.sum(pick * weight, axis=1, keepdims=True)
    pick = pick.astype(jnp.bfloat16)
    parts = []
    for q in range(STACK):
        copies[q].wait()
        parts.append(dot(pick, tokens[q]).astype(jnp.bfloat16))
    for e in range(experts):
        outs[e][...] = jnp.concatenate([p[e * CAP : (e + 1) * CAP] for p in parts], axis=0)


def load_kernel(gate_hbm, up_hbm, down_hbm, gate, up, down, sems):
    width = gate.shape[1]
    copies = []
    for q in range(STACK):
        span = pl.ds(q * width, width)
        copies += [
            pltpu.make_async_copy(gate_hbm.at[0, span], gate.at[q], sems.at[0, q]),
            pltpu.make_async_copy(up_hbm.at[0, span], up.at[q], sems.at[1, q]),
            pltpu.make_async_copy(down_hbm.at[0, :, span], down.at[q], sems.at[2, q]),
        ]
    for copy in copies:
        copy.start()
    for copy in copies:
        copy.wait()


def expert_kernel(gate, up, down, *refs):
    count = len(refs) // 2
    blocks, outs = refs[:count], refs[count:]
    values = [block[...] for block in blocks]
    gate_part = up_part = None
    for q in range(STACK):
        rows = jnp.concatenate([pieces_of(value, q) for value in values], axis=0)
        gate_term = dot(rows, gate[q])
        up_term = dot(rows, up[q])
        gate_part = gate_term if gate_part is None else gate_part + gate_term
        up_part = up_term if up_part is None else up_part + up_term
    hidden = gate_part / (1.0 + jnp.exp(-gate_part)) * up_part
    hidden = hidden.astype(jnp.bfloat16)
    parts = [dot(hidden, down[q]).astype(jnp.bfloat16) for q in range(STACK)]
    for b in range(count):
        outs[b][...] = jnp.concatenate([p[b * CAP : (b + 1) * CAP] for p in parts], axis=0)


def final_kernel(pick_ref, weight_ref, *refs):
    blocks, out_hbm, (out, sems) = refs[:-3], refs[-3], refs[-2:]
    width = blocks[0].shape[1]
    values = [block[...] for block in blocks]
    pick = pick_ref[...]
    copies = []
    for q in range(STACK):
        rows = jnp.concatenate([pieces_of(value, q) for value in values], axis=0)
        rows = (rows.astype(jnp.float32) * weight_ref[...]).astype(jnp.bfloat16)
        placed = lax.dot_general(
            pick, rows, (((0,), (0,)), ((), ())), preferred_element_type=jnp.float32
        )
        out[q] = placed.astype(jnp.bfloat16)
        copies.append(
            pltpu.make_async_copy(
                out.at[q], out_hbm.at[:, pl.ds(q * width, width)], sems.at[q]
            )
        )
        copies[q].start()
    for copy in copies:
        copy.wait()


def in_hbm(value):
    return pltpu.with_memory_space_constraint(value, pltpu.HBM)


def after(value, done):
    done = [d[0] if isinstance(d, (list, tuple)) else d for d in done]
    return lax.optimization_barrier((value, *done))[0] if done else value


def total(*terms):
    summed = terms[0].astype(jnp.float32)
    for term in terms[1:]:
        summed = summed + term.astype(jnp.float32)
    return summed.astype(jnp.bfloat16)


def local(tokens, expert_ids, route_scores, gate_weight, up_weight, down_weight):
    token_count, model_width = tokens.shape
    hidden_width = gate_weight.shape[2]
    nodes = lax.axis_size("node")
    places = lax.axis_size("local")
    teams = places // TEAM
    flight = nodes * teams
    node = lax.axis_index("node")
    team = lax.axis_index("local") // TEAM
    width = model_width // STACK
    block = jax.ShapeDtypeStruct((STACK * CAP, width), jnp.bfloat16)

    offsets = [(n, d) for n in range(nodes) for d in range(teams)]
    flight_ids = jnp.stack(
        [((node + n) % nodes * teams + (team + d) % teams) * GSIZE for n, d in offsets]
    ).astype(jnp.int32)
    packed = pl.pallas_call(
        pack_kernel,
        out_shape=[block] * flight
        + [
            jax.ShapeDtypeStruct((flight * CAP, token_count), jnp.bfloat16),
            jax.ShapeDtypeStruct((flight * CAP, 1), jnp.float32),
        ],
        in_specs=[SMEM] + [HBM] * 3,
        out_specs=[VMEM] * (flight + 2),
        scratch_shapes=[
            pltpu.VMEM((STACK, token_count, width), jnp.bfloat16),
            pltpu.VMEM(expert_ids.shape[::-1], jnp.int32),
            pltpu.VMEM(route_scores.shape[::-1], jnp.float32),
            pltpu.SemaphoreType.DMA((STACK + 2,)),
        ],
        compiler_params=params(20),
        name="pack",
    )(flight_ids, in_hbm(expert_ids.T), in_hbm(route_scores.T), in_hbm(tokens))
    pick, weight = packed[flight:]
    packed = dict(zip(offsets, packed))

    def load(gate):
        return pl.pallas_call(
            load_kernel,
            out_shape=[
                pltpu.VMEM((STACK, width, hidden_width), jnp.bfloat16),
                pltpu.VMEM((STACK, width, hidden_width), jnp.bfloat16),
                pltpu.VMEM((STACK, hidden_width, width), jnp.bfloat16),
            ],
            in_specs=[HBM] * 3,
            out_specs=[VMEM] * 3,
            scratch_shapes=[pltpu.SemaphoreType.DMA((3, STACK))],
            compiler_params=params(20),
            cost_estimate=cost(0),
            name="load",
        )(in_hbm(gate), in_hbm(up_weight), in_hbm(down_weight))

    def experts(*operands):
        blocks, weights = operands[:-1], operands[-1]
        return pl.pallas_call(
            expert_kernel,
            out_shape=[block] * len(blocks),
            in_specs=[VMEM] * (3 + len(blocks)),
            out_specs=[VMEM] * len(blocks),
            compiler_params=params(20),
            cost_estimate=cost(len(blocks)),
            name="experts",
        )(*weights, *blocks)

    def cost(blocks):
        return pl.CostEstimate(
            flops=COST * blocks * CAP * model_width * hidden_width,
            bytes_accessed=COST * model_width * hidden_width,
            transcendentals=0,
        )

    def send(value, n, d, flip):
        pairs = [
            (
                i * places + j,
                (i + n) % nodes * places + ((j + d * TEAM) % places ^ flip),
            )
            for i in range(nodes)
            for j in range(places)
        ]
        return lax.ppermute(value, ("node", "local"), pairs)

    def along_y(value):
        return send(value, 0, 0, 1)

    def along_z(value):
        return send(value, 0, 0, 2)

    fars = [(n, d) for d in range(1, teams) for n in range(nodes)]
    steps = {"load": (load, ("gate",))}
    values = {"gate": gate_weight}
    for n in range(nodes):
        at = str(n)
        values["row_own" + at] = packed[n, 0]
        steps["own" + at] = (
            (lambda v, n=n: send(v, n, 0, 0)) if n else (lambda v: v),
            ("row_own" + at,),
        )
        steps["own_y" + at] = (along_y, ("own" + at,))
        steps["own_z" + at] = (along_z, ("own" + at,))
        steps["own_d" + at] = (along_y, ("own_z" + at,)) if n % 2 else (along_z, ("own_y" + at,))
    for i, (n, d) in enumerate(fars):
        far = "far%d" % i
        values["row_" + far] = packed[n, d]
        steps[far] = (lambda v, n=n, d=d: send(v, n, d, 0), ("row_" + far,))
        steps[far + "_y"] = (along_y, (far,))
        steps[far + "_z"] = (along_z, (far,))
        steps[far + "_d"] = (along_y, (far + "_z",))
    sides = ("", "_y", "_z", "_d")
    steps["own_experts"] = (
        experts,
        (*[v + str(n) for n in range(nodes) for v in ("own", "own_y", "own_z", "own_d")], "load"),
    )
    for i, (n, d) in enumerate(fars):
        far, back = "far%d" % i, "back%d" % i
        steps[far + "_experts"] = (experts, (*[far + v for v in sides], "load"))
        for j, v in enumerate(sides):
            steps[far + "_out" + v] = (lambda out, j=j: out[j], (far + "_experts",))
        steps[back + "_d"] = (along_y, (far + "_out_d",))
        steps[back + "_y"] = (along_y, (far + "_out_y",))
        steps[back + "_zsum"] = (total, (far + "_out_z", back + "_d"))
        steps[back + "_z"] = (along_z, (back + "_zsum",))
        steps[back + "_sum"] = (total, (far + "_out", back + "_y", back + "_z"))
        steps[back] = (lambda v, n=n, d=d: send(v, nodes - n, teams - d, 0), (back + "_sum",))
    for n in range(nodes):
        at = str(n)
        for j, v in enumerate(sides):
            steps["own_out" + v + at] = (lambda out, j=n * TEAM + j: out[j], ("own_experts",))
        first, second = ("z", "y") if n % 2 else ("y", "z")
        steps["mine_d" + at] = (along_y if n % 2 else along_z, ("own_out_d" + at,))
        steps["mine_sum" + at] = (total, ("own_out_" + first + at, "mine_d" + at))
        along = {"y": along_y, "z": along_z}
        steps["mine_" + first + at] = (along[first], ("mine_sum" + at,))
        steps["mine_" + second + at] = (along[second], ("own_out_" + second + at,))
        steps["mine" + at] = (total, ("own_out" + at, "mine_y" + at, "mine_z" + at))
        steps["home" + at] = (
            (lambda v, n=n: send(v, nodes - n, 0, 0)) if n else (lambda v: v),
            ("mine" + at,),
        )

    def value(name):
        if name not in values:
            run, takes = steps[name]
            first, *others = [value(take) for take in takes]
            done = [value(other) for other in AFTER.get(name, ()) if other in steps]
            with jax.named_scope(name):
                values[name] = run(after(first, done), *others)
        return values[name]

    returned = [
        value("home%d" % n) if d == 0 else value("back%d" % fars.index((n, d)))
        for n, d in offsets
    ]
    return pl.pallas_call(
        final_kernel,
        out_shape=jax.ShapeDtypeStruct(tokens.shape, jnp.bfloat16),
        in_specs=[VMEM] * (2 + flight),
        out_specs=pl.BlockSpec(memory_space=pltpu.HBM),
        scratch_shapes=[
            pltpu.VMEM((STACK, token_count, width), jnp.bfloat16),
            pltpu.SemaphoreType.DMA((STACK,)),
        ],
        compiler_params=params(20),
        name="combine",
    )(pick, weight, *returned)


def solution(mesh):
    in_specs = (
        P(("rep", "node", "local"), None),
        P(("rep", "node", "local"), None),
        P(("rep", "node", "local"), None),
        P(("node", "local"), None, None),
        P(("node", "local"), None, None),
        P(("node", "local"), None, None),
    )
    out_specs = P(("rep", "node", "local"), None)
    return jax.shard_map(local, mesh=mesh, in_specs=in_specs, out_specs=out_specs, check_vma=False)
```

time: 111 us -> 102 us (0.919)
  waiting for transfers between devices: 54.2 us -> 47.2 us
  local copies, waits for them, and re-layouts: 1.39 us -> 0 us
    ppermute x30, waiting for transfers between devices: 54.2 us -> 47.2 us  [send(): return lax.ppermute(value, ('node', 'local'), pairs)]
    unnamed x4 -> x0, local copies, waits for them, and re-layouts: 1.39 us -> none
  transfers between devices with their start and end apart: 30 -> 30, of which waited for: 17 -> 17; matrix products, arithmetic and copies ran while one was open for 1% -> 1% of each run, Pallas kernels for 17% -> 19%
where the time goes in v4:
time: 102 us
  waiting for transfers between devices  47.2 us (46%)
  starting transfers between devices  30.7 us (30%)
  Pallas kernels  23.3 us (23%)
    ppermute x30, waiting for transfers between devices, send(): return lax.ppermute(value, ('node', 'local'), pairs)  47.2 us
    ppermute x30, starting transfers between devices, send(): return lax.ppermute(value, ('node', 'local'), pairs)  30.7 us
    pallas_call x3, Pallas kernels, experts(): pl.pallas_call(expert_kernel, out_shape=[block] * len(blocks), in_specs=[...  11.6 us
    pallas_call x1, Pallas kernels, load(): pl.pallas_call(load_kernel, out_shape=[pltpu.VMEM((STACK, width, hidden_w...  7.44 us
    pallas_call x1, Pallas kernels, local(): pl.pallas_call(pack_kernel, out_shape=[block] * flight + [jax.ShapeDtypeS...  2.61 us
  transfers between devices with their start and end apart: 30, of which 17 were waited for; matrix products, arithmetic and copies ran while one was open for 1% of the time, Pallas kernels for 19%

profile of v4, /device:TPU:0, one launch (start us, length us, event | category | flops | bytes accessed | tf_op | source)
XLA Modules:
  0.0 102.1 jit_solution(17011594770620511416)
XLA Ops:
  0.1 2.6 %pack.1 = (bf16[72,1792]{1,0:T(8,128)(2,1)S(1)}, bf16[72,1792]{1,0:T(8,128)(2,1)S(1)}, bf16[72,1792]{1,0:T(8,128)(2,1)S(1)}, bf16[72,1792]{1,0:T(8,128)(2,1)S(1)...) custom-call(s32[4]{0:T(128)S(1)} %pad_add_fusion.flight_ref, s32[8,144]{1,0:T(8,128)} %bitcast.6, f32[8,144]{1,0:T(8,128)} %bitcast.7, ...), custom_call_target="tpu_custom_call" | custom-call | tf_op jit(solution)/shard_map/pack/pallas_call | solution.py:196
  2.7 0.5 collective-permute-start
  3.2 3.7 %collective-permute-start.1 = (bf16[72,1792]{1,0:T(8,128)(2,1)S(1)}, bf16[72,1792]{1,0:T(8,128)(2,1)S(1)}, u32[]{:S(2)}, u32[]{:S(2)}) collective-permute-start(bf16[72,1792]{1,0:T(8,128)(2,1)S(1)} %get-tuple-element.60), channel_id=1, source_target_pairs={{0,4},{1,5},{2,6},{3,7},{4,0},{5,1},{6,2},{7,3},{8,12},{9,13},{10,... | collective-permute-start | bytes 774152 | tf_op jit(solution)/shard_map/far0/ppermute | solution.py:261
  6.9 1.6 %collective-permute-start.4 = (bf16[72,1792]{1,0:T(8,128)(2,1)S(1)}, bf16[72,1792]{1,0:T(8,128)(2,1)S(1)}, u32[]{:S(2)}, u32[]{:S(2)}) collective-permute-start(bf16[72,1792]{1,0:T(8,128)(2,1)S(1)} %collective-permute-done.refs_4_), channel_id=1, source_target_pairs={{0,2},{1,3},{2,0},{3,1},{4,6},{5,7},{6,4},{7,5},{8,10},{9,11},{10,... | collective-permute-start | bytes 774152 | tf_op jit(solution)/shard_map/own_z1/ppermute | solution.py:261
  8.5 1.5 %collective-permute-start.2 = (bf16[72,1792]{1,0:T(8,128)(2,1)S(1)}, bf16[72,1792]{1,0:T(8,128)(2,1)S(1)}, u32[]{:S(2)}, u32[]{:S(2)}) collective-permute-start(bf16[72,1792]{1,0:T(8,128)(2,1)S(1)} %collective-permute-done.refs_4_), channel_id=1, source_target_pairs={{0,1},{1,0},{2,3},{3,2},{4,5},{5,4},{6,7},{7,6},{8,9},{9,8},{10,11... | collective-permute-start | bytes 774152 | tf_op jit(solution)/shard_map/own_y1/ppermute | solution.py:261
  10.0 0.5 collective-permute-start.7
  10.5 7.4 %load.1 = (bf16[4,1792,512]{2,1,0:T(8,128)(2,1)S(1)}, bf16[4,1792,512]{2,1,0:T(8,128)(2,1)S(1)}, bf16[4,512,1792]{2,1,0:T(8,128)(2,1)S(1)}) custom-call(bf16[1,7168,512]{2,1,0:T(8,128)(2,1)} %gate_hbm, bf16[1,7168,512]{2,1,0:T(8,128)(2,1)} %up_hbm.1, bf16[1,512,7168]{2,1,0:T(8,128)(2,1)} %down_hbm.1), custom_call_target="tpu_custom_call" | custom-call | bytes 220200960 | tf_op jit(solution)/shard_map/load/load/pallas_call | solution.py:218
  17.9 1.4 %collective-permute-done.1.refs_0_ = bf16[72,1792]{1,0:T(8,128)(2,1)S(1)} collective-permute-done((bf16[72,1792]{1,0:T(8,128)(2,1)S(1)}, bf16[72,1792]{1,0:T(8,128)(2,1)S(1)}, u32[]{:S(2)}, u32[]{:S(2)}) %collective-permute-start.1) | collective-permute-done | bytes 258080 | tf_op jit(solution)/shard_map/far0/ppermute | solution.py:261
  19.3 0.2 collective-permute-done.4.refs_6_
  19.5 1.6 %collective-permute-start.3 = (bf16[72,1792]{1,0:T(8,128)(2,1)S(1)}, bf16[72,1792]{1,0:T(8,128)(2,1)S(1)}, u32[]{:S(2)}, u32[]{:S(2)}) collective-permute-start(bf16[72,1792]{1,0:T(8,128)(2,1)S(1)} %collective-permute-done.1.refs_0_), channel_id=1, source_target_pairs={{0,1},{1,0},{2,3},{3,2},{4,5},{5,4},{6,7},{7,6},{8,9},{9,8},{10,11... | collective-permute-start | bytes 774152 | tf_op jit(solution)/shard_map/far0_y/ppermute | solution.py:261
  21.1 1.4 %collective-permute-start.5 = (bf16[72,1792]{1,0:T(8,128)(2,1)S(1)}, bf16[72,1792]{1,0:T(8,128)(2,1)S(1)}, u32[]{:S(2)}, u32[]{:S(2)}) collective-permute-start(bf16[72,1792]{1,0:T(8,128)(2,1)S(1)} %collective-permute-done.1.refs_0_), channel_id=1, source_target_pairs={{0,2},{1,3},{2,0},{3,1},{4,6},{5,7},{6,4},{7,5},{8,10},{9,11},{10,... | collective-permute-start | bytes 774152 | tf_op jit(solution)/shard_map/far0_z/ppermute | solution.py:261
  22.5 1.5 %collective-permute-start.12 = (bf16[72,1792]{1,0:T(8,128)(2,1)S(1)}, bf16[72,1792]{1,0:T(8,128)(2,1)S(1)}, u32[]{:S(2)}, u32[]{:S(2)}) collective-permute-start(bf16[72,1792]{1,0:T(8,128)(2,1)S(1)} %get-tuple-element.74), channel_id=1, source_target_pairs={{0,12},{1,13},{2,14},{3,15},{4,8},{5,9},{6,10},{7,11},{8,4},{9,5},... | collective-permute-start | bytes 774152 | tf_op jit(solution)/shard_map/far1/ppermute | solution.py:261
  24.0 0.3 collective-permute-start.8
  24.3 0.5 collective-permute-start.10
  24.8 2.7 %collective-permute-done.3.refs_1_ = bf16[72,1792]{1,0:T(8,128)(2,1)S(1)} collective-permute-done((bf16[72,1792]{1,0:T(8,128)(2,1)S(1)}, bf16[72,1792]{1,0:T(8,128)(2,1)S(1)}, u32[]{:S(2)}, u32[]{:S(2)}) %collective-permute-start.3) | collective-permute-done | bytes 258080 | tf_op jit(solution)/shard_map/far0_y/ppermute | solution.py:261
  27.5 6.7 %collective-permute-done.5.refs_2_ = bf16[72,1792]{1,0:T(8,128)(2,1)S(1)} collective-permute-done((bf16[72,1792]{1,0:T(8,128)(2,1)S(1)}, bf16[72,1792]{1,0:T(8,128)(2,1)S(1)}, u32[]{:S(2)}, u32[]{:S(2)}) %collective-permute-start.5) | collective-permute-done | bytes 258080 | tf_op jit(solution)/shard_map/far0_z/ppermute | solution.py:261
  34.3 0.6 collective-permute-start.6
  34.8 2.3 %collective-permute-done.12.refs_0_ = bf16[72,1792]{1,0:T(8,128)(2,1)S(1)} collective-permute-done((bf16[72,1792]{1,0:T(8,128)(2,1)S(1)}, bf16[72,1792]{1,0:T(8,128)(2,1)S(1)}, u32[]{:S(2)}, u32[]{:S(2)}) %collective-permute-start.12) | collective-permute-done | bytes 258080 | tf_op jit(solution)/shard_map/far1/ppermute | solution.py:261
  37.2 2.3 %collective-permute-done.8.refs_2_ = bf16[72,1792]{1,0:T(8,128)(2,1)S(1)} collective-permute-done((bf16[72,1792]{1,0:T(8,128)(2,1)S(1)}, bf16[72,1792]{1,0:T(8,128)(2,1)S(1)}, u32[]{:S(2)}, u32[]{:S(2)}) %collective-permute-start.8) | collective-permute-done | bytes 258080 | tf_op jit(solution)/shard_map/own_z0/ppermute | solution.py:261
  39.4 2.5 %collective-permute-start.9 = (bf16[72,1792]{1,0:T(8,128)(2,1)S(1)}, bf16[72,1792]{1,0:T(8,128)(2,1)S(1)}, u32[]{:S(2)}, u32[]{:S(2)}) collective-permute-start(bf16[72,1792]{1,0:T(8,128)(2,1)S(1)} %collective-permute-done.7.refs_1_), channel_id=1, source_target_pairs={{0,2},{1,3},{2,0},{3,1},{4,6},{5,7},{6,4},{7,5},{8,10},{9,11},{10,... | collective-permute-start | bytes 774152 | tf_op jit(solution)/shard_map/own_d0/ppermute | solution.py:261
  41.9 0.5 collective-permute-start.13
  42.4 4.0 %experts.3 = (bf16[72,1792]{1,0:T(8,128)(2,1)S(1)}, bf16[72,1792]{1,0:T(8,128)(2,1)S(1)}, bf16[72,1792]{1,0:T(8,128)(2,1)S(1)}, bf16[72,1792]{1,0:T(8,128)(2,1)S(1)}) custom-call(bf16[4,1792,512]{2,1,0:T(8,128)(2,1)S(1)} %get-tuple-element.56.gate, bf16[4,1792,512]{2,1,0:T(8,128)(2,1)S(1)} %get-tuple-element.57.up, ...), custom_call_target="tpu_custom_call" | custom-call | flops 15854469120 | bytes 220200960 | tf_op jit(solution)/shard_map/far0_experts/experts/pallas_call | solution.py:235
  46.4 1.6 %collective-permute-start.16 = (bf16[72,1792]{1,0:T(8,128)(2,1)S(1)}, bf16[72,1792]{1,0:T(8,128)(2,1)S(1)}, u32[]{:S(2)}, u32[]{:S(2)}) collective-permute-start(bf16[72,1792]{1,0:T(8,128)(2,1)S(1)} %get-tuple-element.81), channel_id=1, source_target_pairs={{0,1},{1,0},{2,3},{3,2},{4,5},{5,4},{6,7},{7,6},{8,9},{9,8},{10,11... | collective-permute-start | bytes 774152 | tf_op jit(solution)/shard_map/back0_d/ppermute | solution.py:261
  48.0 0.5 collective-permute-start.15
  48.5 2.6 %collective-permute-done.9.refs_3_ = bf16[72,1792]{1,0:T(8,128)(2,1)S(1)} collective-permute-done((bf16[72,1792]{1,0:T(8,128)(2,1)S(1)}, bf16[72,1792]{1,0:T(8,128)(2,1)S(1)}, u32[]{:S(2)}, u32[]{:S(2)}) %collective-permute-start.9) | collective-permute-done | bytes 258080 | tf_op jit(solution)/shard_map/own_d0/ppermute | solution.py:261
  51.1 3.6 %experts.4 = (bf16[72,1792]{1,0:T(8,128)(2,1)S(1)}, bf16[72,1792]{1,0:T(8,128)(2,1)S(1)}, bf16[72,1792]{1,0:T(8,128)(2,1)S(1)}, bf16[72,1792]{1,0:T(8,128)(2,1)S...) custom-call(bf16[4,1792,512]{2,1,0:T(8,128)(2,1)S(1)} %get-tuple-ele, ...), custom_call_target="tpu_custom_call" | custom-call | flops 31708938240 | bytes 220200960 | tf_op jit(solution)/shard_map/own_experts/experts/pallas_call | solution.py:235
  54.7 1.2 %collective-permute-start.11 = (bf16[72,1792]{1,0:T(8,128)(2,1)S(1)}, bf16[72,1792]{1,0:T(8,128)(2,1)S(1)}, u32[]{:S(2)}, u32[]{:S(2)}) collective-permute-start(bf16[72,1792]{1,0:T(8,128)(2,1)S(1)} %get-tuple-element.72), channel_id=1, source_target_pairs={{0,2},{1,3},{2,0},{3,1},{4,6},{5,7},{6,4},{7,5},{8,10},{9,11},{10,... | collective-permute-start | bytes 774152 | tf_op jit(solution)/shard_map/mine_d0/ppermute | solution.py:261
  55.9 1.2 %collective-permute-start.17 = (bf16[72,1792]{1,0:T(8,128)(2,1)S(1)}, bf16[72,1792]{1,0:T(8,128)(2,1)S(1)}, u32[]{:S(2)}, u32[]{:S(2)}) collective-permute-start(bf16[72,1792]{1,0:T(8,128)(2,1)S(1)} %get-tuple-element.82), channel_id=1, source_target_pairs={{0,1},{1,0},{2,3},{3,2},{4,5},{5,4},{6,7},{7,6},{8,9},{9,8},{10,11... | collective-permute-start | bytes 774152 | tf_op jit(solution)/shard_map/back0_y/ppermute | solution.py:261
  57.1 0.3 collective-permute-start.20
  57.4 3.6 %collective-permute-done.15.refs_3_ = bf16[72,1792]{1,0:T(8,128)(2,1)S(1)} collective-permute-done((bf16[72,1792]{1,0:T(8,128)(2,1)S(1)}, bf16[72,1792]{1,0:T(8,128)(2,1)S(1)}, u32[]{:S(2)}, u32[]{:S(2)}) %collective-permute-start.15) | collective-permute-done | bytes 258080 | tf_op jit(solution)/shard_map/far1_d/ppermute | solution.py:261
  61.0 4.0 %experts.5 = (bf16[72,1792]{1,0:T(8,128)(2,1)S(1)}, bf16[72,1792]{1,0:T(8,128)(2,1)S(1)}, bf16[72,1792]{1,0:T(8,128)(2,1)S(1)}, bf16[72,1792]{1,0:T(8,128)(2,1)S(1)}) custom-call(bf16[4,1792,512]{2,1,0:T(8,128)(2,1)S(1)} %get-tuple-element.56.gate, bf16[4,1792,512]{2,1,0:T(8,128)(2,1)S(1)} %get-tuple-element.57.up, ...), custom_call_target="tpu_custom_call" | custom-call | flops 15854469120 | bytes 220200960 | tf_op jit(solution)/shard_map/far1_experts/experts/pallas_call | solution.py:235
  65.0 0.6 collective-permute-start.27
  65.5 1.5 %collective-permute-start.24 = (bf16[72,1792]{1,0:T(8,128)(2,1)S(1)}, bf16[72,1792]{1,0:T(8,128)(2,1)S(1)}, u32[]{:S(2)}, u32[]{:S(2)}) collective-permute-start(bf16[72,1792]{1,0:T(8,128)(2,1)S(1)} %get-tuple-element.93), channel_id=1, source_target_pairs={{0,1},{1,0},{2,3},{3,2},{4,5},{5,4},{6,7},{7,6},{8,9},{9,8},{10,11... | collective-permute-start | bytes 774152 | tf_op jit(solution)/shard_map/mine_d1/ppermute | solution.py:261
  67.2 0.8 collective-permute-done.20
  68.0 3.8 %collective-permute-start.22 = (bf16[72,1792]{1,0:T(8,128)(2,1)S(1)}, bf16[72,1792]{1,0:T(8,128)(2,1)S(1)}, u32[]{:S(2)}, u32[]{:S(2)}) collective-permute-start(bf16[72,1792]{1,0:T(8,128)(2,1)S(1)} %add_convert_fusion.4), channel_id=1, source_target_pairs={{0,4},{1,5},{2,6},{3,7},{4,0},{5,1},{6,2},{7,3},{8,12},{9,13},{10,... | collective-permute-start | bytes 774152 | tf_op jit(solution)/shard_map/back0/ppermute | solution.py:261
  71.8 0.6 collective-permute-start.18
  72.4 1.8 %collective-permute-done.27 = bf16[72,1792]{1,0:T(8,128)(2,1)S(1)} collective-permute-done((bf16[72,1792]{1,0:T(8,128)(2,1)S(1)}, bf16[72,1792]{1,0:T(8,128)(2,1)S(1)}, u32[]{:S(2)}, u32[]{:S(2)}) %collective-permute-start.27) | collective-permute-done | bytes 258080 | tf_op jit(solution)/shard_map/back1_d/ppermute | solution.py:261
  74.4 4.3 %collective-permute-done.24 = bf16[72,1792]{1,0:T(8,128)(2,1)S(1)} collective-permute-done((bf16[72,1792]{1,0:T(8,128)(2,1)S(1)}, bf16[72,1792]{1,0:T(8,128)(2,1)S(1)}, u32[]{:S(2)}, u32[]{:S(2)}) %collective-permute-start.24) | collective-permute-done | bytes 258080 | tf_op jit(solution)/shard_map/mine_d1/ppermute | solution.py:261
  78.8 2.0 %collective-permute-start.21 = (bf16[72,1792]{1,0:T(8,128)(2,1)S(1)}, bf16[72,1792]{1,0:T(8,128)(2,1)S(1)}, u32[]{:S(2)}, u32[]{:S(2)}) collective-permute-start(bf16[72,1792]{1,0:T(8,128)(2,1)S(1)} %get-tuple-element.87), channel_id=1, source_target_pairs={{0,2},{1,3},{2,0},{3,1},{4,6},{5,7},{6,4},{7,5},{8,10},{9,11},{10,... | collective-permute-start | bytes 774152 | tf_op jit(solution)/shard_map/mine_z0/ppermute | solution.py:261
  80.8 1.7 %collective-permute-done.18 = bf16[72,1792]{1,0:T(8,128)(2,1)S(1)} collective-permute-done((bf16[72,1792]{1,0:T(8,128)(2,1)S(1)}, bf16[72,1792]{1,0:T(8,128)(2,1)S(1)}, u32[]{:S(2)}, u32[]{:S(2)}) %collective-permute-start.18) | collective-permute-done | bytes 258080 | tf_op jit(solution)/shard_map/back1_y/ppermute | solution.py:261
  82.5 0.5 collective-permute-start.23
  83.0 3.5 %collective-permute-done.28 = bf16[72,1792]{1,0:T(8,128)(2,1)S(1)} collective-permute-done((bf16[72,1792]{1,0:T(8,128)(2,1)S(1)}, bf16[72,1792]{1,0:T(8,128)(2,1)S(1)}, u32[]{:S(2)}, u32[]{:S(2)}) %collective-permute-start.28) | collective-permute-done | bytes 258080 | tf_op jit(solution)/shard_map/back1_z/ppermute | solution.py:261
  86.7 5.7 %collective-permute-done.25 = bf16[72,1792]{1,0:T(8,128)(2,1)S(1)} collective-permute-done((bf16[72,1792]{1,0:T(8,128)(2,1)S(1)}, bf16[72,1792]{1,0:T(8,128)(2,1)S(1)}, u32[]{:S(2)}, u32[]{:S(2)}) %collective-permute-start.25) | collective-permute-done | bytes 258080 | tf_op jit(solution)/shard_map/mine_z1/ppermute | solution.py:261
  92.4 0.1 add_convert_fusion.2
  92.6 4.0 %collective-permute-done.21 = bf16[72,1792]{1,0:T(8,128)(2,1)S(1)} collective-permute-done((bf16[72,1792]{1,0:T(8,128)(2,1)S(1)}, bf16[72,1792]{1,0:T(8,128)(2,1)S(1)}, u32[]{:S(2)}, u32[]{:S(2)}) %collective-permute-start.21) | collective-permute-done | bytes 258080 | tf_op jit(solution)/shard_map/mine_z0/ppermute | solution.py:261
  96.6 2.1 %collective-permute-done.19 = bf16[72,1792]{1,0:T(8,128)(2,1)S(1)} collective-permute-done((bf16[72,1792]{1,0:T(8,128)(2,1)S(1)}, bf16[72,1792]{1,0:T(8,128)(2,1)S(1)}, u32[]{:S(2)}, u32[]{:S(2)}) %collective-permute-start.19) | collective-permute-done | bytes 258080 | tf_op jit(solution)/shard_map/mine_y0/ppermute | solution.py:261
  98.8 1.5 %collective-permute-done.29.refs_3_ = bf16[72,1792]{1,0:T(8,128)(2,1)S(1)} collective-permute-done((bf16[72,1792]{1,0:T(8,128)(2,1)S(1)}, bf16[72,1792]{1,0:T(8,128)(2,1)S(1)}, u32[]{:S(2)}, u32[]{:S(2)}) %collective-permute-start.29) | collective-permute-done | bytes 258080 | tf_op jit(solution)/shard_map/back1/ppermute | solution.py:261
  100.4 1.7 %combine.1 = bf16[144,7168]{1,0:T(8,128)(2,1)} custom-call(bf16[72,144]{1,0:T(8,128)(2,1)S(1)} %get-tuple-element.52.pick_ref, f32[72,1]{1,0:T(8,128)S(1)} %get-tuple-element.53.weight_ref, bf16[72,1792]{1,0:T(8,128)(2,1)S(1)} %add_convert_fusion.5.refs_0_, bf16[72,1792]{1,0:T(8,128)(2,1)S(1)} %collective-permute-done.22.refs_1_, ...), custom_call_target="tpu_custom_call" | custom-call | tf_op jit(solution)/shard_map/combine/pallas_call | solution.py:334
  (27 shorter events, 1.0 us)
Async XLA Ops:
  2.7 4.2 %collective-permute-start = (bf16[72,1792]{1,0:T(8,128)(2,1)S(1)}, bf16[72,1792]{1,0:T(8,128)(2,1)S(1)}, u32[]{:S(2)}, u32[]{:S(2)}) collective-permute-start(bf16[72,1792]{1,0:T(8,128)(2,1)S(1)} %get-tuple-element.54), channel_id=1, source_target_pairs={{0,8},{1,9},{2,10},{3,11},{4,12},{5,13},{6,14},{7,15},{8,0},{9,1},... | collective-permute-start | bytes 774152 | tf_op jit(solution)/shard_map/own1/ppermute | solution.py:261
  3.2 16.1 %collective-permute-start.1 = (bf16[72,1792]{1,0:T(8,128)(2,1)S(1)}, bf16[72,1792]{1,0:T(8,128)(2,1)S(1)}, u32[]{:S(2)}, u32[]{:S(2)}) collective-permute-start(bf16[72,1792]{1,0:T(8,128)(2,1)S(1)} %get-tuple-element.60), channel_id=1, source_target_pairs={{0,4},{1,5},{2,6},{3,7},{4,0},{5,1},{6,2},{7,3},{8,12},{9,13},{10,... | collective-permute-start | bytes 774152 | tf_op jit(solution)/shard_map/far0/ppermute | solution.py:261
  6.9 12.6 %collective-permute-start.4 = (bf16[72,1792]{1,0:T(8,128)(2,1)S(1)}, bf16[72,1792]{1,0:T(8,128)(2,1)S(1)}, u32[]{:S(2)}, u32[]{:S(2)}) collective-permute-start(bf16[72,1792]{1,0:T(8,128)(2,1)S(1)} %collective-permute-done.refs_4_), channel_id=1, source_target_pairs={{0,2},{1,3},{2,0},{3,1},{4,6},{5,7},{6,4},{7,5},{8,10},{9,11},{10,... | collective-permute-start | bytes 774152 | tf_op jit(solution)/shard_map/own_z1/ppermute | solution.py:261
  8.5 11.1 %collective-permute-start.2 = (bf16[72,1792]{1,0:T(8,128)(2,1)S(1)}, bf16[72,1792]{1,0:T(8,128)(2,1)S(1)}, u32[]{:S(2)}, u32[]{:S(2)}) collective-permute-start(bf16[72,1792]{1,0:T(8,128)(2,1)S(1)} %collective-permute-done.refs_4_), channel_id=1, source_target_pairs={{0,1},{1,0},{2,3},{3,2},{4,5},{5,4},{6,7},{7,6},{8,9},{9,8},{10,11... | collective-permute-start | bytes 774152 | tf_op jit(solution)/shard_map/own_y1/ppermute | solution.py:261
  10.0 14.3 %collective-permute-start.7 = (bf16[72,1792]{1,0:T(8,128)(2,1)S(1)}, bf16[72,1792]{1,0:T(8,128)(2,1)S(1)}, u32[]{:S(2)}, u32[]{:S(2)}) collective-permute-start(bf16[72,1792]{1,0:T(8,128)(2,1)S(1)} %get-tuple-element.67.refs_0_), channel_id=1, source_target_pairs={{0,1},{1,0},{2,3},{3,2},{4,5},{5,4},{6,7},{7,6},{8,9},{9,8},{10,11... | collective-permute-start | bytes 774152 | tf_op jit(solution)/shard_map/own_y0/ppermute | solution.py:261
  19.5 8.0 %collective-permute-start.3 = (bf16[72,1792]{1,0:T(8,128)(2,1)S(1)}, bf16[72,1792]{1,0:T(8,128)(2,1)S(1)}, u32[]{:S(2)}, u32[]{:S(2)}) collective-permute-start(bf16[72,1792]{1,0:T(8,128)(2,1)S(1)} %collective-permute-done.1.refs_0_), channel_id=1, source_target_pairs={{0,1},{1,0},{2,3},{3,2},{4,5},{5,4},{6,7},{7,6},{8,9},{9,8},{10,11... | collective-permute-start | bytes 774152 | tf_op jit(solution)/shard_map/far0_y/ppermute | solution.py:261
  21.1 13.2 %collective-permute-start.5 = (bf16[72,1792]{1,0:T(8,128)(2,1)S(1)}, bf16[72,1792]{1,0:T(8,128)(2,1)S(1)}, u32[]{:S(2)}, u32[]{:S(2)}) collective-permute-start(bf16[72,1792]{1,0:T(8,128)(2,1)S(1)} %collective-permute-done.1.refs_0_), channel_id=1, source_target_pairs={{0,2},{1,3},{2,0},{3,1},{4,6},{5,7},{6,4},{7,5},{8,10},{9,11},{10,... | collective-permute-start | bytes 774152 | tf_op jit(solution)/shard_map/far0_z/ppermute | solution.py:261
  22.5 14.6 %collective-permute-start.12 = (bf16[72,1792]{1,0:T(8,128)(2,1)S(1)}, bf16[72,1792]{1,0:T(8,128)(2,1)S(1)}, u32[]{:S(2)}, u32[]{:S(2)}) collective-permute-start(bf16[72,1792]{1,0:T(8,128)(2,1)S(1)} %get-tuple-element.74), channel_id=1, source_target_pairs={{0,12},{1,13},{2,14},{3,15},{4,8},{5,9},{6,10},{7,11},{8,4},{9,5},... | collective-permute-start | bytes 774152 | tf_op jit(solution)/shard_map/far1/ppermute | solution.py:261
  24.0 15.4 %collective-permute-start.8 = (bf16[72,1792]{1,0:T(8,128)(2,1)S(1)}, bf16[72,1792]{1,0:T(8,128)(2,1)S(1)}, u32[]{:S(2)}, u32[]{:S(2)}) collective-permute-start(bf16[72,1792]{1,0:T(8,128)(2,1)S(1)} %get-tuple-element.67.refs_0_), channel_id=1, source_target_pairs={{0,2},{1,3},{2,0},{3,1},{4,6},{5,7},{6,4},{7,5},{8,10},{9,11},{10,... | collective-permute-start | bytes 774152 | tf_op jit(solution)/shard_map/own_z0/ppermute | solution.py:261
  24.3 17.6 %collective-permute-start.10 = (bf16[72,1792]{1,0:T(8,128)(2,1)S(1)}, bf16[72,1792]{1,0:T(8,128)(2,1)S(1)}, u32[]{:S(2)}, u32[]{:S(2)}) collective-permute-start(bf16[72,1792]{1,0:T(8,128)(2,1)S(1)} %collective-permute-done.4.refs_6_), channel_id=1, source_target_pairs={{0,1},{1,0},{2,3},{3,2},{4,5},{5,4},{6,7},{7,6},{8,9},{9,8},{10,11... | collective-permute-start | bytes 774152 | tf_op jit(solution)/shard_map/own_d1/ppermute | solution.py:261
  34.3 8.1 %collective-permute-start.6 = (bf16[72,1792]{1,0:T(8,128)(2,1)S(1)}, bf16[72,1792]{1,0:T(8,128)(2,1)S(1)}, u32[]{:S(2)}, u32[]{:S(2)}) collective-permute-start(bf16[72,1792]{1,0:T(8,128)(2,1)S(1)} %collective-permute-done.5.refs_2_), channel_id=1, source_target_pairs={{0,1},{1,0},{2,3},{3,2},{4,5},{5,4},{6,7},{7,6},{8,9},{9,8},{10,11... | collective-permute-start | bytes 774152 | tf_op jit(solution)/shard_map/far0_d/ppermute | solution.py:261
  37.2 10.8 %collective-permute-start.14 = (bf16[72,1792]{1,0:T(8,128)(2,1)S(1)}, bf16[72,1792]{1,0:T(8,128)(2,1)S(1)}, u32[]{:S(2)}, u32[]{:S(2)}) collective-permute-start(bf16[72,1792]{1,0:T(8,128)(2,1)S(1)} %collective-permute-done.12.refs_0_), channel_id=1, source_target_pairs={{0,2},{1,3},{2,0},{3,1},{4,6},{5,7},{6,4},{7,5},{8,10},{9,11},{10,... | collective-permute-start | bytes 774152 | tf_op jit(solution)/shard_map/far1_z/ppermute | solution.py:261
  39.4 11.7 %collective-permute-start.9 = (bf16[72,1792]{1,0:T(8,128)(2,1)S(1)}, bf16[72,1792]{1,0:T(8,128)(2,1)S(1)}, u32[]{:S(2)}, u32[]{:S(2)}) collective-permute-start(bf16[72,1792]{1,0:T(8,128)(2,1)S(1)} %collective-permute-done.7.refs_1_), channel_id=1, source_target_pairs={{0,2},{1,3},{2,0},{3,1},{4,6},{5,7},{6,4},{7,5},{8,10},{9,11},{10,... | collective-permute-start | bytes 774152 | tf_op jit(solution)/shard_map/own_d0/ppermute | solution.py:261
  41.9 15.5 %collective-permute-start.13 = (bf16[72,1792]{1,0:T(8,128)(2,1)S(1)}, bf16[72,1792]{1,0:T(8,128)(2,1)S(1)}, u32[]{:S(2)}, u32[]{:S(2)}) collective-permute-start(bf16[72,1792]{1,0:T(8,128)(2,1)S(1)} %collective-permute-done.12.refs_0_), channel_id=1, source_target_pairs={{0,1},{1,0},{2,3},{3,2},{4,5},{5,4},{6,7},{7,6},{8,9},{9,8},{10,11... | collective-permute-start | bytes 774152 | tf_op jit(solution)/shard_map/far1_y/ppermute | solution.py:261
  46.4 9.5 %collective-permute-start.16 = (bf16[72,1792]{1,0:T(8,128)(2,1)S(1)}, bf16[72,1792]{1,0:T(8,128)(2,1)S(1)}, u32[]{:S(2)}, u32[]{:S(2)}) collective-permute-start(bf16[72,1792]{1,0:T(8,128)(2,1)S(1)} %get-tuple-element.81), channel_id=1, source_target_pairs={{0,1},{1,0},{2,3},{3,2},{4,5},{5,4},{6,7},{7,6},{8,9},{9,8},{10,11... | collective-permute-start | bytes 774152 | tf_op jit(solution)/shard_map/back0_d/ppermute | solution.py:261
  48.0 13.0 %collective-permute-start.15 = (bf16[72,1792]{1,0:T(8,128)(2,1)S(1)}, bf16[72,1792]{1,0:T(8,128)(2,1)S(1)}, u32[]{:S(2)}, u32[]{:S(2)}) collective-permute-start(bf16[72,1792]{1,0:T(8,128)(2,1)S(1)} %collective-permute-done.14.refs_2_), channel_id=1, source_target_pairs={{0,1},{1,0},{2,3},{3,2},{4,5},{5,4},{6,7},{7,6},{8,9},{9,8},{10,11... | collective-permute-start | bytes 774152 | tf_op jit(solution)/shard_map/far1_d/ppermute | solution.py:261
  54.7 12.4 %collective-permute-start.11 = (bf16[72,1792]{1,0:T(8,128)(2,1)S(1)}, bf16[72,1792]{1,0:T(8,128)(2,1)S(1)}, u32[]{:S(2)}, u32[]{:S(2)}) collective-permute-start(bf16[72,1792]{1,0:T(8,128)(2,1)S(1)} %get-tuple-element.72), channel_id=1, source_target_pairs={{0,2},{1,3},{2,0},{3,1},{4,6},{5,7},{6,4},{7,5},{8,10},{9,11},{10,... | collective-permute-start | bytes 774152 | tf_op jit(solution)/shard_map/mine_d0/ppermute | solution.py:261
  55.9 11.3 %collective-permute-start.17 = (bf16[72,1792]{1,0:T(8,128)(2,1)S(1)}, bf16[72,1792]{1,0:T(8,128)(2,1)S(1)}, u32[]{:S(2)}, u32[]{:S(2)}) collective-permute-start(bf16[72,1792]{1,0:T(8,128)(2,1)S(1)} %get-tuple-element.82), channel_id=1, source_target_pairs={{0,1},{1,0},{2,3},{3,2},{4,5},{5,4},{6,7},{7,6},{8,9},{9,8},{10,11... | collective-permute-start | bytes 774152 | tf_op jit(solution)/shard_map/back0_y/ppermute | solution.py:261
  57.1 10.8 %collective-permute-start.20 = (bf16[72,1792]{1,0:T(8,128)(2,1)S(1)}, bf16[72,1792]{1,0:T(8,128)(2,1)S(1)}, u32[]{:S(2)}, u32[]{:S(2)}) collective-permute-start(bf16[72,1792]{1,0:T(8,128)(2,1)S(1)} %add_convert_fusion.6), channel_id=1, source_target_pairs={{0,2},{1,3},{2,0},{3,1},{4,6},{5,7},{6,4},{7,5},{8,10},{9,11},{10,... | collective-permute-start | bytes 774152 | tf_op jit(solution)/shard_map/back0_z/ppermute | solution.py:261
  65.0 9.2 %collective-permute-start.27 = (bf16[72,1792]{1,0:T(8,128)(2,1)S(1)}, bf16[72,1792]{1,0:T(8,128)(2,1)S(1)}, u32[]{:S(2)}, u32[]{:S(2)}) collective-permute-start(bf16[72,1792]{1,0:T(8,128)(2,1)S(1)} %get-tuple-element.97), channel_id=1, source_target_pairs={{0,1},{1,0},{2,3},{3,2},{4,5},{5,4},{6,7},{7,6},{8,9},{9,8},{10,11... | collective-permute-start | bytes 774152 | tf_op jit(solution)/shard_map/back1_d/ppermute | solution.py:261
  65.5 13.1 %collective-permute-start.24 = (bf16[72,1792]{1,0:T(8,128)(2,1)S(1)}, bf16[72,1792]{1,0:T(8,128)(2,1)S(1)}, u32[]{:S(2)}, u32[]{:S(2)}) collective-permute-start(bf16[72,1792]{1,0:T(8,128)(2,1)S(1)} %get-tuple-element.93), channel_id=1, source_target_pairs={{0,1},{1,0},{2,3},{3,2},{4,5},{5,4},{6,7},{7,6},{8,9},{9,8},{10,11... | collective-permute-start | bytes 774152 | tf_op jit(solution)/shard_map/mine_d1/ppermute | solution.py:261
  68.0 30.8 %collective-permute-start.22 = (bf16[72,1792]{1,0:T(8,128)(2,1)S(1)}, bf16[72,1792]{1,0:T(8,128)(2,1)S(1)}, u32[]{:S(2)}, u32[]{:S(2)}) collective-permute-start(bf16[72,1792]{1,0:T(8,128)(2,1)S(1)} %add_convert_fusion.4), channel_id=1, source_target_pairs={{0,4},{1,5},{2,6},{3,7},{4,0},{5,1},{6,2},{7,3},{8,12},{9,13},{10,... | collective-permute-start | bytes 774152 | tf_op jit(solution)/shard_map/back0/ppermute | solution.py:261
  71.8 10.7 %collective-permute-start.18 = (bf16[72,1792]{1,0:T(8,128)(2,1)S(1)}, bf16[72,1792]{1,0:T(8,128)(2,1)S(1)}, u32[]{:S(2)}, u32[]{:S(2)}) collective-permute-start(bf16[72,1792]{1,0:T(8,128)(2,1)S(1)} %get-tuple-element.83), channel_id=1, source_target_pairs={{0,1},{1,0},{2,3},{3,2},{4,5},{5,4},{6,7},{7,6},{8,9},{9,8},{10,11... | collective-permute-start | bytes 774152 | tf_op jit(solution)/shard_map/back1_y/ppermute | solution.py:261
  74.3 12.2 %collective-permute-start.28 = (bf16[72,1792]{1,0:T(8,128)(2,1)S(1)}, bf16[72,1792]{1,0:T(8,128)(2,1)S(1)}, u32[]{:S(2)}, u32[]{:S(2)}) collective-permute-start(bf16[72,1792]{1,0:T(8,128)(2,1)S(1)} %add_convert_fusion.1), channel_id=1, source_target_pairs={{0,2},{1,3},{2,0},{3,1},{4,6},{5,7},{6,4},{7,5},{8,10},{9,11},{10,... | collective-permute-start | bytes 774152 | tf_op jit(solution)/shard_map/back1_z/ppermute | solution.py:261
  78.7 13.7 %collective-permute-start.25 = (bf16[72,1792]{1,0:T(8,128)(2,1)S(1)}, bf16[72,1792]{1,0:T(8,128)(2,1)S(1)}, u32[]{:S(2)}, u32[]{:S(2)}) collective-permute-start(bf16[72,1792]{1,0:T(8,128)(2,1)S(1)} %add_convert_fusion.3), channel_id=1, source_target_pairs={{0,2},{1,3},{2,0},{3,1},{4,6},{5,7},{6,4},{7,5},{8,10},{9,11},{10,... | collective-permute-start | bytes 774152 | tf_op jit(solution)/shard_map/mine_z1/ppermute | solution.py:261
  78.8 17.8 %collective-permute-start.21 = (bf16[72,1792]{1,0:T(8,128)(2,1)S(1)}, bf16[72,1792]{1,0:T(8,128)(2,1)S(1)}, u32[]{:S(2)}, u32[]{:S(2)}) collective-permute-start(bf16[72,1792]{1,0:T(8,128)(2,1)S(1)} %get-tuple-element.87), channel_id=1, source_target_pairs={{0,2},{1,3},{2,0},{3,1},{4,6},{5,7},{6,4},{7,5},{8,10},{9,11},{10,... | collective-permute-start | bytes 774152 | tf_op jit(solution)/shard_map/mine_z0/ppermute | solution.py:261
  82.5 9.9 %collective-permute-start.23 = (bf16[72,1792]{1,0:T(8,128)(2,1)S(1)}, bf16[72,1792]{1,0:T(8,128)(2,1)S(1)}, u32[]{:S(2)}, u32[]{:S(2)}) collective-permute-start(bf16[72,1792]{1,0:T(8,128)(2,1)S(1)} %get-tuple-element.90), channel_id=1, source_target_pairs={{0,1},{1,0},{2,3},{3,2},{4,5},{5,4},{6,7},{7,6},{8,9},{9,8},{10,11... | collective-permute-start | bytes 774152 | tf_op jit(solution)/shard_map/mine_y1/ppermute | solution.py:261
  86.6 13.7 %collective-permute-start.29 = (bf16[72,1792]{1,0:T(8,128)(2,1)S(1)}, bf16[72,1792]{1,0:T(8,128)(2,1)S(1)}, u32[]{:S(2)}, u32[]{:S(2)}) collective-permute-start(bf16[72,1792]{1,0:T(8,128)(2,1)S(1)} %add_convert_fusion), channel_id=1, source_target_pairs={{0,12},{1,13},{2,14},{3,15},{4,8},{5,9},{6,10},{7,11},{8,4},{9,5},... | collective-permute-start | bytes 774152 | tf_op jit(solution)/shard_map/back1/ppermute | solution.py:261
  92.4 6.3 %collective-permute-start.19 = (bf16[72,1792]{1,0:T(8,128)(2,1)S(1)}, bf16[72,1792]{1,0:T(8,128)(2,1)S(1)}, u32[]{:S(2)}, u32[]{:S(2)}) collective-permute-start(bf16[72,1792]{1,0:T(8,128)(2,1)S(1)} %add_convert_fusion.7), channel_id=1, source_target_pairs={{0,1},{1,0},{2,3},{3,2},{4,5},{5,4},{6,7},{7,6},{8,9},{9,8},{10,11... | collective-permute-start | bytes 774152 | tf_op jit(solution)/shard_map/mine_y0/ppermute | solution.py:261
  92.5 7.9 %collective-permute-start.26 = (bf16[72,1792]{1,0:T(8,128)(2,1)S(1)}, bf16[72,1792]{1,0:T(8,128)(2,1)S(1)}, u32[]{:S(2)}, u32[]{:S(2)}) collective-permute-start(bf16[72,1792]{1,0:T(8,128)(2,1)S(1)} %add_convert_fusion.2), channel_id=1, source_target_pairs={{0,8},{1,9},{2,10},{3,11},{4,12},{5,13},{6,14},{7,15},{8,0},{9,1},... | collective-permute-start | bytes 774152 | tf_op jit(solution)/shard_map/home1/ppermute | solution.py:261

commit v5 on v4

--- a/solution.py
+++ b/solution.py
@@ -9,22 +9,23 @@
 CAP = 18
 GSIZE = 32
 STACK = 4
-COST = 60
+COST = 15
+
+HOPS = {"own": "yy", "far": "zy", "mine": "zy", "back": "yy"}
 
 AFTER = {
     "load": ("own1",),
-    "own_y0": ("own1",),
-    "own_z0": ("own_z1",),
-    "own_d0": ("own_z0",),
-    "own_d1": ("own_y0",),
-    "far0_d": ("far0_y",),
-    "far0_y": ("load", "own_y1"),
-    "far0_z": ("load", "own_z1"),
+    "own_z0": ("own1",),
+    "own_d0": ("far0_y",),
+    "own_d1": ("own_y1",),
+    "far0_d": ("own_z0",),
+    "far0_y": ("load", "own_y0", "own_y1"),
+    "far0_z": ("load", "own_z0"),
     "far1": ("far0", "load"),
-    "far1_d": ("far0_d",),
+    "far1_d": ("own_d0",),
     "far1_experts": ("own_experts",),
     "far1_y": ("own_d1",),
-    "far1_z": ("load", "own_z1"),
+    "far1_z": ("far0_z",),
     "own_experts": ("far0_experts",),
     "back0_y": ("back0_d",),
     "back1_y": ("back0_y",),
@@ -34,6 +35,7 @@
     "mine_y1": ("back1_y",),
     "mine_z0": ("back0_z",),
     "mine_z1": ("back0_z",),
+    "home1": ("back1_z",),
 }
 
 route_scale = 2.5
@@ -266,6 +268,12 @@
     def along_z(value):
         return send(value, 0, 0, 2)
 
+    along = {"y": along_y, "z": along_z}
+
+    def hops(kind, i):
+        hop = HOPS[kind][i % 2]
+        return hop, "z" if hop == "y" else "y"
+
     fars = [(n, d) for d in range(1, teams) for n in range(nodes)]
     steps = {"load": (load, ("gate",))}
     values = {"gate": gate_weight}
@@ -278,14 +286,16 @@
         )
         steps["own_y" + at] = (along_y, ("own" + at,))
         steps["own_z" + at] = (along_z, ("own" + at,))
-        steps["own_d" + at] = (along_y, ("own_z" + at,)) if n % 2 else (along_z, ("own_y" + at,))
+        hop, turn = hops("own", n)
+        steps["own_d" + at] = (along[hop], ("own_" + turn + at,))
     for i, (n, d) in enumerate(fars):
         far = "far%d" % i
         values["row_" + far] = packed[n, d]
         steps[far] = (lambda v, n=n, d=d: send(v, n, d, 0), ("row_" + far,))
         steps[far + "_y"] = (along_y, (far,))
         steps[far + "_z"] = (along_z, (far,))
-        steps[far + "_d"] = (along_y, (far + "_z",))
+        hop, turn = hops("far", i)
+        steps[far + "_d"] = (along[hop], (far + "_" + turn,))
     sides = ("", "_y", "_z", "_d")
     steps["own_experts"] = (
         experts,
@@ -296,22 +306,22 @@
         steps[far + "_experts"] = (experts, (*[far + v for v in sides], "load"))
         for j, v in enumerate(sides):
             steps[far + "_out" + v] = (lambda out, j=j: out[j], (far + "_experts",))
-        steps[back + "_d"] = (along_y, (far + "_out_d",))
-        steps[back + "_y"] = (along_y, (far + "_out_y",))
-        steps[back + "_zsum"] = (total, (far + "_out_z", back + "_d"))
-        steps[back + "_z"] = (along_z, (back + "_zsum",))
+        hop, turn = hops("back", i)
+        steps[back + "_d"] = (along[hop], (far + "_out_d",))
+        steps[back + "_" + hop] = (along[hop], (far + "_out_" + hop,))
+        steps[back + "_turn"] = (total, (far + "_out_" + turn, back + "_d"))
+        steps[back + "_" + turn] = (along[turn], (back + "_turn",))
         steps[back + "_sum"] = (total, (far + "_out", back + "_y", back + "_z"))
         steps[back] = (lambda v, n=n, d=d: send(v, nodes - n, teams - d, 0), (back + "_sum",))
     for n in range(nodes):
         at = str(n)
         for j, v in enumerate(sides):
             steps["own_out" + v + at] = (lambda out, j=n * TEAM + j: out[j], ("own_experts",))
-        first, second = ("z", "y") if n % 2 else ("y", "z")
-        steps["mine_d" + at] = (along_y if n % 2 else along_z, ("own_out_d" + at,))
-        steps["mine_sum" + at] = (total, ("own_out_" + first + at, "mine_d" + at))
-        along = {"y": along_y, "z": along_z}
-        steps["mine_" + first + at] = (along[first], ("mine_sum" + at,))
-        steps["mine_" + second + at] = (along[second], ("own_out_" + second + at,))
+        hop, turn = hops("mine", n)
+        steps["mine_d" + at] = (along[hop], ("own_out_d" + at,))
+        steps["mine_" + hop + at] = (along[hop], ("own_out_" + hop + at,))
+        steps["mine_turn" + at] = (total, ("own_out_" + turn + at, "mine_d" + at))
+        steps["mine_" + turn + at] = (along[turn], ("mine_turn" + at,))
         steps["mine" + at] = (total, ("own_out" + at, "mine_y" + at, "mine_z" + at))
         steps["home" + at] = (
             (lambda v, n=n: send(v, nodes - n, 0, 0)) if n else (lambda v: v),

time: 102 us -> 101 us (level)
  starting transfers between devices: 30.7 us -> 28 us
  waiting for transfers between devices: 47.2 us -> 48.9 us
    ppermute x30, starting transfers between devices: 30.7 us -> 28 us  [send(): return lax.ppermute(value, ('node', 'local'), pairs)]
    ppermute x30, waiting for transfers between devices: 47.2 us -> 48.9 us  [send(): return lax.ppermute(value, ('node', 'local'), pairs)]
  transfers between devices with their start and end apart: 30 -> 30, of which waited for: 17 -> 15; matrix products, arithmetic and copies ran while one was open for 1% -> 1% of each run, Pallas kernels for 19% -> 19%
where the time goes in v5:
time: 101 us
  waiting for transfers between devices  48.9 us (48%)
  starting transfers between devices  28 us (28%)
  Pallas kernels  23.3 us (23%)
    ppermute x30, waiting for transfers between devices, send(): return lax.ppermute(value, ('node', 'local'), pairs)  48.9 us
    ppermute x30, starting transfers between devices, send(): return lax.ppermute(value, ('node', 'local'), pairs)  28 us
    pallas_call x3, Pallas kernels, experts(): pl.pallas_call(expert_kernel, out_shape=[block] * len(blocks), in_specs=[...  11.6 us
    pallas_call x1, Pallas kernels, load(): pl.pallas_call(load_kernel, out_shape=[pltpu.VMEM((STACK, width, hidden_w...  7.44 us
    pallas_call x1, Pallas kernels, local(): pl.pallas_call(pack_kernel, out_shape=[block] * flight + [jax.ShapeDtypeS...  2.61 us
  transfers between devices with their start and end apart: 30, of which 15 were waited for; matrix products, arithmetic and copies ran while one was open for 1% of the time, Pallas kernels for 19%

profile of v5, /device:TPU:0, one launch (start us, length us, event | category | flops | bytes accessed | tf_op | source)
XLA Modules:
  0.0 101.1 jit_solution(519233332424391530)
XLA Ops:
  0.0 0.1 pad_add_fusion.flight_ref
  0.1 2.6 %pack.1 = (bf16[72,1792]{1,0:T(8,128)(2,1)S(1)}, bf16[72,1792]{1,0:T(8,128)(2,1)S(1)}, bf16[72,1792]{1,0:T(8,128)(2,1)S(1)}, bf16[72,1792]{1,0:T(8,128)(2,1)S(1)...) custom-call(s32[4]{0:T(128)S(1)} %pad_add_fusion.flight_ref, s32[8,144]{1,0:T(8,128)} %bitcast.6, f32[8,144]{1,0:T(8,128)} %bitcast.7, ...), custom_call_target="tpu_custom_call" | custom-call | tf_op jit(solution)/shard_map/pack/pallas_call | solution.py:198
  2.7 0.5 collective-permute-start
  3.2 3.7 %collective-permute-start.1 = (bf16[72,1792]{1,0:T(8,128)(2,1)S(1)}, bf16[72,1792]{1,0:T(8,128)(2,1)S(1)}, u32[]{:S(2)}, u32[]{:S(2)}) collective-permute-start(bf16[72,1792]{1,0:T(8,128)(2,1)S(1)} %get-tuple-element.60), channel_id=1, source_target_pairs={{0,4},{1,5},{2,6},{3,7},{4,0},{5,1},{6,2},{7,3},{8,12},{9,13},{10,... | collective-permute-start | bytes 774152 | tf_op jit(solution)/shard_map/far0/ppermute | solution.py:263
  6.9 1.5 %collective-permute-start.2 = (bf16[72,1792]{1,0:T(8,128)(2,1)S(1)}, bf16[72,1792]{1,0:T(8,128)(2,1)S(1)}, u32[]{:S(2)}, u32[]{:S(2)}) collective-permute-start(bf16[72,1792]{1,0:T(8,128)(2,1)S(1)} %get-tuple-element.66.refs_0_), channel_id=1, source_target_pairs={{0,1},{1,0},{2,3},{3,2},{4,5},{5,4},{6,7},{7,6},{8,9},{9,8},{10,11... | collective-permute-start | bytes 774152 | tf_op jit(solution)/shard_map/own_y0/ppermute | solution.py:263
  8.4 0.5 collective-permute-start.3
  8.9 1.6 %collective-permute-start.5 = (bf16[72,1792]{1,0:T(8,128)(2,1)S(1)}, bf16[72,1792]{1,0:T(8,128)(2,1)S(1)}, u32[]{:S(2)}, u32[]{:S(2)}) collective-permute-start(bf16[72,1792]{1,0:T(8,128)(2,1)S(1)} %get-tuple-element.66.refs_0_), channel_id=1, source_target_pairs={{0,2},{1,3},{2,0},{3,1},{4,6},{5,7},{6,4},{7,5},{8,10},{9,11},{10,... | collective-permute-start | bytes 774152 | tf_op jit(solution)/shard_map/own_z0/ppermute | solution.py:263
  10.5 7.4 %load.1 = (bf16[4,1792,512]{2,1,0:T(8,128)(2,1)S(1)}, bf16[4,1792,512]{2,1,0:T(8,128)(2,1)S(1)}, bf16[4,512,1792]{2,1,0:T(8,128)(2,1)S(1)}) custom-call(bf16[1,7168,512]{2,1,0:T(8,128)(2,1)} %gate_hbm, bf16[1,7168,512]{2,1,0:T(8,128)(2,1)} %up_hbm.1, bf16[1,512,7168]{2,1,0:T(8,128)(2,1)} %down_hbm.1), custom_call_target="tpu_custom_call" | custom-call | bytes 55050240 | tf_op jit(solution)/shard_map/load/load/pallas_call | solution.py:220
  17.9 0.5 collective-permute-start.9
  18.5 0.9 collective-permute-done.1.refs_0_
  19.3 1.4 %collective-permute-done.3.refs_5_ = bf16[72,1792]{1,0:T(8,128)(2,1)S(1)} collective-permute-done((bf16[72,1792]{1,0:T(8,128)(2,1)S(1)}, bf16[72,1792]{1,0:T(8,128)(2,1)S(1)}, u32[]{:S(2)}, u32[]{:S(2)}) %collective-permute-start.3) | collective-permute-done | bytes 258080 | tf_op jit(solution)/shard_map/own_y1/ppermute | solution.py:263
  20.7 1.5 %collective-permute-start.4 = (bf16[72,1792]{1,0:T(8,128)(2,1)S(1)}, bf16[72,1792]{1,0:T(8,128)(2,1)S(1)}, u32[]{:S(2)}, u32[]{:S(2)}) collective-permute-start(bf16[72,1792]{1,0:T(8,128)(2,1)S(1)} %collective-permute-done.1.refs_0_), channel_id=1, source_target_pairs={{0,1},{1,0},{2,3},{3,2},{4,5},{5,4},{6,7},{7,6},{8,9},{9,8},{10,11... | collective-permute-start | bytes 774152 | tf_op jit(solution)/shard_map/far0_y/ppermute | solution.py:263
  22.2 2.1 %collective-permute-start.6 = (bf16[72,1792]{1,0:T(8,128)(2,1)S(1)}, bf16[72,1792]{1,0:T(8,128)(2,1)S(1)}, u32[]{:S(2)}, u32[]{:S(2)}) collective-permute-start(bf16[72,1792]{1,0:T(8,128)(2,1)S(1)} %collective-permute-done.1.refs_0_), channel_id=1, source_target_pairs={{0,2},{1,3},{2,0},{3,1},{4,6},{5,7},{6,4},{7,5},{8,10},{9,11},{10,... | collective-permute-start | bytes 774152 | tf_op jit(solution)/shard_map/far0_z/ppermute | solution.py:263
  24.3 4.3 %collective-permute-done.9.refs_6_ = bf16[72,1792]{1,0:T(8,128)(2,1)S(1)} collective-permute-done((bf16[72,1792]{1,0:T(8,128)(2,1)S(1)}, bf16[72,1792]{1,0:T(8,128)(2,1)S(1)}, u32[]{:S(2)}, u32[]{:S(2)}) %collective-permute-start.9) | collective-permute-done | bytes 258080 | tf_op jit(solution)/shard_map/own_z1/ppermute | solution.py:263
  28.6 2.2 %collective-permute-start.10 = (bf16[72,1792]{1,0:T(8,128)(2,1)S(1)}, bf16[72,1792]{1,0:T(8,128)(2,1)S(1)}, u32[]{:S(2)}, u32[]{:S(2)}) collective-permute-start(bf16[72,1792]{1,0:T(8,128)(2,1)S(1)} %collective-permute-done.9.refs_6_), channel_id=1, source_target_pairs={{0,1},{1,0},{2,3},{3,2},{4,5},{5,4},{6,7},{7,6},{8,9},{9,8},{10,11... | collective-permute-start | bytes 774152 | tf_op jit(solution)/shard_map/own_d1/ppermute | solution.py:263
  30.8 0.8 collective-permute-start.8
  31.5 5.0 %collective-permute-done.12.refs_0_ = bf16[72,1792]{1,0:T(8,128)(2,1)S(1)} collective-permute-done((bf16[72,1792]{1,0:T(8,128)(2,1)S(1)}, bf16[72,1792]{1,0:T(8,128)(2,1)S(1)}, u32[]{:S(2)}, u32[]{:S(2)}) %collective-permute-start.12) | collective-permute-done | bytes 258080 | tf_op jit(solution)/shard_map/far1/ppermute | solution.py:263
  36.6 2.1 %collective-permute-done.6.refs_2_ = bf16[72,1792]{1,0:T(8,128)(2,1)S(1)} collective-permute-done((bf16[72,1792]{1,0:T(8,128)(2,1)S(1)}, bf16[72,1792]{1,0:T(8,128)(2,1)S(1)}, u32[]{:S(2)}, u32[]{:S(2)}) %collective-permute-start.6) | collective-permute-done | bytes 258080 | tf_op jit(solution)/shard_map/far0_z/ppermute | solution.py:263
  38.6 1.6 %collective-permute-start.13 = (bf16[72,1792]{1,0:T(8,128)(2,1)S(1)}, bf16[72,1792]{1,0:T(8,128)(2,1)S(1)}, u32[]{:S(2)}, u32[]{:S(2)}) collective-permute-start(bf16[72,1792]{1,0:T(8,128)(2,1)S(1)} %collective-permute-done.12.refs_0_), channel_id=1, source_target_pairs={{0,1},{1,0},{2,3},{3,2},{4,5},{5,4},{6,7},{7,6},{8,9},{9,8},{10,11... | collective-permute-start | bytes 774152 | tf_op jit(solution)/shard_map/far1_y/ppermute | solution.py:263
  40.2 3.9 %collective-permute-done.7.refs_3_ = bf16[72,1792]{1,0:T(8,128)(2,1)S(1)} collective-permute-done((bf16[72,1792]{1,0:T(8,128)(2,1)S(1)}, bf16[72,1792]{1,0:T(8,128)(2,1)S(1)}, u32[]{:S(2)}, u32[]{:S(2)}) %collective-permute-start.7) | collective-permute-done | bytes 258080 | tf_op jit(solution)/shard_map/far0_d/ppermute | solution.py:263
  44.1 4.0 %experts.3 = (bf16[72,1792]{1,0:T(8,128)(2,1)S(1)}, bf16[72,1792]{1,0:T(8,128)(2,1)S(1)}, bf16[72,1792]{1,0:T(8,128)(2,1)S(1)}, bf16[72,1792]{1,0:T(8,128)(2,1)S(1)}) custom-call(bf16[4,1792,512]{2,1,0:T(8,128)(2,1)S(1)} %get-tuple-element.56.gate, bf16[4,1792,512]{2,1,0:T(8,128)(2,1)S(1)} %get-tuple-element.57.up, ...), custom_call_target="tpu_custom_call" | custom-call | flops 3963617280 | bytes 55050240 | tf_op jit(solution)/shard_map/far0_experts/experts/pallas_call | solution.py:237
  48.1 1.7 %collective-permute-start.16 = (bf16[72,1792]{1,0:T(8,128)(2,1)S(1)}, bf16[72,1792]{1,0:T(8,128)(2,1)S(1)}, u32[]{:S(2)}, u32[]{:S(2)}) collective-permute-start(bf16[72,1792]{1,0:T(8,128)(2,1)S(1)} %get-tuple-element.80), channel_id=1, source_target_pairs={{0,1},{1,0},{2,3},{3,2},{4,5},{5,4},{6,7},{7,6},{8,9},{9,8},{10,11... | collective-permute-start | bytes 774152 | tf_op jit(solution)/shard_map/back0_d/ppermute | solution.py:263
  49.8 0.4 collective-permute-start.15
  50.2 3.6 %experts.4 = (bf16[72,1792]{1,0:T(8,128)(2,1)S(1)}, bf16[72,1792]{1,0:T(8,128)(2,1)S(1)}, bf16[72,1792]{1,0:T(8,128)(2,1)S(1)}, bf16[72,1792]{1,0:T(8,128)(2,1)S...) custom-call(bf16[4,1792,512]{2,1,0:T(8,128)(2,1)S(1)} %get-tuple-ele, ...), custom_call_target="tpu_custom_call" | custom-call | flops 7927234560 | bytes 55050240 | tf_op jit(solution)/shard_map/own_experts/experts/pallas_call | solution.py:237
  53.9 3.5 %collective-permute-done.16 = bf16[72,1792]{1,0:T(8,128)(2,1)S(1)} collective-permute-done((bf16[72,1792]{1,0:T(8,128)(2,1)S(1)}, bf16[72,1792]{1,0:T(8,128)(2,1)S(1)}, u32[]{:S(2)}, u32[]{:S(2)}) %collective-permute-start.16) | collective-permute-done | bytes 258080 | tf_op jit(solution)/shard_map/back0_d/ppermute | solution.py:263
  57.4 1.6 %collective-permute-start.17 = (bf16[72,1792]{1,0:T(8,128)(2,1)S(1)}, bf16[72,1792]{1,0:T(8,128)(2,1)S(1)}, u32[]{:S(2)}, u32[]{:S(2)}) collective-permute-start(bf16[72,1792]{1,0:T(8,128)(2,1)S(1)} %get-tuple-element.81), channel_id=1, source_target_pairs={{0,1},{1,0},{2,3},{3,2},{4,5},{5,4},{6,7},{7,6},{8,9},{9,8},{10,11... | collective-permute-start | bytes 774152 | tf_op jit(solution)/shard_map/back0_y/ppermute | solution.py:263
  59.1 3.6 %collective-permute-done.15.refs_3_ = bf16[72,1792]{1,0:T(8,128)(2,1)S(1)} collective-permute-done((bf16[72,1792]{1,0:T(8,128)(2,1)S(1)}, bf16[72,1792]{1,0:T(8,128)(2,1)S(1)}, u32[]{:S(2)}, u32[]{:S(2)}) %collective-permute-start.15) | collective-permute-done | bytes 258080 | tf_op jit(solution)/shard_map/far1_d/ppermute | solution.py:263
  62.7 4.0 %experts.5 = (bf16[72,1792]{1,0:T(8,128)(2,1)S(1)}, bf16[72,1792]{1,0:T(8,128)(2,1)S(1)}, bf16[72,1792]{1,0:T(8,128)(2,1)S(1)}, bf16[72,1792]{1,0:T(8,128)(2,1)S(1)}) custom-call(bf16[4,1792,512]{2,1,0:T(8,128)(2,1)S(1)} %get-tuple-element.56.gate, bf16[4,1792,512]{2,1,0:T(8,128)(2,1)S(1)} %get-tuple-element.57.up, ...), custom_call_target="tpu_custom_call" | custom-call | flops 3963617280 | bytes 55050240 | tf_op jit(solution)/shard_map/far1_experts/experts/pallas_call | solution.py:237
  66.7 1.5 %collective-permute-start.26 = (bf16[72,1792]{1,0:T(8,128)(2,1)S(1)}, bf16[72,1792]{1,0:T(8,128)(2,1)S(1)}, u32[]{:S(2)}, u32[]{:S(2)}) collective-permute-start(bf16[72,1792]{1,0:T(8,128)(2,1)S(1)} %get-tuple-element.95), channel_id=1, source_target_pairs={{0,1},{1,0},{2,3},{3,2},{4,5},{5,4},{6,7},{7,6},{8,9},{9,8},{10,11... | collective-permute-start | bytes 774152 | tf_op jit(solution)/shard_map/back1_d/ppermute | solution.py:263
  68.3 0.5 collective-permute-start.24
  68.9 0.1 add_convert_fusion.4
  69.0 1.2 %collective-permute-start.22 = (bf16[72,1792]{1,0:T(8,128)(2,1)S(1)}, bf16[72,1792]{1,0:T(8,128)(2,1)S(1)}, u32[]{:S(2)}, u32[]{:S(2)}) collective-permute-start(bf16[72,1792]{1,0:T(8,128)(2,1)S(1)} %add_convert_fusion.4), channel_id=1, source_target_pairs={{0,4},{1,5},{2,6},{3,7},{4,0},{5,1},{6,2},{7,3},{8,12},{9,13},{10,... | collective-permute-start | bytes 774152 | tf_op jit(solution)/shard_map/back0/ppermute | solution.py:263
  70.2 0.6 collective-permute-start.18
  70.8 5.1 %collective-permute-done.26 = bf16[72,1792]{1,0:T(8,128)(2,1)S(1)} collective-permute-done((bf16[72,1792]{1,0:T(8,128)(2,1)S(1)}, bf16[72,1792]{1,0:T(8,128)(2,1)S(1)}, u32[]{:S(2)}, u32[]{:S(2)}) %collective-permute-start.26) | collective-permute-done | bytes 258080 | tf_op jit(solution)/shard_map/back1_d/ppermute | solution.py:263
  76.0 0.2 collective-permute-start.27
  76.2 3.1 %collective-permute-done.24 = bf16[72,1792]{1,0:T(8,128)(2,1)S(1)} collective-permute-done((bf16[72,1792]{1,0:T(8,128)(2,1)S(1)}, bf16[72,1792]{1,0:T(8,128)(2,1)S(1)}, u32[]{:S(2)}, u32[]{:S(2)}) %collective-permute-start.24) | collective-permute-done | bytes 258080 | tf_op jit(solution)/shard_map/mine_d1/ppermute | solution.py:263
  79.4 0.2 collective-permute-start.25
  79.6 1.9 %collective-permute-start.21 = (bf16[72,1792]{1,0:T(8,128)(2,1)S(1)}, bf16[72,1792]{1,0:T(8,128)(2,1)S(1)}, u32[]{:S(2)}, u32[]{:S(2)}) collective-permute-start(bf16[72,1792]{1,0:T(8,128)(2,1)S(1)} %get-tuple-element.86), channel_id=1, source_target_pairs={{0,2},{1,3},{2,0},{3,1},{4,6},{5,7},{6,4},{7,5},{8,10},{9,11},{10,... | collective-permute-start | bytes 774152 | tf_op jit(solution)/shard_map/mine_z0/ppermute | solution.py:263
  81.5 2.8 %collective-permute-done.18 = bf16[72,1792]{1,0:T(8,128)(2,1)S(1)} collective-permute-done((bf16[72,1792]{1,0:T(8,128)(2,1)S(1)}, bf16[72,1792]{1,0:T(8,128)(2,1)S(1)}, u32[]{:S(2)}, u32[]{:S(2)}) %collective-permute-start.18) | collective-permute-done | bytes 258080 | tf_op jit(solution)/shard_map/back1_y/ppermute | solution.py:263
  84.3 1.5 %collective-permute-start.23 = (bf16[72,1792]{1,0:T(8,128)(2,1)S(1)}, bf16[72,1792]{1,0:T(8,128)(2,1)S(1)}, u32[]{:S(2)}, u32[]{:S(2)}) collective-permute-start(bf16[72,1792]{1,0:T(8,128)(2,1)S(1)} %get-tuple-element.89), channel_id=1, source_target_pairs={{0,1},{1,0},{2,3},{3,2},{4,5},{5,4},{6,7},{7,6},{8,9},{9,8},{10,11... | collective-permute-start | bytes 774152 | tf_op jit(solution)/shard_map/mine_y1/ppermute | solution.py:263
  85.7 0.1 add_convert_fusion
  85.9 6.5 %collective-permute-done.25 = bf16[72,1792]{1,0:T(8,128)(2,1)S(1)} collective-permute-done((bf16[72,1792]{1,0:T(8,128)(2,1)S(1)}, bf16[72,1792]{1,0:T(8,128)(2,1)S(1)}, u32[]{:S(2)}, u32[]{:S(2)}) %collective-permute-start.25) | collective-permute-done | bytes 258080 | tf_op jit(solution)/shard_map/mine_z1/ppermute | solution.py:263
  92.4 0.1 add_convert_fusion.2
  92.6 3.3 %collective-permute-done.21 = bf16[72,1792]{1,0:T(8,128)(2,1)S(1)} collective-permute-done((bf16[72,1792]{1,0:T(8,128)(2,1)S(1)}, bf16[72,1792]{1,0:T(8,128)(2,1)S(1)}, u32[]{:S(2)}, u32[]{:S(2)}) %collective-permute-start.21) | collective-permute-done | bytes 258080 | tf_op jit(solution)/shard_map/mine_z0/ppermute | solution.py:263
  95.9 2.9 %collective-permute-done.19 = bf16[72,1792]{1,0:T(8,128)(2,1)S(1)} collective-permute-done((bf16[72,1792]{1,0:T(8,128)(2,1)S(1)}, bf16[72,1792]{1,0:T(8,128)(2,1)S(1)}, u32[]{:S(2)}, u32[]{:S(2)}) %collective-permute-start.19) | collective-permute-done | bytes 258080 | tf_op jit(solution)/shard_map/mine_y0/ppermute | solution.py:263
  98.7 0.1 add_convert_fusion.5.refs_0_
  98.8 0.6 collective-permute-done.29.refs_3_
  99.4 1.7 %combine.1 = bf16[144,7168]{1,0:T(8,128)(2,1)} custom-call(bf16[72,144]{1,0:T(8,128)(2,1)S(1)} %get-tuple-element.52.pick_ref, f32[72,1]{1,0:T(8,128)S(1)} %get-tuple-element.53.weight_ref, bf16[72,1792]{1,0:T(8,128)(2,1)S(1)} %add_convert_fusion.5.refs_0_, bf16[72,1792]{1,0:T(8,128)(2,1)S(1)} %collective-permute-done.22.refs_1_, ...), custom_call_target="tpu_custom_call" | custom-call | tf_op jit(solution)/shard_map/combine/pallas_call | solution.py:344
  (27 shorter events, 0.6 us)
Async XLA Ops:
  2.7 5.7 %collective-permute-start = (bf16[72,1792]{1,0:T(8,128)(2,1)S(1)}, bf16[72,1792]{1,0:T(8,128)(2,1)S(1)}, u32[]{:S(2)}, u32[]{:S(2)}) collective-permute-start(bf16[72,1792]{1,0:T(8,128)(2,1)S(1)} %get-tuple-element.54), channel_id=1, source_target_pairs={{0,8},{1,9},{2,10},{3,11},{4,12},{5,13},{6,14},{7,15},{8,0},{9,1},... | collective-permute-start | bytes 774152 | tf_op jit(solution)/shard_map/own1/ppermute | solution.py:263
  3.2 16.1 %collective-permute-start.1 = (bf16[72,1792]{1,0:T(8,128)(2,1)S(1)}, bf16[72,1792]{1,0:T(8,128)(2,1)S(1)}, u32[]{:S(2)}, u32[]{:S(2)}) collective-permute-start(bf16[72,1792]{1,0:T(8,128)(2,1)S(1)} %get-tuple-element.60), channel_id=1, source_target_pairs={{0,4},{1,5},{2,6},{3,7},{4,0},{5,1},{6,2},{7,3},{8,12},{9,13},{10,... | collective-permute-start | bytes 774152 | tf_op jit(solution)/shard_map/far0/ppermute | solution.py:263
  6.9 12.5 %collective-permute-start.2 = (bf16[72,1792]{1,0:T(8,128)(2,1)S(1)}, bf16[72,1792]{1,0:T(8,128)(2,1)S(1)}, u32[]{:S(2)}, u32[]{:S(2)}) collective-permute-start(bf16[72,1792]{1,0:T(8,128)(2,1)S(1)} %get-tuple-element.66.refs_0_), channel_id=1, source_target_pairs={{0,1},{1,0},{2,3},{3,2},{4,5},{5,4},{6,7},{7,6},{8,9},{9,8},{10,11... | collective-permute-start | bytes 774152 | tf_op jit(solution)/shard_map/own_y0/ppermute | solution.py:263
  8.4 12.3 %collective-permute-start.3 = (bf16[72,1792]{1,0:T(8,128)(2,1)S(1)}, bf16[72,1792]{1,0:T(8,128)(2,1)S(1)}, u32[]{:S(2)}, u32[]{:S(2)}) collective-permute-start(bf16[72,1792]{1,0:T(8,128)(2,1)S(1)} %collective-permute-done.refs_4_), channel_id=1, source_target_pairs={{0,1},{1,0},{2,3},{3,2},{4,5},{5,4},{6,7},{7,6},{8,9},{9,8},{10,11... | collective-permute-start | bytes 774152 | tf_op jit(solution)/shard_map/own_y1/ppermute | solution.py:263
  8.9 13.3 %collective-permute-start.5 = (bf16[72,1792]{1,0:T(8,128)(2,1)S(1)}, bf16[72,1792]{1,0:T(8,128)(2,1)S(1)}, u32[]{:S(2)}, u32[]{:S(2)}) collective-permute-start(bf16[72,1792]{1,0:T(8,128)(2,1)S(1)} %get-tuple-element.66.refs_0_), channel_id=1, source_target_pairs={{0,2},{1,3},{2,0},{3,1},{4,6},{5,7},{6,4},{7,5},{8,10},{9,11},{10,... | collective-permute-start | bytes 774152 | tf_op jit(solution)/shard_map/own_z0/ppermute | solution.py:263
  17.9 10.7 %collective-permute-start.9 = (bf16[72,1792]{1,0:T(8,128)(2,1)S(1)}, bf16[72,1792]{1,0:T(8,128)(2,1)S(1)}, u32[]{:S(2)}, u32[]{:S(2)}) collective-permute-start(bf16[72,1792]{1,0:T(8,128)(2,1)S(1)} %collective-permute-done.refs_4_), channel_id=1, source_target_pairs={{0,2},{1,3},{2,0},{3,1},{4,6},{5,7},{6,4},{7,5},{8,10},{9,11},{10,... | collective-permute-start | bytes 774152 | tf_op jit(solution)/shard_map/own_z1/ppermute | solution.py:263
  20.7 10.1 %collective-permute-start.4 = (bf16[72,1792]{1,0:T(8,128)(2,1)S(1)}, bf16[72,1792]{1,0:T(8,128)(2,1)S(1)}, u32[]{:S(2)}, u32[]{:S(2)}) collective-permute-start(bf16[72,1792]{1,0:T(8,128)(2,1)S(1)} %collective-permute-done.1.refs_0_), channel_id=1, source_target_pairs={{0,1},{1,0},{2,3},{3,2},{4,5},{5,4},{6,7},{7,6},{8,9},{9,8},{10,11... | collective-permute-start | bytes 774152 | tf_op jit(solution)/shard_map/far0_y/ppermute | solution.py:263
  22.2 14.3 %collective-permute-start.12 = (bf16[72,1792]{1,0:T(8,128)(2,1)S(1)}, bf16[72,1792]{1,0:T(8,128)(2,1)S(1)}, u32[]{:S(2)}, u32[]{:S(2)}) collective-permute-start(bf16[72,1792]{1,0:T(8,128)(2,1)S(1)} %get-tuple-element.73), channel_id=1, source_target_pairs={{0,12},{1,13},{2,14},{3,15},{4,8},{5,9},{6,10},{7,11},{8,4},{9,5},... | collective-permute-start | bytes 774152 | tf_op jit(solution)/shard_map/far1/ppermute | solution.py:263
  22.2 16.4 %collective-permute-start.6 = (bf16[72,1792]{1,0:T(8,128)(2,1)S(1)}, bf16[72,1792]{1,0:T(8,128)(2,1)S(1)}, u32[]{:S(2)}, u32[]{:S(2)}) collective-permute-start(bf16[72,1792]{1,0:T(8,128)(2,1)S(1)} %collective-permute-done.1.refs_0_), channel_id=1, source_target_pairs={{0,2},{1,3},{2,0},{3,1},{4,6},{5,7},{6,4},{7,5},{8,10},{9,11},{10,... | collective-permute-start | bytes 774152 | tf_op jit(solution)/shard_map/far0_z/ppermute | solution.py:263
  28.6 10.0 %collective-permute-start.10 = (bf16[72,1792]{1,0:T(8,128)(2,1)S(1)}, bf16[72,1792]{1,0:T(8,128)(2,1)S(1)}, u32[]{:S(2)}, u32[]{:S(2)}) collective-permute-start(bf16[72,1792]{1,0:T(8,128)(2,1)S(1)} %collective-permute-done.9.refs_6_), channel_id=1, source_target_pairs={{0,1},{1,0},{2,3},{3,2},{4,5},{5,4},{6,7},{7,6},{8,9},{9,8},{10,11... | collective-permute-start | bytes 774152 | tf_op jit(solution)/shard_map/own_d1/ppermute | solution.py:263
  30.8 13.4 %collective-permute-start.7 = (bf16[72,1792]{1,0:T(8,128)(2,1)S(1)}, bf16[72,1792]{1,0:T(8,128)(2,1)S(1)}, u32[]{:S(2)}, u32[]{:S(2)}) collective-permute-start(bf16[72,1792]{1,0:T(8,128)(2,1)S(1)} %collective-permute-done.4.refs_1_), channel_id=1, source_target_pairs={{0,2},{1,3},{2,0},{3,1},{4,6},{5,7},{6,4},{7,5},{8,10},{9,11},{10,... | collective-permute-start | bytes 774152 | tf_op jit(solution)/shard_map/far0_d/ppermute | solution.py:263
  30.8 19.0 %collective-permute-start.8 = (bf16[72,1792]{1,0:T(8,128)(2,1)S(1)}, bf16[72,1792]{1,0:T(8,128)(2,1)S(1)}, u32[]{:S(2)}, u32[]{:S(2)}) collective-permute-start(bf16[72,1792]{1,0:T(8,128)(2,1)S(1)} %collective-permute-done.5.refs_2_), channel_id=1, source_target_pairs={{0,1},{1,0},{2,3},{3,2},{4,5},{5,4},{6,7},{7,6},{8,9},{9,8},{10,11... | collective-permute-start | bytes 774152 | tf_op jit(solution)/shard_map/own_d0/ppermute | solution.py:263
  38.6 24.1 %collective-permute-start.13 = (bf16[72,1792]{1,0:T(8,128)(2,1)S(1)}, bf16[72,1792]{1,0:T(8,128)(2,1)S(1)}, u32[]{:S(2)}, u32[]{:S(2)}) collective-permute-start(bf16[72,1792]{1,0:T(8,128)(2,1)S(1)} %collective-permute-done.12.refs_0_), channel_id=1, source_target_pairs={{0,1},{1,0},{2,3},{3,2},{4,5},{5,4},{6,7},{7,6},{8,9},{9,8},{10,11... | collective-permute-start | bytes 774152 | tf_op jit(solution)/shard_map/far1_y/ppermute | solution.py:263
  40.2 9.6 %collective-permute-start.14 = (bf16[72,1792]{1,0:T(8,128)(2,1)S(1)}, bf16[72,1792]{1,0:T(8,128)(2,1)S(1)}, u32[]{:S(2)}, u32[]{:S(2)}) collective-permute-start(bf16[72,1792]{1,0:T(8,128)(2,1)S(1)} %collective-permute-done.12.refs_0_), channel_id=1, source_target_pairs={{0,2},{1,3},{2,0},{3,1},{4,6},{5,7},{6,4},{7,5},{8,10},{9,11},{10,... | collective-permute-start | bytes 774152 | tf_op jit(solution)/shard_map/far1_z/ppermute | solution.py:263
  48.1 9.2 %collective-permute-start.16 = (bf16[72,1792]{1,0:T(8,128)(2,1)S(1)}, bf16[72,1792]{1,0:T(8,128)(2,1)S(1)}, u32[]{:S(2)}, u32[]{:S(2)}) collective-permute-start(bf16[72,1792]{1,0:T(8,128)(2,1)S(1)} %get-tuple-element.80), channel_id=1, source_target_pairs={{0,1},{1,0},{2,3},{3,2},{4,5},{5,4},{6,7},{7,6},{8,9},{9,8},{10,11... | collective-permute-start | bytes 774152 | tf_op jit(solution)/shard_map/back0_d/ppermute | solution.py:263
  49.8 12.9 %collective-permute-start.15 = (bf16[72,1792]{1,0:T(8,128)(2,1)S(1)}, bf16[72,1792]{1,0:T(8,128)(2,1)S(1)}, u32[]{:S(2)}, u32[]{:S(2)}) collective-permute-start(bf16[72,1792]{1,0:T(8,128)(2,1)S(1)} %collective-permute-done.14.refs_2_), channel_id=1, source_target_pairs={{0,1},{1,0},{2,3},{3,2},{4,5},{5,4},{6,7},{7,6},{8,9},{9,8},{10,11... | collective-permute-start | bytes 774152 | tf_op jit(solution)/shard_map/far1_d/ppermute | solution.py:263
  53.8 15.0 %collective-permute-start.11 = (bf16[72,1792]{1,0:T(8,128)(2,1)S(1)}, bf16[72,1792]{1,0:T(8,128)(2,1)S(1)}, u32[]{:S(2)}, u32[]{:S(2)}) collective-permute-start(bf16[72,1792]{1,0:T(8,128)(2,1)S(1)} %get-tuple-element.71), channel_id=1, source_target_pairs={{0,2},{1,3},{2,0},{3,1},{4,6},{5,7},{6,4},{7,5},{8,10},{9,11},{10,... | collective-permute-start | bytes 774152 | tf_op jit(solution)/shard_map/mine_d0/ppermute | solution.py:263
  57.4 11.5 %collective-permute-start.17 = (bf16[72,1792]{1,0:T(8,128)(2,1)S(1)}, bf16[72,1792]{1,0:T(8,128)(2,1)S(1)}, u32[]{:S(2)}, u32[]{:S(2)}) collective-permute-start(bf16[72,1792]{1,0:T(8,128)(2,1)S(1)} %get-tuple-element.81), channel_id=1, source_target_pairs={{0,1},{1,0},{2,3},{3,2},{4,5},{5,4},{6,7},{7,6},{8,9},{9,8},{10,11... | collective-permute-start | bytes 774152 | tf_op jit(solution)/shard_map/back0_y/ppermute | solution.py:263
  59.0 9.9 %collective-permute-start.20 = (bf16[72,1792]{1,0:T(8,128)(2,1)S(1)}, bf16[72,1792]{1,0:T(8,128)(2,1)S(1)}, u32[]{:S(2)}, u32[]{:S(2)}) collective-permute-start(bf16[72,1792]{1,0:T(8,128)(2,1)S(1)} %add_convert_fusion.6), channel_id=1, source_target_pairs={{0,2},{1,3},{2,0},{3,1},{4,6},{5,7},{6,4},{7,5},{8,10},{9,11},{10,... | collective-permute-start | bytes 774152 | tf_op jit(solution)/shard_map/back0_z/ppermute | solution.py:263
  66.7 9.2 %collective-permute-start.26 = (bf16[72,1792]{1,0:T(8,128)(2,1)S(1)}, bf16[72,1792]{1,0:T(8,128)(2,1)S(1)}, u32[]{:S(2)}, u32[]{:S(2)}) collective-permute-start(bf16[72,1792]{1,0:T(8,128)(2,1)S(1)} %get-tuple-element.95), channel_id=1, source_target_pairs={{0,1},{1,0},{2,3},{3,2},{4,5},{5,4},{6,7},{7,6},{8,9},{9,8},{10,11... | collective-permute-start | bytes 774152 | tf_op jit(solution)/shard_map/back1_d/ppermute | solution.py:263
  68.3 11.0 %collective-permute-start.24 = (bf16[72,1792]{1,0:T(8,128)(2,1)S(1)}, bf16[72,1792]{1,0:T(8,128)(2,1)S(1)}, u32[]{:S(2)}, u32[]{:S(2)}) collective-permute-start(bf16[72,1792]{1,0:T(8,128)(2,1)S(1)} %get-tuple-element.92), channel_id=1, source_target_pairs={{0,1},{1,0},{2,3},{3,2},{4,5},{5,4},{6,7},{7,6},{8,9},{9,8},{10,11... | collective-permute-start | bytes 774152 | tf_op jit(solution)/shard_map/mine_d1/ppermute | solution.py:263
  69.0 29.8 %collective-permute-start.22 = (bf16[72,1792]{1,0:T(8,128)(2,1)S(1)}, bf16[72,1792]{1,0:T(8,128)(2,1)S(1)}, u32[]{:S(2)}, u32[]{:S(2)}) collective-permute-start(bf16[72,1792]{1,0:T(8,128)(2,1)S(1)} %add_convert_fusion.4), channel_id=1, source_target_pairs={{0,4},{1,5},{2,6},{3,7},{4,0},{5,1},{6,2},{7,3},{8,12},{9,13},{10,... | collective-permute-start | bytes 774152 | tf_op jit(solution)/shard_map/back0/ppermute | solution.py:263
  70.2 14.0 %collective-permute-start.18 = (bf16[72,1792]{1,0:T(8,128)(2,1)S(1)}, bf16[72,1792]{1,0:T(8,128)(2,1)S(1)}, u32[]{:S(2)}, u32[]{:S(2)}) collective-permute-start(bf16[72,1792]{1,0:T(8,128)(2,1)S(1)} %get-tuple-element.82), channel_id=1, source_target_pairs={{0,1},{1,0},{2,3},{3,2},{4,5},{5,4},{6,7},{7,6},{8,9},{9,8},{10,11... | collective-permute-start | bytes 774152 | tf_op jit(solution)/shard_map/back1_y/ppermute | solution.py:263
  76.0 9.7 %collective-permute-start.27 = (bf16[72,1792]{1,0:T(8,128)(2,1)S(1)}, bf16[72,1792]{1,0:T(8,128)(2,1)S(1)}, u32[]{:S(2)}, u32[]{:S(2)}) collective-permute-start(bf16[72,1792]{1,0:T(8,128)(2,1)S(1)} %add_convert_fusion.1), channel_id=1, source_target_pairs={{0,2},{1,3},{2,0},{3,1},{4,6},{5,7},{6,4},{7,5},{8,10},{9,11},{10,... | collective-permute-start | bytes 774152 | tf_op jit(solution)/shard_map/back1_z/ppermute | solution.py:263
  79.4 13.0 %collective-permute-start.25 = (bf16[72,1792]{1,0:T(8,128)(2,1)S(1)}, bf16[72,1792]{1,0:T(8,128)(2,1)S(1)}, u32[]{:S(2)}, u32[]{:S(2)}) collective-permute-start(bf16[72,1792]{1,0:T(8,128)(2,1)S(1)} %add_convert_fusion.3), channel_id=1, source_target_pairs={{0,2},{1,3},{2,0},{3,1},{4,6},{5,7},{6,4},{7,5},{8,10},{9,11},{10,... | collective-permute-start | bytes 774152 | tf_op jit(solution)/shard_map/mine_z1/ppermute | solution.py:263
  79.6 16.3 %collective-permute-start.21 = (bf16[72,1792]{1,0:T(8,128)(2,1)S(1)}, bf16[72,1792]{1,0:T(8,128)(2,1)S(1)}, u32[]{:S(2)}, u32[]{:S(2)}) collective-permute-start(bf16[72,1792]{1,0:T(8,128)(2,1)S(1)} %get-tuple-element.86), channel_id=1, source_target_pairs={{0,2},{1,3},{2,0},{3,1},{4,6},{5,7},{6,4},{7,5},{8,10},{9,11},{10,... | collective-permute-start | bytes 774152 | tf_op jit(solution)/shard_map/mine_z0/ppermute | solution.py:263
  84.3 8.1 %collective-permute-start.23 = (bf16[72,1792]{1,0:T(8,128)(2,1)S(1)}, bf16[72,1792]{1,0:T(8,128)(2,1)S(1)}, u32[]{:S(2)}, u32[]{:S(2)}) collective-permute-start(bf16[72,1792]{1,0:T(8,128)(2,1)S(1)} %get-tuple-element.89), channel_id=1, source_target_pairs={{0,1},{1,0},{2,3},{3,2},{4,5},{5,4},{6,7},{7,6},{8,9},{9,8},{10,11... | collective-permute-start | bytes 774152 | tf_op jit(solution)/shard_map/mine_y1/ppermute | solution.py:263
  85.8 13.6 %collective-permute-start.29 = (bf16[72,1792]{1,0:T(8,128)(2,1)S(1)}, bf16[72,1792]{1,0:T(8,128)(2,1)S(1)}, u32[]{:S(2)}, u32[]{:S(2)}) collective-permute-start(bf16[72,1792]{1,0:T(8,128)(2,1)S(1)} %add_convert_fusion), channel_id=1, source_target_pairs={{0,12},{1,13},{2,14},{3,15},{4,8},{5,9},{6,10},{7,11},{8,4},{9,5},... | collective-permute-start | bytes 774152 | tf_op jit(solution)/shard_map/back1/ppermute | solution.py:263
  92.4 6.3 %collective-permute-start.19 = (bf16[72,1792]{1,0:T(8,128)(2,1)S(1)}, bf16[72,1792]{1,0:T(8,128)(2,1)S(1)}, u32[]{:S(2)}, u32[]{:S(2)}) collective-permute-start(bf16[72,1792]{1,0:T(8,128)(2,1)S(1)} %add_convert_fusion.7), channel_id=1, source_target_pairs={{0,1},{1,0},{2,3},{3,2},{4,5},{5,4},{6,7},{7,6},{8,9},{9,8},{10,11... | collective-permute-start | bytes 774152 | tf_op jit(solution)/shard_map/mine_y0/ppermute | solution.py:263
  92.5 6.9 %collective-permute-start.28 = (bf16[72,1792]{1,0:T(8,128)(2,1)S(1)}, bf16[72,1792]{1,0:T(8,128)(2,1)S(1)}, u32[]{:S(2)}, u32[]{:S(2)}) collective-permute-start(bf16[72,1792]{1,0:T(8,128)(2,1)S(1)} %add_convert_fusion.2), channel_id=1, source_target_pairs={{0,8},{1,9},{2,10},{3,11},{4,12},{5,13},{6,14},{7,15},{8,0},{9,1},... | collective-permute-start | bytes 774152 | tf_op jit(solution)/shard_map/home1/ppermute | solution.py:263

commit v6 on v5

--- a/solution.py
+++ b/solution.py
@@ -11,7 +11,7 @@
 STACK = 4
 COST = 15
 
-HOPS = {"own": "yy", "far": "zy", "mine": "zy", "back": "yy"}
+HOPS = {"own": "yy", "far": "zy", "mine": "zy", "back": "zy"}
 
 AFTER = {
     "load": ("own1",),
@@ -28,12 +28,13 @@
     "far1_z": ("far0_z",),
     "own_experts": ("far0_experts",),
     "back0_y": ("back0_d",),
+    "back0_z": ("back0_d",),
     "back1_y": ("back0_y",),
     "back1_z": ("back0_z",),
     "mine_d1": ("far1_d",),
     "mine_y0": ("back1_y",),
     "mine_y1": ("back1_y",),
-    "mine_z0": ("back0_z",),
+    "mine_z0": ("back1_z",),
     "mine_z1": ("back0_z",),
     "home1": ("back1_z",),
 }

time: 101 us -> 99.4 us (0.984)
  waiting for transfers between devices: 48.9 us -> 41.9 us
  starting transfers between devices: 28 us -> 33 us
    ppermute x30, waiting for transfers between devices: 48.9 us -> 41.9 us  [send(): return lax.ppermute(value, ('node', 'local'), pairs)]
    ppermute x30, starting transfers between devices: 28 us -> 33 us  [send(): return lax.ppermute(value, ('node', 'local'), pairs)]
  transfers between devices with their start and end apart: 30 -> 30, of which waited for: 15 -> 17; matrix products, arithmetic and copies ran while one was open for 1% -> 1% of each run, Pallas kernels for 19% -> 19%
where the time goes in v6:
time: 99.4 us; the launch traced here: 99.1 us
  waiting for transfers between devices  41.9 us (42%)
  starting transfers between devices  33 us (33%)
  Pallas kernels  23.3 us (23%)
    ppermute x30, waiting for transfers between devices, send(): return lax.ppermute(value, ('node', 'local'), pairs)  41.9 us
    ppermute x30, starting transfers between devices, send(): return lax.ppermute(value, ('node', 'local'), pairs)  33 us
    pallas_call x3, Pallas kernels, experts(): pl.pallas_call(expert_kernel, out_shape=[block] * len(blocks), in_specs=[...  11.6 us
    pallas_call x1, Pallas kernels, load(): pl.pallas_call(load_kernel, out_shape=[pltpu.VMEM((STACK, width, hidden_w...  7.44 us
    pallas_call x1, Pallas kernels, local(): pl.pallas_call(pack_kernel, out_shape=[block] * flight + [jax.ShapeDtypeS...  2.61 us
  transfers between devices with their start and end apart: 30, of which 17 were waited for; matrix products, arithmetic and copies ran while one was open for 1% of the time, Pallas kernels for 19%

profile of v6, /device:TPU:0, one launch (start us, length us, event | category | flops | bytes accessed | tf_op | source)
XLA Modules:
  0.0 99.1 jit_solution(11667831827714226424)
XLA Ops:
  0.1 2.6 %pack.1 = (bf16[72,1792]{1,0:T(8,128)(2,1)S(1)}, bf16[72,1792]{1,0:T(8,128)(2,1)S(1)}, bf16[72,1792]{1,0:T(8,128)(2,1)S(1)}, bf16[72,1792]{1,0:T(8,128)(2,1)S(1)...) custom-call(s32[4]{0:T(128)S(1)} %pad_add_fusion.flight_ref, s32[8,144]{1,0:T(8,128)} %bitcast.6, f32[8,144]{1,0:T(8,128)} %bitcast.7, ...), custom_call_target="tpu_custom_call" | custom-call | tf_op jit(solution)/shard_map/pack/pallas_call | solution.py:199
  2.7 0.5 collective-permute-start
  3.2 3.7 %collective-permute-start.1 = (bf16[72,1792]{1,0:T(8,128)(2,1)S(1)}, bf16[72,1792]{1,0:T(8,128)(2,1)S(1)}, u32[]{:S(2)}, u32[]{:S(2)}) collective-permute-start(bf16[72,1792]{1,0:T(8,128)(2,1)S(1)} %get-tuple-element.61), channel_id=1, source_target_pairs={{0,4},{1,5},{2,6},{3,7},{4,0},{5,1},{6,2},{7,3},{8,12},{9,13},{10,... | collective-permute-start | bytes 774152 | tf_op jit(solution)/shard_map/far0/ppermute | solution.py:264
  6.9 1.5 %collective-permute-start.2 = (bf16[72,1792]{1,0:T(8,128)(2,1)S(1)}, bf16[72,1792]{1,0:T(8,128)(2,1)S(1)}, u32[]{:S(2)}, u32[]{:S(2)}) collective-permute-start(bf16[72,1792]{1,0:T(8,128)(2,1)S(1)} %get-tuple-element.67.refs_0_), channel_id=1, source_target_pairs={{0,1},{1,0},{2,3},{3,2},{4,5},{5,4},{6,7},{7,6},{8,9},{9,8},{10,11... | collective-permute-start | bytes 774152 | tf_op jit(solution)/shard_map/own_y0/ppermute | solution.py:264
  8.4 0.5 collective-permute-start.3
  8.9 1.6 %collective-permute-start.5 = (bf16[72,1792]{1,0:T(8,128)(2,1)S(1)}, bf16[72,1792]{1,0:T(8,128)(2,1)S(1)}, u32[]{:S(2)}, u32[]{:S(2)}) collective-permute-start(bf16[72,1792]{1,0:T(8,128)(2,1)S(1)} %get-tuple-element.67.refs_0_), channel_id=1, source_target_pairs={{0,2},{1,3},{2,0},{3,1},{4,6},{5,7},{6,4},{7,5},{8,10},{9,11},{10,... | collective-permute-start | bytes 774152 | tf_op jit(solution)/shard_map/own_z0/ppermute | solution.py:264
  10.5 7.4 %load.1 = (bf16[4,1792,512]{2,1,0:T(8,128)(2,1)S(1)}, bf16[4,1792,512]{2,1,0:T(8,128)(2,1)S(1)}, bf16[4,512,1792]{2,1,0:T(8,128)(2,1)S(1)}) custom-call(bf16[1,7168,512]{2,1,0:T(8,128)(2,1)} %gate_hbm, bf16[1,7168,512]{2,1,0:T(8,128)(2,1)} %up_hbm.1, bf16[1,512,7168]{2,1,0:T(8,128)(2,1)} %down_hbm.1), custom_call_target="tpu_custom_call" | custom-call | bytes 55050240 | tf_op jit(solution)/shard_map/load/load/pallas_call | solution.py:221
  17.9 0.5 collective-permute-start.9
  18.5 0.9 collective-permute-done.1.refs_0_
  19.3 1.4 %collective-permute-done.3.refs_5_ = bf16[72,1792]{1,0:T(8,128)(2,1)S(1)} collective-permute-done((bf16[72,1792]{1,0:T(8,128)(2,1)S(1)}, bf16[72,1792]{1,0:T(8,128)(2,1)S(1)}, u32[]{:S(2)}, u32[]{:S(2)}) %collective-permute-start.3) | collective-permute-done | bytes 258080 | tf_op jit(solution)/shard_map/own_y1/ppermute | solution.py:264
  20.7 1.5 %collective-permute-start.4 = (bf16[72,1792]{1,0:T(8,128)(2,1)S(1)}, bf16[72,1792]{1,0:T(8,128)(2,1)S(1)}, u32[]{:S(2)}, u32[]{:S(2)}) collective-permute-start(bf16[72,1792]{1,0:T(8,128)(2,1)S(1)} %collective-permute-done.1.refs_0_), channel_id=1, source_target_pairs={{0,1},{1,0},{2,3},{3,2},{4,5},{5,4},{6,7},{7,6},{8,9},{9,8},{10,11... | collective-permute-start | bytes 774152 | tf_op jit(solution)/shard_map/far0_y/ppermute | solution.py:264
  22.2 2.1 %collective-permute-start.6 = (bf16[72,1792]{1,0:T(8,128)(2,1)S(1)}, bf16[72,1792]{1,0:T(8,128)(2,1)S(1)}, u32[]{:S(2)}, u32[]{:S(2)}) collective-permute-start(bf16[72,1792]{1,0:T(8,128)(2,1)S(1)} %collective-permute-done.1.refs_0_), channel_id=1, source_target_pairs={{0,2},{1,3},{2,0},{3,1},{4,6},{5,7},{6,4},{7,5},{8,10},{9,11},{10,... | collective-permute-start | bytes 774152 | tf_op jit(solution)/shard_map/far0_z/ppermute | solution.py:264
  24.3 4.3 %collective-permute-done.9.refs_6_ = bf16[72,1792]{1,0:T(8,128)(2,1)S(1)} collective-permute-done((bf16[72,1792]{1,0:T(8,128)(2,1)S(1)}, bf16[72,1792]{1,0:T(8,128)(2,1)S(1)}, u32[]{:S(2)}, u32[]{:S(2)}) %collective-permute-start.9) | collective-permute-done | bytes 258080 | tf_op jit(solution)/shard_map/own_z1/ppermute | solution.py:264
  28.6 2.2 %collective-permute-start.10 = (bf16[72,1792]{1,0:T(8,128)(2,1)S(1)}, bf16[72,1792]{1,0:T(8,128)(2,1)S(1)}, u32[]{:S(2)}, u32[]{:S(2)}) collective-permute-start(bf16[72,1792]{1,0:T(8,128)(2,1)S(1)} %collective-permute-done.9.refs_6_), channel_id=1, source_target_pairs={{0,1},{1,0},{2,3},{3,2},{4,5},{5,4},{6,7},{7,6},{8,9},{9,8},{10,11... | collective-permute-start | bytes 774152 | tf_op jit(solution)/shard_map/own_d1/ppermute | solution.py:264
  30.8 0.8 collective-permute-start.8
  31.5 5.0 %collective-permute-done.12.refs_0_ = bf16[72,1792]{1,0:T(8,128)(2,1)S(1)} collective-permute-done((bf16[72,1792]{1,0:T(8,128)(2,1)S(1)}, bf16[72,1792]{1,0:T(8,128)(2,1)S(1)}, u32[]{:S(2)}, u32[]{:S(2)}) %collective-permute-start.12) | collective-permute-done | bytes 258080 | tf_op jit(solution)/shard_map/far1/ppermute | solution.py:264
  36.6 2.1 %collective-permute-done.6.refs_2_ = bf16[72,1792]{1,0:T(8,128)(2,1)S(1)} collective-permute-done((bf16[72,1792]{1,0:T(8,128)(2,1)S(1)}, bf16[72,1792]{1,0:T(8,128)(2,1)S(1)}, u32[]{:S(2)}, u32[]{:S(2)}) %collective-permute-start.6) | collective-permute-done | bytes 258080 | tf_op jit(solution)/shard_map/far0_z/ppermute | solution.py:264
  38.6 1.6 %collective-permute-start.13 = (bf16[72,1792]{1,0:T(8,128)(2,1)S(1)}, bf16[72,1792]{1,0:T(8,128)(2,1)S(1)}, u32[]{:S(2)}, u32[]{:S(2)}) collective-permute-start(bf16[72,1792]{1,0:T(8,128)(2,1)S(1)} %collective-permute-done.12.refs_0_), channel_id=1, source_target_pairs={{0,1},{1,0},{2,3},{3,2},{4,5},{5,4},{6,7},{7,6},{8,9},{9,8},{10,11... | collective-permute-start | bytes 774152 | tf_op jit(solution)/shard_map/far1_y/ppermute | solution.py:264
  40.2 3.9 %collective-permute-done.7.refs_3_ = bf16[72,1792]{1,0:T(8,128)(2,1)S(1)} collective-permute-done((bf16[72,1792]{1,0:T(8,128)(2,1)S(1)}, bf16[72,1792]{1,0:T(8,128)(2,1)S(1)}, u32[]{:S(2)}, u32[]{:S(2)}) %collective-permute-start.7) | collective-permute-done | bytes 258080 | tf_op jit(solution)/shard_map/far0_d/ppermute | solution.py:264
  44.1 4.0 %experts.3 = (bf16[72,1792]{1,0:T(8,128)(2,1)S(1)}, bf16[72,1792]{1,0:T(8,128)(2,1)S(1)}, bf16[72,1792]{1,0:T(8,128)(2,1)S(1)}, bf16[72,1792]{1,0:T(8,128)(2,1)S(1)}) custom-call(bf16[4,1792,512]{2,1,0:T(8,128)(2,1)S(1)} %get-tuple-element.57.gate, bf16[4,1792,512]{2,1,0:T(8,128)(2,1)S(1)} %get-tuple-element.58.up, ...), custom_call_target="tpu_custom_call" | custom-call | flops 3963617280 | bytes 55050240 | tf_op jit(solution)/shard_map/far0_experts/experts/pallas_call | solution.py:238
  48.2 0.4 collective-permute-done.14.refs_2_
  48.7 1.6 %collective-permute-start.15 = (bf16[72,1792]{1,0:T(8,128)(2,1)S(1)}, bf16[72,1792]{1,0:T(8,128)(2,1)S(1)}, u32[]{:S(2)}, u32[]{:S(2)}) collective-permute-start(bf16[72,1792]{1,0:T(8,128)(2,1)S(1)} %collective-permute-done.14.refs_2_), channel_id=1, source_target_pairs={{0,1},{1,0},{2,3},{3,2},{4,5},{5,4},{6,7},{7,6},{8,9},{9,8},{10,11... | collective-permute-start | bytes 774152 | tf_op jit(solution)/shard_map/far1_d/ppermute | solution.py:264
  50.2 3.6 %experts.4 = (bf16[72,1792]{1,0:T(8,128)(2,1)S(1)}, bf16[72,1792]{1,0:T(8,128)(2,1)S(1)}, bf16[72,1792]{1,0:T(8,128)(2,1)S(1)}, bf16[72,1792]{1,0:T(8,128)(2,1)S...) custom-call(bf16[4,1792,512]{2,1,0:T(8,128)(2,1)S(1)} %get-tuple-ele, ...), custom_call_target="tpu_custom_call" | custom-call | flops 7927234560 | bytes 55050240 | tf_op jit(solution)/shard_map/own_experts/experts/pallas_call | solution.py:238
  53.8 1.7 %collective-permute-start.11 = (bf16[72,1792]{1,0:T(8,128)(2,1)S(1)}, bf16[72,1792]{1,0:T(8,128)(2,1)S(1)}, u32[]{:S(2)}, u32[]{:S(2)}) collective-permute-start(bf16[72,1792]{1,0:T(8,128)(2,1)S(1)} %get-tuple-element.72), channel_id=1, source_target_pairs={{0,2},{1,3},{2,0},{3,1},{4,6},{5,7},{6,4},{7,5},{8,10},{9,11},{10,... | collective-permute-start | bytes 774152 | tf_op jit(solution)/shard_map/mine_d0/ppermute | solution.py:264
  55.6 0.5 collective-permute-start.21
  56.0 0.6 collective-permute-start.17
  56.7 4.0 %experts.5 = (bf16[72,1792]{1,0:T(8,128)(2,1)S(1)}, bf16[72,1792]{1,0:T(8,128)(2,1)S(1)}, bf16[72,1792]{1,0:T(8,128)(2,1)S(1)}, bf16[72,1792]{1,0:T(8,128)(2,1)S(1)}) custom-call(bf16[4,1792,512]{2,1,0:T(8,128)(2,1)S(1)} %get-tuple-element.57.gate, bf16[4,1792,512]{2,1,0:T(8,128)(2,1)S(1)} %get-tuple-element.58.up, ...), custom_call_target="tpu_custom_call" | custom-call | flops 3963617280 | bytes 55050240 | tf_op jit(solution)/shard_map/far1_experts/experts/pallas_call | solution.py:238
  60.7 1.4 %collective-permute-start.20 = (bf16[72,1792]{1,0:T(8,128)(2,1)S(1)}, bf16[72,1792]{1,0:T(8,128)(2,1)S(1)}, u32[]{:S(2)}, u32[]{:S(2)}) collective-permute-start(bf16[72,1792]{1,0:T(8,128)(2,1)S(1)} %get-tuple-element.87), channel_id=1, source_target_pairs={{0,1},{1,0},{2,3},{3,2},{4,5},{5,4},{6,7},{7,6},{8,9},{9,8},{10,11... | collective-permute-start | bytes 774152 | tf_op jit(solution)/shard_map/back1_d/ppermute | solution.py:264
  62.1 0.6 collective-permute-start.26
  62.8 0.3 collective-permute-done.11
  63.1 3.2 %collective-permute-done.21 = bf16[72,1792]{1,0:T(8,128)(2,1)S(1)} collective-permute-done((bf16[72,1792]{1,0:T(8,128)(2,1)S(1)}, bf16[72,1792]{1,0:T(8,128)(2,1)S(1)}, u32[]{:S(2)}, u32[]{:S(2)}) %collective-permute-start.21) | collective-permute-done | bytes 258080 | tf_op jit(solution)/shard_map/back0_z/ppermute | solution.py:264
  66.3 0.1 add_convert_fusion.3
  66.4 1.8 %collective-permute-start.24 = (bf16[72,1792]{1,0:T(8,128)(2,1)S(1)}, bf16[72,1792]{1,0:T(8,128)(2,1)S(1)}, u32[]{:S(2)}, u32[]{:S(2)}) collective-permute-start(bf16[72,1792]{1,0:T(8,128)(2,1)S(1)} %add_convert_fusion.3), channel_id=1, source_target_pairs={{0,4},{1,5},{2,6},{3,7},{4,0},{5,1},{6,2},{7,3},{8,12},{9,13},{10,... | collective-permute-start | bytes 774152 | tf_op jit(solution)/shard_map/back0/ppermute | solution.py:264
  68.2 0.7 collective-permute-start.18
  69.0 0.9 collective-permute-done.20
  70.0 2.1 %collective-permute-start.22 = (bf16[72,1792]{1,0:T(8,128)(2,1)S(1)}, bf16[72,1792]{1,0:T(8,128)(2,1)S(1)}, u32[]{:S(2)}, u32[]{:S(2)}) collective-permute-start(bf16[72,1792]{1,0:T(8,128)(2,1)S(1)} %add_convert_fusion.5), channel_id=1, source_target_pairs={{0,2},{1,3},{2,0},{3,1},{4,6},{5,7},{6,4},{7,5},{8,10},{9,11},{10,... | collective-permute-start | bytes 774152 | tf_op jit(solution)/shard_map/back1_z/ppermute | solution.py:264
  72.1 3.3 %collective-permute-done.26 = bf16[72,1792]{1,0:T(8,128)(2,1)S(1)} collective-permute-done((bf16[72,1792]{1,0:T(8,128)(2,1)S(1)}, bf16[72,1792]{1,0:T(8,128)(2,1)S(1)}, u32[]{:S(2)}, u32[]{:S(2)}) %collective-permute-start.26) | collective-permute-done | bytes 258080 | tf_op jit(solution)/shard_map/mine_d1/ppermute | solution.py:264
  75.5 2.1 %collective-permute-start.27 = (bf16[72,1792]{1,0:T(8,128)(2,1)S(1)}, bf16[72,1792]{1,0:T(8,128)(2,1)S(1)}, u32[]{:S(2)}, u32[]{:S(2)}) collective-permute-start(bf16[72,1792]{1,0:T(8,128)(2,1)S(1)} %add_convert_fusion.2), channel_id=1, source_target_pairs={{0,2},{1,3},{2,0},{3,1},{4,6},{5,7},{6,4},{7,5},{8,10},{9,11},{10,... | collective-permute-start | bytes 774152 | tf_op jit(solution)/shard_map/mine_z1/ppermute | solution.py:264
  77.6 1.3 %collective-permute-done.18 = bf16[72,1792]{1,0:T(8,128)(2,1)S(1)} collective-permute-done((bf16[72,1792]{1,0:T(8,128)(2,1)S(1)}, bf16[72,1792]{1,0:T(8,128)(2,1)S(1)}, u32[]{:S(2)}, u32[]{:S(2)}) %collective-permute-start.18) | collective-permute-done | bytes 258080 | tf_op jit(solution)/shard_map/back1_y/ppermute | solution.py:264
  79.0 0.6 collective-permute-start.25
  79.6 3.0 %collective-permute-done.22 = bf16[72,1792]{1,0:T(8,128)(2,1)S(1)} collective-permute-done((bf16[72,1792]{1,0:T(8,128)(2,1)S(1)}, bf16[72,1792]{1,0:T(8,128)(2,1)S(1)}, u32[]{:S(2)}, u32[]{:S(2)}) %collective-permute-start.22) | collective-permute-done | bytes 258080 | tf_op jit(solution)/shard_map/back1_z/ppermute | solution.py:264
  82.6 0.3 collective-permute-start.23
  83.1 7.6 %collective-permute-done.27 = bf16[72,1792]{1,0:T(8,128)(2,1)S(1)} collective-permute-done((bf16[72,1792]{1,0:T(8,128)(2,1)S(1)}, bf16[72,1792]{1,0:T(8,128)(2,1)S(1)}, u32[]{:S(2)}, u32[]{:S(2)}) %collective-permute-start.27) | collective-permute-done | bytes 258080 | tf_op jit(solution)/shard_map/mine_z1/ppermute | solution.py:264
  90.8 2.2 %collective-permute-start.19 = (bf16[72,1792]{1,0:T(8,128)(2,1)S(1)}, bf16[72,1792]{1,0:T(8,128)(2,1)S(1)}, u32[]{:S(2)}, u32[]{:S(2)}) collective-permute-start(bf16[72,1792]{1,0:T(8,128)(2,1)S(1)} %add_convert_fusion.7), channel_id=1, source_target_pairs={{0,1},{1,0},{2,3},{3,2},{4,5},{5,4},{6,7},{7,6},{8,9},{9,8},{10,11... | collective-permute-start | bytes 774152 | tf_op jit(solution)/shard_map/mine_y0/ppermute | solution.py:264
  92.9 0.1 add_convert_fusion.1
  93.1 2.0 %collective-permute-done.23 = bf16[72,1792]{1,0:T(8,128)(2,1)S(1)} collective-permute-done((bf16[72,1792]{1,0:T(8,128)(2,1)S(1)}, bf16[72,1792]{1,0:T(8,128)(2,1)S(1)}, u32[]{:S(2)}, u32[]{:S(2)}) %collective-permute-start.23) | collective-permute-done | bytes 258080 | tf_op jit(solution)/shard_map/mine_z0/ppermute | solution.py:264
  95.1 2.1 %collective-permute-done.19 = bf16[72,1792]{1,0:T(8,128)(2,1)S(1)} collective-permute-done((bf16[72,1792]{1,0:T(8,128)(2,1)S(1)}, bf16[72,1792]{1,0:T(8,128)(2,1)S(1)}, u32[]{:S(2)}, u32[]{:S(2)}) %collective-permute-start.19) | collective-permute-done | bytes 258080 | tf_op jit(solution)/shard_map/mine_y0/ppermute | solution.py:264
  97.4 1.7 %combine.1 = bf16[144,7168]{1,0:T(8,128)(2,1)} custom-call(bf16[72,144]{1,0:T(8,128)(2,1)S(1)} %get-tuple-element.53.pick_ref, f32[72,1]{1,0:T(8,128)S(1)} %get-tuple-element.54.weight_ref, bf16[72,1792]{1,0:T(8,128)(2,1)S(1)} %add_convert_fusion.4.refs_0_, bf16[72,1792]{1,0:T(8,128)(2,1)S(1)} %collective-permute-done.24.refs_1_, ...), custom_call_target="tpu_custom_call" | custom-call | tf_op jit(solution)/shard_map/combine/pallas_call | solution.py:345
  (27 shorter events, 0.9 us)
Async XLA Ops:
  2.7 5.7 %collective-permute-start = (bf16[72,1792]{1,0:T(8,128)(2,1)S(1)}, bf16[72,1792]{1,0:T(8,128)(2,1)S(1)}, u32[]{:S(2)}, u32[]{:S(2)}) collective-permute-start(bf16[72,1792]{1,0:T(8,128)(2,1)S(1)} %get-tuple-element.55), channel_id=1, source_target_pairs={{0,8},{1,9},{2,10},{3,11},{4,12},{5,13},{6,14},{7,15},{8,0},{9,1},... | collective-permute-start | bytes 774152 | tf_op jit(solution)/shard_map/own1/ppermute | solution.py:264
  3.2 16.1 %collective-permute-start.1 = (bf16[72,1792]{1,0:T(8,128)(2,1)S(1)}, bf16[72,1792]{1,0:T(8,128)(2,1)S(1)}, u32[]{:S(2)}, u32[]{:S(2)}) collective-permute-start(bf16[72,1792]{1,0:T(8,128)(2,1)S(1)} %get-tuple-element.61), channel_id=1, source_target_pairs={{0,4},{1,5},{2,6},{3,7},{4,0},{5,1},{6,2},{7,3},{8,12},{9,13},{10,... | collective-permute-start | bytes 774152 | tf_op jit(solution)/shard_map/far0/ppermute | solution.py:264
  6.9 12.5 %collective-permute-start.2 = (bf16[72,1792]{1,0:T(8,128)(2,1)S(1)}, bf16[72,1792]{1,0:T(8,128)(2,1)S(1)}, u32[]{:S(2)}, u32[]{:S(2)}) collective-permute-start(bf16[72,1792]{1,0:T(8,128)(2,1)S(1)} %get-tuple-element.67.refs_0_), channel_id=1, source_target_pairs={{0,1},{1,0},{2,3},{3,2},{4,5},{5,4},{6,7},{7,6},{8,9},{9,8},{10,11... | collective-permute-start | bytes 774152 | tf_op jit(solution)/shard_map/own_y0/ppermute | solution.py:264
  8.4 12.3 %collective-permute-start.3 = (bf16[72,1792]{1,0:T(8,128)(2,1)S(1)}, bf16[72,1792]{1,0:T(8,128)(2,1)S(1)}, u32[]{:S(2)}, u32[]{:S(2)}) collective-permute-start(bf16[72,1792]{1,0:T(8,128)(2,1)S(1)} %collective-permute-done.refs_4_), channel_id=1, source_target_pairs={{0,1},{1,0},{2,3},{3,2},{4,5},{5,4},{6,7},{7,6},{8,9},{9,8},{10,11... | collective-permute-start | bytes 774152 | tf_op jit(solution)/shard_map/own_y1/ppermute | solution.py:264
  8.9 13.3 %collective-permute-start.5 = (bf16[72,1792]{1,0:T(8,128)(2,1)S(1)}, bf16[72,1792]{1,0:T(8,128)(2,1)S(1)}, u32[]{:S(2)}, u32[]{:S(2)}) collective-permute-start(bf16[72,1792]{1,0:T(8,128)(2,1)S(1)} %get-tuple-element.67.refs_0_), channel_id=1, source_target_pairs={{0,2},{1,3},{2,0},{3,1},{4,6},{5,7},{6,4},{7,5},{8,10},{9,11},{10,... | collective-permute-start | bytes 774152 | tf_op jit(solution)/shard_map/own_z0/ppermute | solution.py:264
  17.9 10.7 %collective-permute-start.9 = (bf16[72,1792]{1,0:T(8,128)(2,1)S(1)}, bf16[72,1792]{1,0:T(8,128)(2,1)S(1)}, u32[]{:S(2)}, u32[]{:S(2)}) collective-permute-start(bf16[72,1792]{1,0:T(8,128)(2,1)S(1)} %collective-permute-done.refs_4_), channel_id=1, source_target_pairs={{0,2},{1,3},{2,0},{3,1},{4,6},{5,7},{6,4},{7,5},{8,10},{9,11},{10,... | collective-permute-start | bytes 774152 | tf_op jit(solution)/shard_map/own_z1/ppermute | solution.py:264
  20.7 10.1 %collective-permute-start.4 = (bf16[72,1792]{1,0:T(8,128)(2,1)S(1)}, bf16[72,1792]{1,0:T(8,128)(2,1)S(1)}, u32[]{:S(2)}, u32[]{:S(2)}) collective-permute-start(bf16[72,1792]{1,0:T(8,128)(2,1)S(1)} %collective-permute-done.1.refs_0_), channel_id=1, source_target_pairs={{0,1},{1,0},{2,3},{3,2},{4,5},{5,4},{6,7},{7,6},{8,9},{9,8},{10,11... | collective-permute-start | bytes 774152 | tf_op jit(solution)/shard_map/far0_y/ppermute | solution.py:264
  22.2 14.3 %collective-permute-start.12 = (bf16[72,1792]{1,0:T(8,128)(2,1)S(1)}, bf16[72,1792]{1,0:T(8,128)(2,1)S(1)}, u32[]{:S(2)}, u32[]{:S(2)}) collective-permute-start(bf16[72,1792]{1,0:T(8,128)(2,1)S(1)} %get-tuple-element.74), channel_id=1, source_target_pairs={{0,12},{1,13},{2,14},{3,15},{4,8},{5,9},{6,10},{7,11},{8,4},{9,5},... | collective-permute-start | bytes 774152 | tf_op jit(solution)/shard_map/far1/ppermute | solution.py:264
  22.2 16.4 %collective-permute-start.6 = (bf16[72,1792]{1,0:T(8,128)(2,1)S(1)}, bf16[72,1792]{1,0:T(8,128)(2,1)S(1)}, u32[]{:S(2)}, u32[]{:S(2)}) collective-permute-start(bf16[72,1792]{1,0:T(8,128)(2,1)S(1)} %collective-permute-done.1.refs_0_), channel_id=1, source_target_pairs={{0,2},{1,3},{2,0},{3,1},{4,6},{5,7},{6,4},{7,5},{8,10},{9,11},{10,... | collective-permute-start | bytes 774152 | tf_op jit(solution)/shard_map/far0_z/ppermute | solution.py:264
  28.6 10.0 %collective-permute-start.10 = (bf16[72,1792]{1,0:T(8,128)(2,1)S(1)}, bf16[72,1792]{1,0:T(8,128)(2,1)S(1)}, u32[]{:S(2)}, u32[]{:S(2)}) collective-permute-start(bf16[72,1792]{1,0:T(8,128)(2,1)S(1)} %collective-permute-done.9.refs_6_), channel_id=1, source_target_pairs={{0,1},{1,0},{2,3},{3,2},{4,5},{5,4},{6,7},{7,6},{8,9},{9,8},{10,11... | collective-permute-start | bytes 774152 | tf_op jit(solution)/shard_map/own_d1/ppermute | solution.py:264
  30.8 13.4 %collective-permute-start.7 = (bf16[72,1792]{1,0:T(8,128)(2,1)S(1)}, bf16[72,1792]{1,0:T(8,128)(2,1)S(1)}, u32[]{:S(2)}, u32[]{:S(2)}) collective-permute-start(bf16[72,1792]{1,0:T(8,128)(2,1)S(1)} %collective-permute-done.4.refs_1_), channel_id=1, source_target_pairs={{0,2},{1,3},{2,0},{3,1},{4,6},{5,7},{6,4},{7,5},{8,10},{9,11},{10,... | collective-permute-start | bytes 774152 | tf_op jit(solution)/shard_map/far0_d/ppermute | solution.py:264
  30.8 17.4 %collective-permute-start.8 = (bf16[72,1792]{1,0:T(8,128)(2,1)S(1)}, bf16[72,1792]{1,0:T(8,128)(2,1)S(1)}, u32[]{:S(2)}, u32[]{:S(2)}) collective-permute-start(bf16[72,1792]{1,0:T(8,128)(2,1)S(1)} %collective-permute-done.5.refs_2_), channel_id=1, source_target_pairs={{0,1},{1,0},{2,3},{3,2},{4,5},{5,4},{6,7},{7,6},{8,9},{9,8},{10,11... | collective-permute-start | bytes 774152 | tf_op jit(solution)/shard_map/own_d0/ppermute | solution.py:264
  38.6 18.1 %collective-permute-start.13 = (bf16[72,1792]{1,0:T(8,128)(2,1)S(1)}, bf16[72,1792]{1,0:T(8,128)(2,1)S(1)}, u32[]{:S(2)}, u32[]{:S(2)}) collective-permute-start(bf16[72,1792]{1,0:T(8,128)(2,1)S(1)} %collective-permute-done.12.refs_0_), channel_id=1, source_target_pairs={{0,1},{1,0},{2,3},{3,2},{4,5},{5,4},{6,7},{7,6},{8,9},{9,8},{10,11... | collective-permute-start | bytes 774152 | tf_op jit(solution)/shard_map/far1_y/ppermute | solution.py:264
  40.2 8.4 %collective-permute-start.14 = (bf16[72,1792]{1,0:T(8,128)(2,1)S(1)}, bf16[72,1792]{1,0:T(8,128)(2,1)S(1)}, u32[]{:S(2)}, u32[]{:S(2)}) collective-permute-start(bf16[72,1792]{1,0:T(8,128)(2,1)S(1)} %collective-permute-done.12.refs_0_), channel_id=1, source_target_pairs={{0,2},{1,3},{2,0},{3,1},{4,6},{5,7},{6,4},{7,5},{8,10},{9,11},{10,... | collective-permute-start | bytes 774152 | tf_op jit(solution)/shard_map/far1_z/ppermute | solution.py:264
  48.1 7.4 %collective-permute-start.16 = (bf16[72,1792]{1,0:T(8,128)(2,1)S(1)}, bf16[72,1792]{1,0:T(8,128)(2,1)S(1)}, u32[]{:S(2)}, u32[]{:S(2)}) collective-permute-start(bf16[72,1792]{1,0:T(8,128)(2,1)S(1)} %get-tuple-element.81), channel_id=1, source_target_pairs={{0,2},{1,3},{2,0},{3,1},{4,6},{5,7},{6,4},{7,5},{8,10},{9,11},{10,... | collective-permute-start | bytes 774152 | tf_op jit(solution)/shard_map/back0_d/ppermute | solution.py:264
  48.7 8.0 %collective-permute-start.15 = (bf16[72,1792]{1,0:T(8,128)(2,1)S(1)}, bf16[72,1792]{1,0:T(8,128)(2,1)S(1)}, u32[]{:S(2)}, u32[]{:S(2)}) collective-permute-start(bf16[72,1792]{1,0:T(8,128)(2,1)S(1)} %collective-permute-done.14.refs_2_), channel_id=1, source_target_pairs={{0,1},{1,0},{2,3},{3,2},{4,5},{5,4},{6,7},{7,6},{8,9},{9,8},{10,11... | collective-permute-start | bytes 774152 | tf_op jit(solution)/shard_map/far1_d/ppermute | solution.py:264
  53.8 9.2 %collective-permute-start.11 = (bf16[72,1792]{1,0:T(8,128)(2,1)S(1)}, bf16[72,1792]{1,0:T(8,128)(2,1)S(1)}, u32[]{:S(2)}, u32[]{:S(2)}) collective-permute-start(bf16[72,1792]{1,0:T(8,128)(2,1)S(1)} %get-tuple-element.72), channel_id=1, source_target_pairs={{0,2},{1,3},{2,0},{3,1},{4,6},{5,7},{6,4},{7,5},{8,10},{9,11},{10,... | collective-permute-start | bytes 774152 | tf_op jit(solution)/shard_map/mine_d0/ppermute | solution.py:264
  55.6 10.7 %collective-permute-start.21 = (bf16[72,1792]{1,0:T(8,128)(2,1)S(1)}, bf16[72,1792]{1,0:T(8,128)(2,1)S(1)}, u32[]{:S(2)}, u32[]{:S(2)}) collective-permute-start(bf16[72,1792]{1,0:T(8,128)(2,1)S(1)} %get-tuple-element.89), channel_id=1, source_target_pairs={{0,2},{1,3},{2,0},{3,1},{4,6},{5,7},{6,4},{7,5},{8,10},{9,11},{10,... | collective-permute-start | bytes 774152 | tf_op jit(solution)/shard_map/back0_z/ppermute | solution.py:264
  56.0 10.3 %collective-permute-start.17 = (bf16[72,1792]{1,0:T(8,128)(2,1)S(1)}, bf16[72,1792]{1,0:T(8,128)(2,1)S(1)}, u32[]{:S(2)}, u32[]{:S(2)}) collective-permute-start(bf16[72,1792]{1,0:T(8,128)(2,1)S(1)} %add_convert_fusion.6), channel_id=1, source_target_pairs={{0,1},{1,0},{2,3},{3,2},{4,5},{5,4},{6,7},{7,6},{8,9},{9,8},{10,11... | collective-permute-start | bytes 774152 | tf_op jit(solution)/shard_map/back0_y/ppermute | solution.py:264
  60.7 9.2 %collective-permute-start.20 = (bf16[72,1792]{1,0:T(8,128)(2,1)S(1)}, bf16[72,1792]{1,0:T(8,128)(2,1)S(1)}, u32[]{:S(2)}, u32[]{:S(2)}) collective-permute-start(bf16[72,1792]{1,0:T(8,128)(2,1)S(1)} %get-tuple-element.87), channel_id=1, source_target_pairs={{0,1},{1,0},{2,3},{3,2},{4,5},{5,4},{6,7},{7,6},{8,9},{9,8},{10,11... | collective-permute-start | bytes 774152 | tf_op jit(solution)/shard_map/back1_d/ppermute | solution.py:264
  62.1 13.3 %collective-permute-start.26 = (bf16[72,1792]{1,0:T(8,128)(2,1)S(1)}, bf16[72,1792]{1,0:T(8,128)(2,1)S(1)}, u32[]{:S(2)}, u32[]{:S(2)}) collective-permute-start(bf16[72,1792]{1,0:T(8,128)(2,1)S(1)} %get-tuple-element.97), channel_id=1, source_target_pairs={{0,1},{1,0},{2,3},{3,2},{4,5},{5,4},{6,7},{7,6},{8,9},{9,8},{10,11... | collective-permute-start | bytes 774152 | tf_op jit(solution)/shard_map/mine_d1/ppermute | solution.py:264
  66.4 30.9 %collective-permute-start.24 = (bf16[72,1792]{1,0:T(8,128)(2,1)S(1)}, bf16[72,1792]{1,0:T(8,128)(2,1)S(1)}, u32[]{:S(2)}, u32[]{:S(2)}) collective-permute-start(bf16[72,1792]{1,0:T(8,128)(2,1)S(1)} %add_convert_fusion.3), channel_id=1, source_target_pairs={{0,4},{1,5},{2,6},{3,7},{4,0},{5,1},{6,2},{7,3},{8,12},{9,13},{10,... | collective-permute-start | bytes 774152 | tf_op jit(solution)/shard_map/back0/ppermute | solution.py:264
  68.2 10.7 %collective-permute-start.18 = (bf16[72,1792]{1,0:T(8,128)(2,1)S(1)}, bf16[72,1792]{1,0:T(8,128)(2,1)S(1)}, u32[]{:S(2)}, u32[]{:S(2)}) collective-permute-start(bf16[72,1792]{1,0:T(8,128)(2,1)S(1)} %get-tuple-element.83), channel_id=1, source_target_pairs={{0,1},{1,0},{2,3},{3,2},{4,5},{5,4},{6,7},{7,6},{8,9},{9,8},{10,11... | collective-permute-start | bytes 774152 | tf_op jit(solution)/shard_map/back1_y/ppermute | solution.py:264
  70.0 12.7 %collective-permute-start.22 = (bf16[72,1792]{1,0:T(8,128)(2,1)S(1)}, bf16[72,1792]{1,0:T(8,128)(2,1)S(1)}, u32[]{:S(2)}, u32[]{:S(2)}) collective-permute-start(bf16[72,1792]{1,0:T(8,128)(2,1)S(1)} %add_convert_fusion.5), channel_id=1, source_target_pairs={{0,2},{1,3},{2,0},{3,1},{4,6},{5,7},{6,4},{7,5},{8,10},{9,11},{10,... | collective-permute-start | bytes 774152 | tf_op jit(solution)/shard_map/back1_z/ppermute | solution.py:264
  75.5 15.3 %collective-permute-start.27 = (bf16[72,1792]{1,0:T(8,128)(2,1)S(1)}, bf16[72,1792]{1,0:T(8,128)(2,1)S(1)}, u32[]{:S(2)}, u32[]{:S(2)}) collective-permute-start(bf16[72,1792]{1,0:T(8,128)(2,1)S(1)} %add_convert_fusion.2), channel_id=1, source_target_pairs={{0,2},{1,3},{2,0},{3,1},{4,6},{5,7},{6,4},{7,5},{8,10},{9,11},{10,... | collective-permute-start | bytes 774152 | tf_op jit(solution)/shard_map/mine_z1/ppermute | solution.py:264
  79.0 14.0 %collective-permute-start.25 = (bf16[72,1792]{1,0:T(8,128)(2,1)S(1)}, bf16[72,1792]{1,0:T(8,128)(2,1)S(1)}, u32[]{:S(2)}, u32[]{:S(2)}) collective-permute-start(bf16[72,1792]{1,0:T(8,128)(2,1)S(1)} %get-tuple-element.94), channel_id=1, source_target_pairs={{0,1},{1,0},{2,3},{3,2},{4,5},{5,4},{6,7},{7,6},{8,9},{9,8},{10,11... | collective-permute-start | bytes 774152 | tf_op jit(solution)/shard_map/mine_y1/ppermute | solution.py:264
  82.6 12.5 %collective-permute-start.23 = (bf16[72,1792]{1,0:T(8,128)(2,1)S(1)}, bf16[72,1792]{1,0:T(8,128)(2,1)S(1)}, u32[]{:S(2)}, u32[]{:S(2)}) collective-permute-start(bf16[72,1792]{1,0:T(8,128)(2,1)S(1)} %get-tuple-element.91), channel_id=1, source_target_pairs={{0,2},{1,3},{2,0},{3,1},{4,6},{5,7},{6,4},{7,5},{8,10},{9,11},{10,... | collective-permute-start | bytes 774152 | tf_op jit(solution)/shard_map/mine_z0/ppermute | solution.py:264
  83.0 14.4 %collective-permute-start.29 = (bf16[72,1792]{1,0:T(8,128)(2,1)S(1)}, bf16[72,1792]{1,0:T(8,128)(2,1)S(1)}, u32[]{:S(2)}, u32[]{:S(2)}) collective-permute-start(bf16[72,1792]{1,0:T(8,128)(2,1)S(1)} %add_convert_fusion), channel_id=1, source_target_pairs={{0,12},{1,13},{2,14},{3,15},{4,8},{5,9},{6,10},{7,11},{8,4},{9,5},... | collective-permute-start | bytes 774152 | tf_op jit(solution)/shard_map/back1/ppermute | solution.py:264
  90.8 6.5 %collective-permute-start.19 = (bf16[72,1792]{1,0:T(8,128)(2,1)S(1)}, bf16[72,1792]{1,0:T(8,128)(2,1)S(1)}, u32[]{:S(2)}, u32[]{:S(2)}) collective-permute-start(bf16[72,1792]{1,0:T(8,128)(2,1)S(1)} %add_convert_fusion.7), channel_id=1, source_target_pairs={{0,1},{1,0},{2,3},{3,2},{4,5},{5,4},{6,7},{7,6},{8,9},{9,8},{10,11... | collective-permute-start | bytes 774152 | tf_op jit(solution)/shard_map/mine_y0/ppermute | solution.py:264
  93.0 4.4 %collective-permute-start.28 = (bf16[72,1792]{1,0:T(8,128)(2,1)S(1)}, bf16[72,1792]{1,0:T(8,128)(2,1)S(1)}, u32[]{:S(2)}, u32[]{:S(2)}) collective-permute-start(bf16[72,1792]{1,0:T(8,128)(2,1)S(1)} %add_convert_fusion.1), channel_id=1, source_target_pairs={{0,8},{1,9},{2,10},{3,11},{4,12},{5,13},{6,14},{7,15},{8,0},{9,1},... | collective-permute-start | bytes 774152 | tf_op jit(solution)/shard_map/home1/ppermute | solution.py:264
